TPU v7x, 32 devices: a whole 2x2x4 slice. The times are simulated.
32 devices in a mesh: block: 8 (over y, x, core), walker: 4 (over z).
Axes of the slice: x: 2, y: 2, z: 4, core: 2. Of those that a mesh axis runs over, the one named last changes fastest.
Arguments:
- green: bfloat16 [20, 294912], P('walker', 'block'), may hold values from -6 to 6
- chol: bfloat16 [64, 192, 1536], P('block'), may hold values from -0.15625 to 0.15625
- counts: int32 [4], replicated, may hold values from 1 to 5, as said below
- move_slot: int32 [4, 2], replicated, may hold values from -1 to 4, as said below
- move_dest: int32 [4, 2], replicated, may hold values from -1 to 3, as said below
Outputs:
- new_green: bfloat16 [12, 294912], P('walker', 'block')
- energy: float32 [12], P('walker')
Inputs may be any that keep to these rules, and one draw needn't show every extreme that they name: On every device, counts minus the walkers it sends plus the walkers it receives equals 3; in every draw some device has count 5 and some device has count 1. `move_slot`: in each row the entries >= 0 come first, are distinct, and name live slots of that device; the rest are -1. `move_dest`: -1 exactly where move_slot is -1, else another device's index; from one device at most 1 walker goes to any one device, and some device sends that many to one.
All inputs are finite; a program needn't handle non-finite values.
Results may differ from a plain program's by a relative error of at most 0.0004.
Values may be sent and summed in bfloat16 or wider, within the bound.
No kernel may reach another device: no remote copies, remote signals or barrier semaphores. Data moves between devices by JAX's collectives and lax.ppermute only.
A program may use at most 64 MiB of HBM per device.

v0:
```python
import functools
import math

import jax
import jax.numpy as jnp
from jax import lax
from jax.experimental import pallas as pl
from jax.experimental.pallas import tpu as pltpu
from jax.sharding import PartitionSpec as P


def arrival_ranks(move_slot, move_dest):
    active = move_slot >= 0
    move_total = move_slot.shape[1]
    earlier = jnp.arange(move_total)[None, :] < jnp.arange(move_total)[:, None]
    same_target = (
        (move_dest[:, :, None] == move_dest[:, None, :]) & earlier[None, :, :] & active[:, None, :]
    )
    return (active, jnp.sum(same_target.astype(jnp.int32), axis=2))


def general_body(green, chol, counts, move_slot, move_dest):
    walker_total = lax.axis_size("walker")
    own_index = lax.axis_index("walker")
    slot_total = green.shape[0]
    share_width = green.shape[1]
    keep_total = slot_total - move_slot.shape[1]
    capacity = (move_slot.shape[1] + walker_total - 2) // (walker_total - 1)
    occ_count = chol.shape[1]
    orb_count = chol.shape[2]
    energy_scale = 0.5 / (occ_count * math.sqrt(chol.shape[0] * lax.axis_size("block")))
    active, move_rank = arrival_ranks(move_slot, move_dest)
    own_slots = move_slot[own_index]
    own_dests = move_dest[own_index]
    own_active = active[own_index]
    own_rank = move_rank[own_index]
    peer_ids = jnp.arange(walker_total)
    place_ids = jnp.arange(capacity)
    chosen = (
        (own_dests[None, None, :] == peer_ids[:, None, None])
        & (own_rank[None, None, :] == place_ids[None, :, None])
        & own_active[None, None, :]
    )
    send_slot = jnp.sum(jnp.where(chosen, own_slots[None, None, :], 0), axis=2).reshape(-1)
    present = jnp.any(chosen, axis=2).reshape(-1)
    arrive = jnp.any(
        (move_dest[:, None, :] == own_index)
        & (move_rank[:, None, :] == place_ids[None, :, None])
        & active[:, None, :],
        axis=2,
    ).reshape(-1)
    slot_ids = jnp.arange(slot_total)
    occupied = slot_ids < counts[own_index]
    leaving = jnp.any(own_slots[:, None] == slot_ids[None, :], axis=0)
    staying = occupied & jnp.logical_not(leaving)
    stay_rank = jnp.cumsum(staying.astype(jnp.int32)) - 1
    arrive_rank = jnp.cumsum(arrive.astype(jnp.int32)) - 1
    stay_total = jnp.sum(staying.astype(jnp.int32))
    targets = jnp.arange(keep_total)
    from_stay = jnp.sum(
        jnp.where(
            staying[None, :] & (stay_rank[None, :] == targets[:, None]), slot_ids[None, :], 0
        ),
        axis=1,
    )
    arrive_ids = jnp.arange(arrive.shape[0]) + slot_total
    from_arrive = jnp.sum(
        jnp.where(
            arrive[None, :] & (arrive_rank[None, :] == (targets - stay_total)[:, None]),
            arrive_ids[None, :],
            0,
        ),
        axis=1,
    )
    source_row = jnp.where(targets < stay_total, from_stay, from_arrive)
    outgoing = jnp.where(
        present[:, None], jnp.take(green, send_slot, axis=0), jnp.zeros((), jnp.bfloat16)
    )
    outgoing = outgoing.reshape(walker_total, capacity, share_width)

    def walker_energy(walker_row):
        green_mat = walker_row.reshape(occ_count, orb_count)
        transfer = jnp.einsum("gip,jp->gij", chol, green_mat, preferred_element_type=jnp.float32)
        return jnp.sum(transfer * jnp.swapaxes(transfer, 1, 2))

    got_rows = lax.all_to_all(outgoing, "walker", split_axis=0, concat_axis=0, tiled=True)
    source_pool = jnp.concatenate([green, got_rows.reshape(-1, share_width)], axis=0)
    new_green = jnp.take(source_pool, source_row, axis=0)
    complete = lax.all_gather(new_green, "block", axis=1, tiled=True)
    partial_value = lax.map(walker_energy, complete)
    energy = -energy_scale * lax.psum(partial_value, "block")
    return (new_green, energy)


LANES = 128
ROWS = 8


def spread_slots(green_ref, spread, share_rows):
    slots = green_ref.shape[0]
    tiles = spread.shape[0]
    for row in range(share_rows):
        for tile in range(tiles):
            col = (row * tiles + tile) * LANES
            block = green_ref[:, col : col + LANES].astype(jnp.float32)
            spread[tile, row * ROWS : row * ROWS + slots, :] = block


def pack_kernel(dims, green_ref, own_ref, spread):
    slots, share_rows, orb_count, pad_rows = dims
    spread_slots(green_ref, spread, share_rows)
    for tile in range(orb_count // LANES):
        dense = [spread[tile, pl.ds(slot, share_rows, stride=ROWS), :] for slot in range(slots)]
        if pad_rows > slots * share_rows:
            dense.append(jnp.zeros((pad_rows - slots * share_rows, LANES), jnp.float32))
        packed = jnp.concatenate(dense, axis=0).astype(jnp.bfloat16)
        own_ref[:, tile * LANES : (tile + 1) * LANES] = packed


class Moves:
    def __init__(self, table_ref, moves):
        self.table, self.moves = table_ref, moves

    def count(self, device):
        return self.table[0, device]

    def slot(self, device, move):
        return self.table[1 + move, device]

    def dest(self, device, move):
        return self.table[1 + self.moves + move, device]

    def staying(self, device):
        total = self.count(device)
        for move in range(self.moves):
            total = total - jnp.where(self.slot(device, move) >= 0, 1, 0)
        return total

    def goes_to(self, own, slot):
        target = jnp.int32(-1)
        for move in range(self.moves):
            target = jnp.where(self.slot(own, move) == slot, self.dest(own, move), target)
        return target


def leave_kernel(dims, ident_ref, table_ref, own_ref, *refs):
    slots, share_rows, orb_count, walkers, moves, keep = dims
    leave_refs, place_ref, wide = refs[:-2], refs[-2], refs[-1]
    table = Moves(table_ref, moves)
    wide[...] = own_ref[...].astype(jnp.float32)
    own = ident_ref[0]
    for shift in range(1, walkers):
        target = lax.rem(own + shift, walkers)
        chosen = jnp.int32(0)
        for move in range(moves):
            hit = (table.dest(own, move) == target) & (table.slot(own, move) >= 0)
            chosen = jnp.where(hit, table.slot(own, move), chosen)
        start = pl.multiple_of(chosen * share_rows, ROWS)
        leave_refs[shift - 1][...] = wide[pl.ds(start, share_rows), :].astype(jnp.bfloat16)
    rank = jnp.int32(0)
    for slot in range(slots):
        live = slot < table.count(own)
        gone_to = table.goes_to(own, slot)
        stays = live & (gone_to < 0)
        there = jnp.maximum(gone_to, 0)
        ahead = table.staying(there)
        for device in range(walkers):
            for move in range(moves):
                hit = (
                    (device < own)
                    & (table.dest(device, move) == there)
                    & (table.slot(device, move) >= 0)
                )
                ahead = ahead + jnp.where(hit, 1, 0)
        place = jnp.where(stays, own * keep + rank, there * keep + ahead)
        place_ref[slot] = jnp.where(live, place, -1)
        rank = rank + jnp.where(stays, 1, 0)


def assemble_kernel(dims, ident_ref, table_ref, green_ref, *refs):
    slots, share_rows, orb_count, walkers, moves, keep = dims
    table = Moves(table_ref, moves)
    come_refs = refs[: walkers - 1]
    new_ref, spread, pool, out = refs[walkers - 1 :]
    own = ident_ref[0]
    tiles = orb_count // LANES
    spread_slots(green_ref, spread, share_rows)
    for slot in range(slots):
        for tile in range(tiles):
            pool[
                slot * share_rows : (slot + 1) * share_rows, tile * LANES : (tile + 1) * LANES
            ] = spread[tile, pl.ds(slot, share_rows, stride=ROWS), :]
    for shift in range(1, walkers):
        start = (slots + shift - 1) * share_rows
        pool[start : start + share_rows, :] = come_refs[shift - 1][...].astype(jnp.float32)

    sources = [jnp.int32(0)] * keep
    rank = jnp.int32(0)
    for slot in range(slots):
        stays = (slot < table.count(own)) & (table.goes_to(own, slot) < 0)
        for target in range(keep):
            sources[target] = jnp.where(stays & (rank == target), slot, sources[target])
        rank = rank + jnp.where(stays, 1, 0)
    for device in range(walkers):
        comes = jnp.bool_(False)
        for move in range(moves):
            comes = comes | ((table.dest(device, move) == own) & (table.slot(device, move) >= 0))
        comes = comes & (device != own)
        shift = lax.rem(own - device + walkers, walkers)
        for target in range(keep):
            sources[target] = jnp.where(
                comes & (rank == target), slots + shift - 1, sources[target]
            )
        rank = rank + jnp.where(comes, 1, 0)
    for target in range(keep):
        start = pl.multiple_of(sources[target] * share_rows, ROWS)
        for tile in range(tiles):
            out[tile, pl.ds(target, share_rows, stride=ROWS), :] = pool[
                pl.ds(start, share_rows), tile * LANES : (tile + 1) * LANES
            ]
    for row in range(share_rows):
        for tile in range(tiles):
            col = (row * tiles + tile) * LANES
            new_ref[:, col : col + LANES] = out[
                tile, row * ROWS : row * ROWS + keep, :
            ].astype(jnp.bfloat16)


def order_kernel(dims, ident_ref, chol_ref, own_ref, out_ref, sems):
    del own_ref
    group, groups, chip_rows = dims
    chip = ident_ref[0] // 2
    edge = LANES - 2 * chip_rows
    rest = 2 * chip_rows - edge
    copies = []

    def add(vec, distance, start, size, place):
        row = pl.multiple_of(jnp.bitwise_xor(chip, distance) * chip_rows + start, 16)
        copies.append(
            pltpu.make_async_copy(
                chol_ref.at[vec, pl.ds(row, size), :],
                out_ref.at[pl.ds(place, size), :],
                sems.at[len(copies)],
            )
        )

    for index in range(groups):
        for item in range(group):
            vec = index * group + item
            place = index * group * 4 * chip_rows + item * LANES
            add(vec, 0, 0, chip_rows, place)
            add(vec, 1, 0, chip_rows, place + chip_rows)
            add(vec, 2, 0, edge, place + 2 * chip_rows)
            place = index * group * 4 * chip_rows + group * LANES + item * rest
            add(vec, 2, edge, chip_rows - edge, place)
            add(vec, 3, 0, chip_rows, place + chip_rows - edge)
    for copy in copies:
        copy.start()
    for copy in copies:
        copy.wait()


def times(left, right):
    return lax.dot_general(
        left, right, (((1,), (1,)), ((), ())), preferred_element_type=jnp.float32
    )


def near_kernel(dims, ident_ref, weight_ref, *refs):
    slots, share_rows, group, groups, chip_rows = dims
    piece_refs = refs[:6]
    sum_ref, late_ref = refs[6:8]
    trans_refs = refs[8:]
    own = ident_ref[0]
    core = lax.rem(own, 2)
    pad_rows = piece_refs[0].shape[0]
    near = 3 * chip_rows
    size = 4 * chip_rows * group
    edge = near - LANES
    half = LANES // 2
    left = jnp.concatenate([ref[...] for ref in piece_refs], axis=0)
    lane = lax.broadcasted_iota(jnp.int32, (1, LANES), 1)
    low_half = lane < half
    in_edge = jnp.where(low_half, lane, lane - half) < edge
    sums = [jnp.zeros((ROWS, LANES), jnp.float32) for _ in range(slots)]

    def fold(value):
        return jnp.sum(value.reshape(-1, ROWS, LANES), axis=0)

    for index in range(groups):
        trans = trans_refs[index]
        result = times(left, weight_ref[index * size : (index + 1) * size, :])
        for piece in range(6):
            source = jnp.bitwise_xor(core, piece % 2)
            for slot in range(slots):
                start = piece * pad_rows + slot * share_rows
                place = slot * near + (piece // 2) * chip_rows + source * share_rows
                trans[pl.ds(pl.multiple_of(place, ROWS), share_rows), :] = result[
                    start : start + share_rows, :
                ]
        for slot in range(slots):
            base = slot * near
            late = slice(slot * chip_rows, (slot + 1) * chip_rows)
            acc = sums[slot]
            for pair in range(group // 2):
                col = (group + pair) * LANES
                top = trans[base : base + LANES, col : col + LANES].T
                edge_rows = trans[base + LANES : base + near, col : col + LANES]
                gap = jnp.zeros((half - edge, LANES), jnp.float32)
                bottom = jnp.concatenate([edge_rows, gap, edge_rows, gap], axis=0).T
                for side in range(2):
                    vec = 2 * pair + side
                    high = trans[base : base + LANES, vec * LANES : (vec + 1) * LANES]
                    acc = acc + fold(high * high.T)
                    across = trans[base + LANES : base + near, vec * LANES : (vec + 1) * LANES]
                    acc = acc + 2.0 * fold(across * top[side * half : side * half + edge, :])
                    late_ref[
                        late, (index * (group + group // 2) + vec) * LANES : (
                            index * (group + group // 2) + vec + 1
                        ) * LANES
                    ] = top[side * half + edge : (side + 1) * half, :]
                corner = jnp.where(low_half, bottom[:edge, :], bottom[half : half + edge, :])
                acc = acc + fold(jnp.where(in_edge, edge_rows * corner, 0.0))
                rest = jnp.where(low_half, bottom[edge:half, :], bottom[half + edge :, :])
                place = (index * (group + group // 2) + group + pair) * LANES
                late_ref[late, place : place + LANES] = jnp.where(in_edge, rest, 0.0)
            sums[slot] = acc
    sum_ref[...] = jnp.concatenate(sums, axis=0)


def far_kernel(dims, ident_ref, place_ref, weight_ref, near_sum_ref, late_ref, *refs):
    slots, share_rows, group, groups, chip_rows = dims
    piece_refs = refs[:4]
    sum_ref = refs[4]
    trans_refs = refs[5:]
    own = ident_ref[0]
    core = lax.rem(own, 2)
    pad_rows, width = piece_refs[0].shape
    half = LANES // 2
    edge = half - chip_rows
    size = 4 * chip_rows * group
    lane = lax.broadcasted_iota(jnp.int32, (1, LANES), 1)
    low_half = lane < half
    in_rest = jnp.where(low_half, lane, lane - half) >= edge
    lefts = [
        jnp.concatenate([piece_refs[part][...], piece_refs[2 + part][...]], axis=0)
        for part in range(2)
    ]
    twice = [jnp.zeros((ROWS, LANES), jnp.float32) for _ in range(slots)]
    once = [near_sum_ref[slot * ROWS : (slot + 1) * ROWS, :] for slot in range(slots)]

    def fold(value):
        return jnp.sum(value.reshape(-1, ROWS, LANES), axis=0)

    tiles = group + group // 2
    for index in range(groups):
        trans = trans_refs[index]
        rows = slice(index * size, (index + 1) * size)
        result = times(lefts[0], weight_ref[rows, :width])
        result = result + times(lefts[1], weight_ref[rows, width:])
        for piece in range(2):
            source = jnp.bitwise_xor(core, piece)
            for slot in range(slots):
                start = piece * pad_rows + slot * share_rows
                place = slot * chip_rows + source * share_rows
                trans[pl.ds(pl.multiple_of(place, ROWS), share_rows), :] = result[
                    start : start + share_rows, :
                ]
        for slot in range(slots):
            rows = slice(slot * chip_rows, (slot + 1) * chip_rows)
            for tile in range(tiles):
                here = trans[rows, tile * LANES : (tile + 1) * LANES]
                met = late_ref[rows, (index * tiles + tile) * LANES : (index * tiles + tile + 1) * LANES]
                twice[slot] = twice[slot] + fold(here * met)
                if tile >= group:
                    gap = jnp.zeros((edge, LANES), jnp.float32)
                    turned = jnp.concatenate([gap, here, gap, here], axis=0).T
                    corner = jnp.where(low_half, turned[edge:half, :], turned[half + edge :, :])
                    once[slot] = once[slot] + fold(jnp.where(in_rest, here * corner, 0.0))
    value = jnp.zeros((1, LANES), jnp.float32)
    for slot in range(slots):
        slot_sum = jnp.sum(once[slot] + 2.0 * twice[slot])
        value = jnp.where(lane == place_ref[slot], slot_sum, value)
    sum_ref[...] = value


def swap(value, mask, blocks):
    return lax.ppermute(value, "block", [(index, index ^ mask) for index in range(blocks)])


def body(green, chol, counts, move_slot, move_dest):
    walkers = lax.axis_size("walker")
    blocks = lax.axis_size("block")
    slots, share_width = green.shape
    vectors, occ_count, orb_count = chol.shape
    moves = move_slot.shape[1]
    keep = slots - moves
    share_rows = share_width // orb_count
    pad_rows = -(-slots * share_rows // 16) * 16
    table = jnp.concatenate([counts[None, :], move_slot.T, move_dest.T], axis=0)
    walker_index = lax.axis_index("walker").astype(jnp.int32).reshape(1)
    block_index = lax.axis_index("block").astype(jnp.int32).reshape(1)
    smem = pl.BlockSpec(memory_space=pltpu.SMEM)
    vmem = pl.BlockSpec(memory_space=pltpu.VMEM)
    limit = pltpu.CompilerParams(vmem_limit_bytes=32 * 1024 * 1024)

    spread = pltpu.VMEM((orb_count // LANES, share_rows * ROWS, LANES), jnp.float32)
    own_rows = pl.pallas_call(
        functools.partial(pack_kernel, (slots, share_rows, orb_count, pad_rows)),
        out_shape=jax.ShapeDtypeStruct((pad_rows, orb_count), jnp.bfloat16),
        in_specs=[vmem],
        out_specs=vmem,
        scratch_shapes=[spread],
        compiler_params=limit,
        name="pack",
    )(green)
    move_dims = (slots, share_rows, orb_count, walkers, moves, keep)
    *leaving, place = pl.pallas_call(
        functools.partial(leave_kernel, move_dims),
        out_shape=[jax.ShapeDtypeStruct((share_rows, orb_count), jnp.bfloat16)] * (walkers - 1)
        + [jax.ShapeDtypeStruct((slots,), jnp.int32)],
        in_specs=[smem, smem, vmem],
        out_specs=[vmem] * (walkers - 1) + [smem],
        scratch_shapes=[pltpu.VMEM((pad_rows, orb_count), jnp.float32)],
        compiler_params=limit,
        name="leave",
    )(walker_index, table, own_rows)
    coming = [
        lax.ppermute(
            leaving[shift - 1], "walker", [(z, (z + shift) % walkers) for z in range(walkers)]
        )
        for shift in range(1, walkers)
    ]

    group = 4
    groups = vectors // group
    chip_rows = 2 * share_rows
    weights = pl.pallas_call(
        functools.partial(order_kernel, (group, groups, chip_rows)),
        out_shape=jax.ShapeDtypeStruct((vectors * occ_count, orb_count), jnp.bfloat16),
        in_specs=[smem] + [pl.BlockSpec(memory_space=pl.ANY)] * 2,
        out_specs=vmem,
        scratch_shapes=[pltpu.SemaphoreType.DMA((5 * vectors,))],
        compiler_params=pltpu.CompilerParams(vmem_limit_bytes=48 * 1024 * 1024),
        cost_estimate=pl.CostEstimate(
            flops=0, bytes_accessed=4 * chol.size, transcendentals=0
        ),
        name="order",
    )(block_index, chol, own_rows)

    core, near_x, near_y = 1, 2, 4
    from_x = swap(own_rows, near_x, blocks)
    from_y = swap(own_rows, near_y, blocks)
    from_core = swap(own_rows, core, blocks)
    width = orb_count // 2
    from_x, from_y, weights, coming[:2] = lax.optimization_barrier(
        (from_x, from_y, weights, coming[:2])
    )
    far = [swap(from_y[:, :width], near_x, blocks), swap(from_x[:, width:], near_y, blocks)]
    near_pieces = [own_rows, from_core]
    for piece in (from_x, from_y):
        near_pieces += [piece, swap(piece, core, blocks)]

    dims = (slots, share_rows, group, groups, chip_rows)
    work = 2 * vectors * occ_count * orb_count * pad_rows
    near_sums, late = pl.pallas_call(
        functools.partial(near_kernel, dims),
        out_shape=[
            jax.ShapeDtypeStruct((slots * ROWS, LANES), jnp.float32),
            jax.ShapeDtypeStruct((slots * chip_rows, vectors * occ_count), jnp.float32),
        ],
        in_specs=[smem] + [vmem] * 7,
        out_specs=[vmem] * 2,
        scratch_shapes=[pltpu.VMEM((slots * 3 * chip_rows, group * occ_count), jnp.float32)]
        * groups,
        compiler_params=limit,
        cost_estimate=pl.CostEstimate(
            flops=6 * work, bytes_accessed=2 * chol.size, transcendentals=0
        ),
        name="near",
    )(block_index, weights, *near_pieces)
    far, near_sums = lax.optimization_barrier((far, near_sums))
    far_pieces = far + [swap(piece, core, blocks) for piece in far]
    all_sums = pl.pallas_call(
        functools.partial(far_kernel, dims),
        out_shape=jax.ShapeDtypeStruct((1, LANES), jnp.float32),
        in_specs=[smem] * 2 + [vmem] * 7,
        out_specs=vmem,
        scratch_shapes=[pltpu.VMEM((slots * chip_rows, group * occ_count), jnp.float32)] * groups,
        compiler_params=limit,
        cost_estimate=pl.CostEstimate(
            flops=2 * work, bytes_accessed=2 * chol.size, transcendentals=0
        ),
        name="far",
    )(block_index, place, weights, near_sums, late, *far_pieces)

    coming, _ = lax.optimization_barrier((coming, all_sums))
    new_green = pl.pallas_call(
        functools.partial(assemble_kernel, move_dims),
        out_shape=jax.ShapeDtypeStruct((keep, share_width), jnp.bfloat16),
        in_specs=[smem] * 2 + [vmem] * walkers,
        out_specs=vmem,
        scratch_shapes=[
            pltpu.VMEM((orb_count // LANES, share_rows * ROWS, LANES), jnp.float32),
            pltpu.VMEM(((slots + walkers - 1) * share_rows, orb_count), jnp.float32),
            pltpu.VMEM((orb_count // LANES, share_rows * ROWS, LANES), jnp.float32),
        ],
        compiler_params=limit,
        name="assemble",
    )(walker_index, table, green, *coming)

    energy_scale = 0.5 / (occ_count * math.sqrt(vectors * blocks))
    for mask in (core, near_x, near_y):
        all_sums = all_sums + swap(all_sums, mask, blocks)
    mask = 1
    while mask < walkers:
        pairs = [(index, index ^ mask) for index in range(walkers)]
        all_sums = all_sums + lax.ppermute(all_sums, "walker", pairs)
        mask *= 2
    own_sums = lax.dynamic_slice(all_sums[0], (walker_index[0] * keep,), (keep,))
    return (new_green, -energy_scale * own_sums)


def fits(mesh):
    blocks = mesh.shape["block"]
    walkers = mesh.shape["walker"]

    def check(green, chol, counts, move_slot, move_dest):
        vectors, occ_count, orb_count = chol.shape
        share_width = green.shape[1] // blocks
        moves = move_slot.shape[1]
        slots = green.shape[0] // walkers
        return (
            blocks == 8
            and walkers >= 2
            and walkers & (walkers - 1) == 0
            and (moves + walkers - 2) // (walkers - 1) == 1
            and slots <= ROWS
            and share_width % (orb_count * ROWS) == 0
            and orb_count % (2 * LANES) == 0
            and occ_count == blocks * (share_width // orb_count)
            and occ_count == LANES + LANES // 2
            and (vectors // blocks) % 4 == 0
            and walkers * (slots - moves) <= LANES
        )

    return check


def solution(mesh):
    in_specs = (P("walker", "block"), P("block", None, None), P(), P(), P())
    out_specs = (P("walker", "block"), P("walker"))
    check = fits(mesh)

    def run(*args):
        chosen = body if check(*args) else general_body
        return jax.shard_map(
            chosen, mesh=mesh, in_specs=in_specs, out_specs=out_specs, check_vma=False
        )(*args)

    return run
```

profile of v0, /device:TPU:0, one launch (start us, length us, event | category | flops | bytes accessed | tf_op | source)
XLA Modules:
  0.0 46.6 jit_solution(6815842200616170667)
XLA Ops:
  0.6 1.1 %copy-done = bf16[5,36864]{1,0:T(8,128)(2,1)S(1)} copy-done((bf16[5,36864]{1,0:T(8,128)(2,1)S(1)}, bf16[5,36864]{1,0:T(8,128)(2,1)}, u32[]{:S(2)}) %copy-start) | copy-done | bytes 368664
  2.0 3.0 %collective-permute-start = (bf16[128,1536]{1,0:T(8,128)(2,1)S(1)}, bf16[128,1536]{1,0:T(8,128)(2,1)S(1)}, u32[]{:S(2)}, u32[]{:S(2)}) collective-permute-start(bf16[128,1536]{1,0:T(8,128)(2,1)S(1)} %pack.1.own_ref.refs_0_), channel_id=1, source_target_pairs={{0,8},{4,12},{8,0},{12,4},{16,24},{20,28},{24,16},{28,20},{1,9},{5... | collective-permute-start | bytes 1179656 | tf_op jit(solution)/shard_map/ppermute | solution.py:388
  5.0 1.5 %collective-permute-start.1 = (bf16[128,1536]{1,0:T(8,128)(2,1)S(1)}, bf16[128,1536]{1,0:T(8,128)(2,1)S(1)}, u32[]{:S(2)}, u32[]{:S(2)}) collective-permute-start(bf16[128,1536]{1,0:T(8,128)(2,1)S(1)} %pack.1.own_ref.refs_0_), channel_id=1, source_target_pairs={{0,16},{4,20},{8,24},{12,28},{16,0},{20,4},{24,8},{28,12},{1,17},{... | collective-permute-start | bytes 1179656 | tf_op jit(solution)/shard_map/ppermute | solution.py:388
  6.5 0.7 %pad_add_fusion.table_ref = s32[5,4]{1,0:T(8,128)S(1)} fusion(s32[2,4]{1,0:T(2,128)} %bitcast.7, s32[2,4]{1,0:T(2,128)} %bitcast.8, s32[1,4]{1,0:T(1,128)} %bitcast.9), kind=kLoop, calls=%fused_computation | loop fusion | flops 40 | bytes 160 | tf_op jit(solution)/shard_map/concatenate | solution.py:400
  7.2 1.4 %leave.1 = (bf16[24,1536]{1,0:T(8,128)(2,1)S(1)}, bf16[24,1536]{1,0:T(8,128)(2,1)S(1)}, bf16[24,1536]{1,0:T(8,128)(2,1)S(1)}, s32[5]{0:T(128)S(1)}) custom-call(s32[1]{0:T(128)} %bitcast.ident_ref, s32[5,4]{1,0:T(8,128)S(1)} %pad_add_fusion.table_ref, bf16[128,1536]{1,0:T(8,128)(2,1)S(1)} %pack.1.own_ref.refs_0_), custom_call_target="tpu_custom_call" | custom-call | tf_op jit(solution)/shard_map/leave/pallas_call | solution.py:418
  8.6 1.6 %collective-permute-start.2 = (bf16[24,1536]{1,0:T(8,128)(2,1)S(1)}, bf16[24,1536]{1,0:T(8,128)(2,1)S(1)}, u32[]{:S(2)}, u32[]{:S(2)}) collective-permute-start(bf16[24,1536]{1,0:T(8,128)(2,1)S(1)} %get-tuple-element.19), channel_id=1, source_target_pairs={{0,1},{1,2},{2,3},{3,0},{4,5},{5,6},{6,7},{7,4},{8,9},{9,10},{10,1... | collective-permute-start | bytes 221192 | tf_op jit(solution)/shard_map/ppermute | solution.py:429
  10.3 2.6 %collective-permute-start.3 = (bf16[24,1536]{1,0:T(8,128)(2,1)S(1)}, bf16[24,1536]{1,0:T(8,128)(2,1)S(1)}, u32[]{:S(2)}, u32[]{:S(2)}) collective-permute-start(bf16[24,1536]{1,0:T(8,128)(2,1)S(1)} %get-tuple-element.20), channel_id=1, source_target_pairs={{0,2},{1,3},{2,0},{3,1},{4,6},{5,7},{6,4},{7,5},{8,10},{9,11},{10,... | collective-permute-start | bytes 221192 | tf_op jit(solution)/shard_map/ppermute | solution.py:429
  12.9 2.8 %order.1.weight_ref = bf16[1536,1536]{1,0:T(8,128)(2,1)S(1)} custom-call(s32[1]{0:T(128)} %bitcast.4.ident_ref, bf16[8,192,1536]{2,1,0:T(8,128)(2,1)} %chol_ref.1, bf16[128,1536]{1,0:T(8,128)(2,1)S(1)} %pack.1.own_ref.refs_0_), custom_call_target="tpu_custom_call" | custom-call | bytes 9437184 | tf_op jit(solution)/shard_map/order/pallas_call | solution.py:438
  15.6 1.5 %collective-permute-done.3.refs_1_ = bf16[24,1536]{1,0:T(8,128)(2,1)S(1)} collective-permute-done((bf16[24,1536]{1,0:T(8,128)(2,1)S(1)}, bf16[24,1536]{1,0:T(8,128)(2,1)S(1)}, u32[]{:S(2)}, u32[]{:S(2)}) %collective-permute-start.3) | collective-permute-done | bytes 73760 | tf_op jit(solution)/shard_map/ppermute | solution.py:429
  17.7 0.6 %collective-permute-start.5 = (bf16[128,768]{1,0:T(8,128)(2,1)S(1)}, bf16[128,768]{1,0:T(8,128)(2,1)S(1)}, u32[]{:S(2)}, u32[]{:S(2)}) collective-permute-start(bf16[128,768]{1,0:T(8,128)(2,1)S(1)} %slice.6), channel_id=1, source_target_pairs={{0,8},{4,12},{8,0},{12,4},{16,24},{20,28},{24,16},{28,20},{1,9},{5... | collective-permute-start | bytes 589832 | tf_op jit(solution)/shard_map/ppermute | solution.py:388
  18.9 0.6 %collective-permute-done.9.refs_5_ = bf16[128,1536]{1,0:T(8,128)(2,1)S(1)} collective-permute-done((bf16[128,1536]{1,0:T(8,128)(2,1)S(1)}, bf16[128,1536]{1,0:T(8,128)(2,1)S(1)}, u32[]{:S(2)}, u32[]{:S(2)}) %collective-permute-start.9) | collective-permute-done | bytes 393248 | tf_op jit(solution)/shard_map/ppermute | solution.py:388
  19.4 4.7 %near.1 = (f32[40,128]{1,0:T(8,128)S(1)}, f32[240,1536]{1,0:T(8,128)S(1)}) custom-call(s32[1]{0:T(128)} %bitcast.4.ident_ref, bf16[1536,1536]{1,0:T(8,128)(2,1)S(1)} %order.1.weight_ref, bf16[128,1536]{1,0:T(8,128)(2,1)S(1)} %pack.1.own_ref.refs_0_, bf16[128,1536]{1,0:T(8,128)(2,1)S(1)} %collective-permute-done.7.refs_1_, ...), custom_call_target="tpu_custom_call" | custom-call | flops 3623878656 | bytes 4718592 | tf_op jit(solution)/shard_map/near/pallas_call | solution.py:466
  24.9 0.5 %collective-permute-start.11 = (bf16[128,768]{1,0:T(8,128)(2,1)S(1)}, bf16[128,768]{1,0:T(8,128)(2,1)S(1)}, u32[]{:S(2)}, u32[]{:S(2)}) collective-permute-start(bf16[128,768]{1,0:T(8,128)(2,1)S(1)} %collective-permute-done.6.refs_1_), channel_id=1, source_target_pairs={{0,4},{4,0},{8,12},{12,8},{16,20},{20,16},{24,28},{28,24},{1,5},{5... | collective-permute-start | bytes 589832 | tf_op jit(solution)/shard_map/ppermute | solution.py:388
  25.4 1.9 %collective-permute-start.4 = (bf16[24,1536]{1,0:T(8,128)(2,1)S(1)}, bf16[24,1536]{1,0:T(8,128)(2,1)S(1)}, u32[]{:S(2)}, u32[]{:S(2)}) collective-permute-start(bf16[24,1536]{1,0:T(8,128)(2,1)S(1)} %get-tuple-element.23), channel_id=1, source_target_pairs={{0,3},{1,0},{2,1},{3,2},{4,7},{5,4},{6,5},{7,6},{8,11},{9,8},{10,9... | collective-permute-start | bytes 221192 | tf_op jit(solution)/shard_map/ppermute | solution.py:429
  27.4 2.4 %far.1 = f32[1,128]{1,0:T(1,128)S(1)} custom-call(s32[1]{0:T(128)} %bitcast.4.ident_ref, s32[5]{0:T(128)S(1)} %get-tuple-element.24.place_ref, bf16[1536,1536]{1,0:T(8,128)(2,1)S(1)} %order.1.weight_ref, f32[40,128]{1,0:T(8,128)S(1)} %get-tuple-element.29.near_sum_ref, f32[240,1536]{1,0:T(8,128)S(1)} %get-tuple-element.30.late_ref, ...), custom_call_target="tpu_custom_call" | custom-call | flops 1207959552 | bytes 4718592 | tf_op jit(solution)/shard_map/far/pallas_call | solution.py:484
  29.9 1.1 %collective-permute-done.12 = f32[1,128]{1,0:T(1,128)S(1)} collective-permute-done((f32[1,128]{1,0:T(1,128)S(1)}, f32[1,128]{1,0:T(1,128)S(1)}, u32[]{:S(2)}, u32[]{:S(2)}) %collective-permute-start.12) | collective-permute-done | bytes 544 | tf_op jit(solution)/shard_map/ppermute | solution.py:388
  31.0 1.5 %collective-permute-start.13 = (f32[1,128]{1,0:T(1,128)S(1)}, f32[1,128]{1,0:T(1,128)S(1)}, u32[]{:S(2)}, u32[]{:S(2)}) collective-permute-start(f32[1,128]{1,0:T(1,128)S(1)} %add.18), channel_id=1, source_target_pairs={{0,8},{4,12},{8,0},{12,4},{16,24},{20,28},{24,16},{28,20},{1,9},{5... | collective-permute-start | bytes 1544 | tf_op jit(solution)/shard_map/ppermute | solution.py:388
  32.5 2.0 %collective-permute-done.13 = f32[1,128]{1,0:T(1,128)S(1)} collective-permute-done((f32[1,128]{1,0:T(1,128)S(1)}, f32[1,128]{1,0:T(1,128)S(1)}, u32[]{:S(2)}, u32[]{:S(2)}) %collective-permute-start.13) | collective-permute-done | bytes 544 | tf_op jit(solution)/shard_map/ppermute | solution.py:388
  34.5 1.5 %collective-permute-start.14 = (f32[1,128]{1,0:T(1,128)S(1)}, f32[1,128]{1,0:T(1,128)S(1)}, u32[]{:S(2)}, u32[]{:S(2)}) collective-permute-start(f32[1,128]{1,0:T(1,128)S(1)} %add.19), channel_id=1, source_target_pairs={{0,16},{4,20},{8,24},{12,28},{16,0},{20,4},{24,8},{28,12},{1,17},{... | collective-permute-start | bytes 1544 | tf_op jit(solution)/shard_map/ppermute | solution.py:388
  36.0 2.0 %collective-permute-done.14 = f32[1,128]{1,0:T(1,128)S(1)} collective-permute-done((f32[1,128]{1,0:T(1,128)S(1)}, f32[1,128]{1,0:T(1,128)S(1)}, u32[]{:S(2)}, u32[]{:S(2)}) %collective-permute-start.14) | collective-permute-done | bytes 544 | tf_op jit(solution)/shard_map/ppermute | solution.py:388
  38.2 3.5 %collective-permute-done.15 = f32[1,128]{1,0:T(1,128)S(1)} collective-permute-done((f32[1,128]{1,0:T(1,128)S(1)}, f32[1,128]{1,0:T(1,128)S(1)}, u32[]{:S(2)}, u32[]{:S(2)}) %collective-permute-start.15) | collective-permute-done | bytes 544 | tf_op jit(solution)/shard_map/ppermute | solution.py:518
  41.9 1.9 %assemble.1 = bf16[3,36864]{1,0:T(4,128)(2,1)} custom-call(s32[1]{0:T(128)} %bitcast.ident_ref, s32[5,4]{1,0:T(8,128)S(1)} %pad_add_fusion.table_ref, bf16[5,36864]{1,0:T(8,128)(2,1)S(1)} %copy-done.1, bf16[24,1536]{1,0:T(8,128)(2,1)S(1)} %collective-permute-done.2.refs_0_, bf16[24,1536]{1,0:T(8,128)(2,1)S(1)} %collective-permute-done.3.refs_1_, ...), custom_call_target="tpu_custom_call" | custom-call | tf_op jit(solution)/shard_map/assemble/pallas_call | solution.py:498
  43.8 2.2 %collective-permute-done.16 = f32[1,128]{1,0:T(1,128)S(1)} collective-permute-done((f32[1,128]{1,0:T(1,128)S(1)}, f32[1,128]{1,0:T(1,128)S(1)}, u32[]{:S(2)}, u32[]{:S(2)}) %collective-permute-start.16) | collective-permute-done | bytes 544 | tf_op jit(solution)/shard_map/ppermute | solution.py:518
  46.1 0.6 %multiply_bitcast_fusion = f32[3]{0:T(128)} fusion(f32[1,128]{1,0:T(1,128)S(1)} %add.22, s32[]{:T(128)S(6)} %select_n.3), kind=kLoop, calls=%fused_computation.1 | loop fusion | flops 3 | bytes 28 | tf_op jit(solution)/shard_map/mul | solution.py:521
  (29 shorter events, 2.6 us)
Async XLA Ops:
  0.6 1.1 %copy-start = (bf16[5,36864]{1,0:T(8,128)(2,1)S(1)}, bf16[5,36864]{1,0:T(8,128)(2,1)}, u32[]{:S(2)}) copy-start(bf16[5,36864]{1,0:T(8,128)(2,1)} %green_ref.3) | copy-start | bytes 1105924
  2.0 15.2 %collective-permute-start = (bf16[128,1536]{1,0:T(8,128)(2,1)S(1)}, bf16[128,1536]{1,0:T(8,128)(2,1)S(1)}, u32[]{:S(2)}, u32[]{:S(2)}) collective-permute-start(bf16[128,1536]{1,0:T(8,128)(2,1)S(1)} %pack.1.own_ref.refs_0_), channel_id=1, source_target_pairs={{0,8},{4,12},{8,0},{12,4},{16,24},{20,28},{24,16},{28,20},{1,9},{5... | collective-permute-start | bytes 1179656 | tf_op jit(solution)/shard_map/ppermute | solution.py:388
  5.0 12.2 %collective-permute-start.1 = (bf16[128,1536]{1,0:T(8,128)(2,1)S(1)}, bf16[128,1536]{1,0:T(8,128)(2,1)S(1)}, u32[]{:S(2)}, u32[]{:S(2)}) collective-permute-start(bf16[128,1536]{1,0:T(8,128)(2,1)S(1)} %pack.1.own_ref.refs_0_), channel_id=1, source_target_pairs={{0,16},{4,20},{8,24},{12,28},{16,0},{20,4},{24,8},{28,12},{1,17},{... | collective-permute-start | bytes 1179656 | tf_op jit(solution)/shard_map/ppermute | solution.py:388
  8.6 7.0 %collective-permute-start.2 = (bf16[24,1536]{1,0:T(8,128)(2,1)S(1)}, bf16[24,1536]{1,0:T(8,128)(2,1)S(1)}, u32[]{:S(2)}, u32[]{:S(2)}) collective-permute-start(bf16[24,1536]{1,0:T(8,128)(2,1)S(1)} %get-tuple-element.19), channel_id=1, source_target_pairs={{0,1},{1,2},{2,3},{3,0},{4,5},{5,6},{6,7},{7,4},{8,9},{9,10},{10,1... | collective-permute-start | bytes 221192 | tf_op jit(solution)/shard_map/ppermute | solution.py:429
  10.3 6.9 %collective-permute-start.3 = (bf16[24,1536]{1,0:T(8,128)(2,1)S(1)}, bf16[24,1536]{1,0:T(8,128)(2,1)S(1)}, u32[]{:S(2)}, u32[]{:S(2)}) collective-permute-start(bf16[24,1536]{1,0:T(8,128)(2,1)S(1)} %get-tuple-element.20), channel_id=1, source_target_pairs={{0,2},{1,3},{2,0},{3,1},{4,6},{5,7},{6,4},{7,5},{8,10},{9,11},{10,... | collective-permute-start | bytes 221192 | tf_op jit(solution)/shard_map/ppermute | solution.py:429
  12.8 6.0 %collective-permute-start.7 = (bf16[128,1536]{1,0:T(8,128)(2,1)S(1)}, bf16[128,1536]{1,0:T(8,128)(2,1)S(1)}, u32[]{:S(2)}, u32[]{:S(2)}) collective-permute-start(bf16[128,1536]{1,0:T(8,128)(2,1)S(1)} %pack.1.own_ref.refs_0_), channel_id=1, source_target_pairs={{0,4},{4,0},{8,12},{12,8},{16,20},{20,16},{24,28},{28,24},{1,5},{5... | collective-permute-start | bytes 1179656 | tf_op jit(solution)/shard_map/ppermute | solution.py:388
  17.2 1.7 %collective-permute-start.8 = (bf16[128,1536]{1,0:T(8,128)(2,1)S(1)}, bf16[128,1536]{1,0:T(8,128)(2,1)S(1)}, u32[]{:S(2)}, u32[]{:S(2)}) collective-permute-start(bf16[128,1536]{1,0:T(8,128)(2,1)S(1)} %collective-permute-done.refs_2_), channel_id=1, source_target_pairs={{0,4},{4,0},{8,12},{12,8},{16,20},{20,16},{24,28},{28,24},{1,5},{5... | collective-permute-start | bytes 1179656 | tf_op jit(solution)/shard_map/ppermute | solution.py:388
  17.2 2.3 %collective-permute-start.9 = (bf16[128,1536]{1,0:T(8,128)(2,1)S(1)}, bf16[128,1536]{1,0:T(8,128)(2,1)S(1)}, u32[]{:S(2)}, u32[]{:S(2)}) collective-permute-start(bf16[128,1536]{1,0:T(8,128)(2,1)S(1)} %collective-permute-done.1.refs_4_), channel_id=1, source_target_pairs={{0,4},{4,0},{8,12},{12,8},{16,20},{20,16},{24,28},{28,24},{1,5},{5... | collective-permute-start | bytes 1179656 | tf_op jit(solution)/shard_map/ppermute | solution.py:388
  17.7 6.9 %collective-permute-start.5 = (bf16[128,768]{1,0:T(8,128)(2,1)S(1)}, bf16[128,768]{1,0:T(8,128)(2,1)S(1)}, u32[]{:S(2)}, u32[]{:S(2)}) collective-permute-start(bf16[128,768]{1,0:T(8,128)(2,1)S(1)} %slice.6), channel_id=1, source_target_pairs={{0,8},{4,12},{8,0},{12,4},{16,24},{20,28},{24,16},{28,20},{1,9},{5... | collective-permute-start | bytes 589832 | tf_op jit(solution)/shard_map/ppermute | solution.py:388
  18.3 6.6 %collective-permute-start.6 = (bf16[128,768]{1,0:T(8,128)(2,1)S(1)}, bf16[128,768]{1,0:T(8,128)(2,1)S(1)}, u32[]{:S(2)}, u32[]{:S(2)}) collective-permute-start(bf16[128,768]{1,0:T(8,128)(2,1)S(1)} %slice.7), channel_id=1, source_target_pairs={{0,16},{4,20},{8,24},{12,28},{16,0},{20,4},{24,8},{28,12},{1,17},{... | collective-permute-start | bytes 589832 | tf_op jit(solution)/shard_map/ppermute | solution.py:388
  24.2 17.8 %copy-start.1 = (bf16[5,36864]{1,0:T(8,128)(2,1)S(1)}, bf16[5,36864]{1,0:T(8,128)(2,1)}, u32[]{:S(2)}) copy-start(bf16[5,36864]{1,0:T(8,128)(2,1)} %green_ref.3) | copy-start | bytes 1105924
  24.9 2.5 %collective-permute-start.10 = (bf16[128,768]{1,0:T(8,128)(2,1)S(1)}, bf16[128,768]{1,0:T(8,128)(2,1)S(1)}, u32[]{:S(2)}, u32[]{:S(2)}) collective-permute-start(bf16[128,768]{1,0:T(8,128)(2,1)S(1)} %collective-permute-done.5.refs_0_), channel_id=1, source_target_pairs={{0,4},{4,0},{8,12},{12,8},{16,20},{20,16},{24,28},{28,24},{1,5},{5... | collective-permute-start | bytes 589832 | tf_op jit(solution)/shard_map/ppermute | solution.py:388
  24.9 2.5 %collective-permute-start.11 = (bf16[128,768]{1,0:T(8,128)(2,1)S(1)}, bf16[128,768]{1,0:T(8,128)(2,1)S(1)}, u32[]{:S(2)}, u32[]{:S(2)}) collective-permute-start(bf16[128,768]{1,0:T(8,128)(2,1)S(1)} %collective-permute-done.6.refs_1_), channel_id=1, source_target_pairs={{0,4},{4,0},{8,12},{12,8},{16,20},{20,16},{24,28},{28,24},{1,5},{5... | collective-permute-start | bytes 589832 | tf_op jit(solution)/shard_map/ppermute | solution.py:388
  25.4 16.5 %collective-permute-start.4 = (bf16[24,1536]{1,0:T(8,128)(2,1)S(1)}, bf16[24,1536]{1,0:T(8,128)(2,1)S(1)}, u32[]{:S(2)}, u32[]{:S(2)}) collective-permute-start(bf16[24,1536]{1,0:T(8,128)(2,1)S(1)} %get-tuple-element.23), channel_id=1, source_target_pairs={{0,3},{1,0},{2,1},{3,2},{4,7},{5,4},{6,5},{7,6},{8,11},{9,8},{10,9... | collective-permute-start | bytes 221192 | tf_op jit(solution)/shard_map/ppermute | solution.py:429
  29.8 1.2 %collective-permute-start.12 = (f32[1,128]{1,0:T(1,128)S(1)}, f32[1,128]{1,0:T(1,128)S(1)}, u32[]{:S(2)}, u32[]{:S(2)}) collective-permute-start(f32[1,128]{1,0:T(1,128)S(1)} %far.1), channel_id=1, source_target_pairs={{0,4},{4,0},{8,12},{12,8},{16,20},{20,16},{24,28},{28,24},{1,5},{5... | collective-permute-start | bytes 1544 | tf_op jit(solution)/shard_map/ppermute | solution.py:388
  31.0 3.5 %collective-permute-start.13 = (f32[1,128]{1,0:T(1,128)S(1)}, f32[1,128]{1,0:T(1,128)S(1)}, u32[]{:S(2)}, u32[]{:S(2)}) collective-permute-start(f32[1,128]{1,0:T(1,128)S(1)} %add.18), channel_id=1, source_target_pairs={{0,8},{4,12},{8,0},{12,4},{16,24},{20,28},{24,16},{28,20},{1,9},{5... | collective-permute-start | bytes 1544 | tf_op jit(solution)/shard_map/ppermute | solution.py:388
  34.5 3.5 %collective-permute-start.14 = (f32[1,128]{1,0:T(1,128)S(1)}, f32[1,128]{1,0:T(1,128)S(1)}, u32[]{:S(2)}, u32[]{:S(2)}) collective-permute-start(f32[1,128]{1,0:T(1,128)S(1)} %add.19), channel_id=1, source_target_pairs={{0,16},{4,20},{8,24},{12,28},{16,0},{20,4},{24,8},{28,12},{1,17},{... | collective-permute-start | bytes 1544 | tf_op jit(solution)/shard_map/ppermute | solution.py:388
  38.1 3.5 %collective-permute-start.15 = (f32[1,128]{1,0:T(1,128)S(1)}, f32[1,128]{1,0:T(1,128)S(1)}, u32[]{:S(2)}, u32[]{:S(2)}) collective-permute-start(f32[1,128]{1,0:T(1,128)S(1)} %add.20), channel_id=1, source_target_pairs={{0,1},{1,0},{2,3},{3,2},{4,5},{5,4},{6,7},{7,6},{8,9},{9,8},{10,11... | collective-permute-start | bytes 1544 | tf_op jit(solution)/shard_map/ppermute | solution.py:518
  41.6 4.4 %collective-permute-start.16 = (f32[1,128]{1,0:T(1,128)S(1)}, f32[1,128]{1,0:T(1,128)S(1)}, u32[]{:S(2)}, u32[]{:S(2)}) collective-permute-start(f32[1,128]{1,0:T(1,128)S(1)} %add.21), channel_id=1, source_target_pairs={{0,2},{1,3},{2,0},{3,1},{4,6},{5,7},{6,4},{7,5},{8,10},{9,11},{10,... | collective-permute-start | bytes 1544 | tf_op jit(solution)/shard_map/ppermute | solution.py:518
where the time goes:
time: 46.8 us; the launch traced here: 46.6 us
  starting transfers between devices  16.3 us (35%)
  waiting for transfers between devices  13.7 us (29%)
  Pallas kernels  13.5 us (29%)
  other arithmetic  1.31 us (3%)
  local copies, waits for them, and re-layouts  1.09 us (2%)
  between operations  0.73 us (2%)
    ppermute x12, starting transfers between devices, swap(): lax.ppermute(value, 'block', [(index, index ^ mask) for index in range(bl...  9.73 us
    ppermute x12, waiting for transfers between devices, swap(): lax.ppermute(value, 'block', [(index, index ^ mask) for index in range(bl...  6.56 us
    ppermute x3, starting transfers between devices, body(): lax.ppermute(leaving[shift - 1], 'walker', [(z, (z + shift) % walkers) fo...  6.15 us
    ppermute x2, waiting for transfers between devices, body(): all_sums = all_sums + lax.ppermute(all_sums, 'walker', pairs)  5.66 us
    pallas_call x1, Pallas kernels, body(): pl.pallas_call(functools.partial(near_kernel, dims), out_shape=[jax.Shape...  4.71 us
    pallas_call x1, Pallas kernels, body(): pl.pallas_call(functools.partial(order_kernel, (group, groups, chip_rows)...  2.76 us
    pallas_call x1, Pallas kernels, body(): pl.pallas_call(functools.partial(far_kernel, dims), out_shape=jax.ShapeDt...  2.41 us
    pallas_call x1, Pallas kernels, body(): pl.pallas_call(functools.partial(assemble_kernel, move_dims), out_shape=j...  1.93 us
  transfers between devices with their start and end apart: 17, of which 10 were waited for; matrix products, arithmetic and copies ran while one was open for 2% of the time, Pallas kernels for 28%

commit v1 on v0

--- a/solution.py
+++ b/solution.py
@@ -381,7 +381,7 @@
     for slot in range(slots):
         slot_sum = jnp.sum(once[slot] + 2.0 * twice[slot])
         value = jnp.where(lane == place_ref[slot], slot_sum, value)
-    sum_ref[...] = value
+    sum_ref[...] = jnp.broadcast_to(value, sum_ref.shape)
 
 
 def swap(value, mask, blocks):
@@ -483,7 +483,7 @@
     far_pieces = far + [swap(piece, core, blocks) for piece in far]
     all_sums = pl.pallas_call(
         functools.partial(far_kernel, dims),
-        out_shape=jax.ShapeDtypeStruct((1, LANES), jnp.float32),
+        out_shape=jax.ShapeDtypeStruct((blocks * walkers, LANES), jnp.float32),
         in_specs=[smem] * 2 + [vmem] * 7,
         out_specs=vmem,
         scratch_shapes=[pltpu.VMEM((slots * chip_rows, group * occ_count), jnp.float32)] * groups,
@@ -510,14 +510,11 @@
     )(walker_index, table, green, *coming)
 
     energy_scale = 0.5 / (occ_count * math.sqrt(vectors * blocks))
-    for mask in (core, near_x, near_y):
-        all_sums = all_sums + swap(all_sums, mask, blocks)
-    mask = 1
-    while mask < walkers:
-        pairs = [(index, index ^ mask) for index in range(walkers)]
-        all_sums = all_sums + lax.ppermute(all_sums, "walker", pairs)
-        mask *= 2
-    own_sums = lax.dynamic_slice(all_sums[0], (walker_index[0] * keep,), (keep,))
+    got = lax.all_to_all(
+        all_sums, ("block", "walker"), split_axis=0, concat_axis=0, tiled=True
+    )
+    got_sums = jnp.sum(got, axis=0)
+    own_sums = lax.dynamic_slice(got_sums, (walker_index[0] * keep,), (keep,))
     return (new_green, -energy_scale * own_sums)
 
 

time: 46.8 us -> 41.9 us (0.90)
  waiting for transfers between devices: 13.7 us -> 8.12 us
  Pallas kernels: 13.5 us -> 14.1 us
    ppermute x2 -> x0, waiting for transfers between devices: 5.66 us -> none  [body(): all_sums = all_sums + lax.ppermute(all_sums, 'walker', pairs)]
    all_to_all x0 -> x1, waiting for transfers between devices: none -> 5.21 us  [body(): lax.all_to_all(all_sums, ('block', 'walker'), split_axis=0, concat_axis=0...]
    ppermute x12 -> x9, waiting for transfers between devices: 6.56 us -> 1.38 us  [swap(): lax.ppermute(value, 'block', [(index, index ^ mask) for index in range(bl...]
    all_to_all x0 -> x1, starting transfers between devices: none -> 3.45 us  [body(): lax.all_to_all(all_sums, ('block', 'walker'), split_axis=0, concat_axis=0...]
    ppermute x12 -> x9, starting transfers between devices: 9.73 us -> 6.65 us  [swap(): lax.ppermute(value, 'block', [(index, index ^ mask) for index in range(bl...]
    pallas_call x1, Pallas kernels: 2.41 us -> 3.01 us  [body(): pl.pallas_call(functools.partial(far_kernel, dims), out_shape=jax.ShapeDt...]
  transfers between devices with their start and end apart: 17 -> 13, of which waited for: 10 -> 6; matrix products, arithmetic and copies ran while one was open for 2% -> 2% of each run, Pallas kernels for 28% -> 33%
where the time goes in v1:
time: 41.9 us; the launch traced here: 41.6 us
  starting transfers between devices  16.3 us (39%)
  Pallas kernels  14.1 us (34%)
  waiting for transfers between devices  8.12 us (19%)
  other arithmetic  1.34 us (3%)
  local copies, waits for them, and re-layouts  1.09 us (3%)
  between operations  0.74 us (2%)
    ppermute x9, starting transfers between devices, swap(): lax.ppermute(value, 'block', [(index, index ^ mask) for index in range(bl...  6.65 us
    ppermute x3, starting transfers between devices, body(): lax.ppermute(leaving[shift - 1], 'walker', [(z, (z + shift) % walkers) fo...  6.15 us
    all_to_all x1, waiting for transfers between devices, body(): lax.all_to_all(all_sums, ('block', 'walker'), split_axis=0, concat_axis=0...  5.21 us
    pallas_call x1, Pallas kernels, body(): pl.pallas_call(functools.partial(near_kernel, dims), out_shape=[jax.Shape...  4.71 us
    all_to_all x1, starting transfers between devices, body(): lax.all_to_all(all_sums, ('block', 'walker'), split_axis=0, concat_axis=0...  3.45 us
    pallas_call x1, Pallas kernels, body(): pl.pallas_call(functools.partial(far_kernel, dims), out_shape=jax.ShapeDt...  3.01 us
    pallas_call x1, Pallas kernels, body(): pl.pallas_call(functools.partial(order_kernel, (group, groups, chip_rows)...  2.76 us
    pallas_call x1, Pallas kernels, body(): pl.pallas_call(functools.partial(assemble_kernel, move_dims), out_shape=j...  1.93 us
  transfers between devices with their start and end apart: 13, of which 6 were waited for; matrix products, arithmetic and copies ran while one was open for 2% of the time, Pallas kernels for 33%

profile of v1, /device:TPU:0, one launch (start us, length us, event | category | flops | bytes accessed | tf_op | source)
XLA Modules:
  0.0 41.6 jit_solution(5130722110825052659)
XLA Ops:
  0.6 1.1 %copy-done = bf16[5,36864]{1,0:T(8,128)(2,1)S(1)} copy-done((bf16[5,36864]{1,0:T(8,128)(2,1)S(1)}, bf16[5,36864]{1,0:T(8,128)(2,1)}, u32[]{:S(2)}) %copy-start) | copy-done | bytes 368664
  1.7 0.3 pack.1.own_ref.refs_0_
  2.0 3.0 %collective-permute-start = (bf16[128,1536]{1,0:T(8,128)(2,1)S(1)}, bf16[128,1536]{1,0:T(8,128)(2,1)S(1)}, u32[]{:S(2)}, u32[]{:S(2)}) collective-permute-start(bf16[128,1536]{1,0:T(8,128)(2,1)S(1)} %pack.1.own_ref.refs_0_), channel_id=1, source_target_pairs={{0,8},{4,12},{8,0},{12,4},{16,24},{20,28},{24,16},{28,20},{1,9},{5... | collective-permute-start | bytes 1179656 | tf_op jit(solution)/shard_map/ppermute | solution.py:388
  5.0 1.5 %collective-permute-start.1 = (bf16[128,1536]{1,0:T(8,128)(2,1)S(1)}, bf16[128,1536]{1,0:T(8,128)(2,1)S(1)}, u32[]{:S(2)}, u32[]{:S(2)}) collective-permute-start(bf16[128,1536]{1,0:T(8,128)(2,1)S(1)} %pack.1.own_ref.refs_0_), channel_id=1, source_target_pairs={{0,16},{4,20},{8,24},{12,28},{16,0},{20,4},{24,8},{28,12},{1,17},{... | collective-permute-start | bytes 1179656 | tf_op jit(solution)/shard_map/ppermute | solution.py:388
  6.5 0.7 %pad_add_fusion.table_ref = s32[5,4]{1,0:T(8,128)S(1)} fusion(s32[2,4]{1,0:T(2,128)} %bitcast.8, s32[2,4]{1,0:T(2,128)} %bitcast.9, s32[1,4]{1,0:T(1,128)} %bitcast.10), kind=kLoop, calls=%fused_computation | loop fusion | flops 40 | bytes 160 | tf_op jit(solution)/shard_map/concatenate | solution.py:400
  7.2 1.4 %leave.1 = (bf16[24,1536]{1,0:T(8,128)(2,1)S(1)}, bf16[24,1536]{1,0:T(8,128)(2,1)S(1)}, bf16[24,1536]{1,0:T(8,128)(2,1)S(1)}, s32[5]{0:T(128)S(1)}) custom-call(s32[1]{0:T(128)} %bitcast.ident_ref, s32[5,4]{1,0:T(8,128)S(1)} %pad_add_fusion.table_ref, bf16[128,1536]{1,0:T(8,128)(2,1)S(1)} %pack.1.own_ref.refs_0_), custom_call_target="tpu_custom_call" | custom-call | tf_op jit(solution)/shard_map/leave/pallas_call | solution.py:418
  8.6 1.6 %collective-permute-start.2 = (bf16[24,1536]{1,0:T(8,128)(2,1)S(1)}, bf16[24,1536]{1,0:T(8,128)(2,1)S(1)}, u32[]{:S(2)}, u32[]{:S(2)}) collective-permute-start(bf16[24,1536]{1,0:T(8,128)(2,1)S(1)} %get-tuple-element.19), channel_id=1, source_target_pairs={{0,1},{1,2},{2,3},{3,0},{4,5},{5,6},{6,7},{7,4},{8,9},{9,10},{10,1... | collective-permute-start | bytes 221192 | tf_op jit(solution)/shard_map/ppermute | solution.py:429
  10.3 2.6 %collective-permute-start.3 = (bf16[24,1536]{1,0:T(8,128)(2,1)S(1)}, bf16[24,1536]{1,0:T(8,128)(2,1)S(1)}, u32[]{:S(2)}, u32[]{:S(2)}) collective-permute-start(bf16[24,1536]{1,0:T(8,128)(2,1)S(1)} %get-tuple-element.20), channel_id=1, source_target_pairs={{0,2},{1,3},{2,0},{3,1},{4,6},{5,7},{6,4},{7,5},{8,10},{9,11},{10,... | collective-permute-start | bytes 221192 | tf_op jit(solution)/shard_map/ppermute | solution.py:429
  12.9 2.8 %order.1.weight_ref = bf16[1536,1536]{1,0:T(8,128)(2,1)S(1)} custom-call(s32[1]{0:T(128)} %bitcast.4.ident_ref, bf16[8,192,1536]{2,1,0:T(8,128)(2,1)} %chol_ref.1, bf16[128,1536]{1,0:T(8,128)(2,1)S(1)} %pack.1.own_ref.refs_0_), custom_call_target="tpu_custom_call" | custom-call | bytes 9437184 | tf_op jit(solution)/shard_map/order/pallas_call | solution.py:438
  15.6 1.5 %collective-permute-done.3.refs_1_ = bf16[24,1536]{1,0:T(8,128)(2,1)S(1)} collective-permute-done((bf16[24,1536]{1,0:T(8,128)(2,1)S(1)}, bf16[24,1536]{1,0:T(8,128)(2,1)S(1)}, u32[]{:S(2)}, u32[]{:S(2)}) %collective-permute-start.3) | collective-permute-done | bytes 73760 | tf_op jit(solution)/shard_map/ppermute | solution.py:429
  17.2 0.5 %collective-permute-start.9 = (bf16[128,1536]{1,0:T(8,128)(2,1)S(1)}, bf16[128,1536]{1,0:T(8,128)(2,1)S(1)}, u32[]{:S(2)}, u32[]{:S(2)}) collective-permute-start(bf16[128,1536]{1,0:T(8,128)(2,1)S(1)} %collective-permute-done.1.refs_4_), channel_id=1, source_target_pairs={{0,4},{4,0},{8,12},{12,8},{16,20},{20,16},{24,28},{28,24},{1,5},{5... | collective-permute-start | bytes 1179656 | tf_op jit(solution)/shard_map/ppermute | solution.py:388
  17.7 0.6 %collective-permute-start.5 = (bf16[128,768]{1,0:T(8,128)(2,1)S(1)}, bf16[128,768]{1,0:T(8,128)(2,1)S(1)}, u32[]{:S(2)}, u32[]{:S(2)}) collective-permute-start(bf16[128,768]{1,0:T(8,128)(2,1)S(1)} %slice.6), channel_id=1, source_target_pairs={{0,8},{4,12},{8,0},{12,4},{16,24},{20,28},{24,16},{28,20},{1,9},{5... | collective-permute-start | bytes 589832 | tf_op jit(solution)/shard_map/ppermute | solution.py:388
  18.3 0.5 %collective-permute-start.6 = (bf16[128,768]{1,0:T(8,128)(2,1)S(1)}, bf16[128,768]{1,0:T(8,128)(2,1)S(1)}, u32[]{:S(2)}, u32[]{:S(2)}) collective-permute-start(bf16[128,768]{1,0:T(8,128)(2,1)S(1)} %slice.7), channel_id=1, source_target_pairs={{0,16},{4,20},{8,24},{12,28},{16,0},{20,4},{24,8},{28,12},{1,17},{... | collective-permute-start | bytes 589832 | tf_op jit(solution)/shard_map/ppermute | solution.py:388
  18.9 0.6 %collective-permute-done.9.refs_5_ = bf16[128,1536]{1,0:T(8,128)(2,1)S(1)} collective-permute-done((bf16[128,1536]{1,0:T(8,128)(2,1)S(1)}, bf16[128,1536]{1,0:T(8,128)(2,1)S(1)}, u32[]{:S(2)}, u32[]{:S(2)}) %collective-permute-start.9) | collective-permute-done | bytes 393248 | tf_op jit(solution)/shard_map/ppermute | solution.py:388
  19.4 4.7 %near.1 = (f32[40,128]{1,0:T(8,128)S(1)}, f32[240,1536]{1,0:T(8,128)S(1)}) custom-call(s32[1]{0:T(128)} %bitcast.4.ident_ref, bf16[1536,1536]{1,0:T(8,128)(2,1)S(1)} %order.1.weight_ref, bf16[128,1536]{1,0:T(8,128)(2,1)S(1)} %pack.1.own_ref.refs_0_, bf16[128,1536]{1,0:T(8,128)(2,1)S(1)} %collective-permute-done.7.refs_1_, ...), custom_call_target="tpu_custom_call" | custom-call | flops 3623878656 | bytes 4718592 | tf_op jit(solution)/shard_map/near/pallas_call | solution.py:466
  24.2 0.5 %collective-permute-done.5.refs_0_ = bf16[128,768]{1,0:T(8,128)(2,1)S(1)} collective-permute-done((bf16[128,768]{1,0:T(8,128)(2,1)S(1)}, bf16[128,768]{1,0:T(8,128)(2,1)S(1)}, u32[]{:S(2)}, u32[]{:S(2)}) %collective-permute-start.5) | collective-permute-done | bytes 196640 | tf_op jit(solution)/shard_map/ppermute | solution.py:388
  24.7 0.3 collective-permute-done.6.refs_1_
  24.9 0.5 %collective-permute-start.11 = (bf16[128,768]{1,0:T(8,128)(2,1)S(1)}, bf16[128,768]{1,0:T(8,128)(2,1)S(1)}, u32[]{:S(2)}, u32[]{:S(2)}) collective-permute-start(bf16[128,768]{1,0:T(8,128)(2,1)S(1)} %collective-permute-done.6.refs_1_), channel_id=1, source_target_pairs={{0,4},{4,0},{8,12},{12,8},{16,20},{20,16},{24,28},{28,24},{1,5},{5... | collective-permute-start | bytes 589832 | tf_op jit(solution)/shard_map/ppermute | solution.py:388
  25.4 1.9 %collective-permute-start.4 = (bf16[24,1536]{1,0:T(8,128)(2,1)S(1)}, bf16[24,1536]{1,0:T(8,128)(2,1)S(1)}, u32[]{:S(2)}, u32[]{:S(2)}) collective-permute-start(bf16[24,1536]{1,0:T(8,128)(2,1)S(1)} %get-tuple-element.23), channel_id=1, source_target_pairs={{0,3},{1,0},{2,1},{3,2},{4,7},{5,4},{6,5},{7,6},{8,11},{9,8},{10,9... | collective-permute-start | bytes 221192 | tf_op jit(solution)/shard_map/ppermute | solution.py:429
  27.4 3.0 %far.1 = f32[32,128]{1,0:T(8,128)} custom-call(s32[1]{0:T(128)} %bitcast.4.ident_ref, s32[5]{0:T(128)S(1)} %get-tuple-element.24.place_ref, bf16[1536,1536]{1,0:T(8,128)(2,1)S(1)} %order.1.weight_ref, f32[40,128]{1,0:T(8,128)S(1)} %get-tuple-element.29.near_sum_ref, f32[240,1536]{1,0:T(8,128)S(1)} %get-tuple-element.30.late_ref, ...), custom_call_target="tpu_custom_call" | custom-call | flops 1207959552 | bytes 4718592 | tf_op jit(solution)/shard_map/far/pallas_call | solution.py:484
  30.4 3.5 %all-to-all-start = ((f32[32,1,128]{2,1,0:T(1,128)}), f32[32,1,128]{2,1,0:T(1,128)S(1)}, u32[]{:S(2)}, u32[]{:S(2)}) async-start(f32[32,1,128]{2,1,0:T(1,128)} %bitcast.6), calls=%async_computation | async-start | bytes 32768 | tf_op jit(solution)/shard_map/all_to_all | solution.py:513
  33.9 1.9 %assemble.1 = bf16[3,36864]{1,0:T(4,128)(2,1)} custom-call(s32[1]{0:T(128)} %bitcast.ident_ref, s32[5,4]{1,0:T(8,128)S(1)} %pad_add_fusion.table_ref, bf16[5,36864]{1,0:T(8,128)(2,1)S(1)} %copy-done.1, bf16[24,1536]{1,0:T(8,128)(2,1)S(1)} %collective-permute-done.2.refs_0_, bf16[24,1536]{1,0:T(8,128)(2,1)S(1)} %collective-permute-done.3.refs_1_, ...), custom_call_target="tpu_custom_call" | custom-call | tf_op jit(solution)/shard_map/assemble/pallas_call | solution.py:498
  35.8 5.2 %all-to-all-done = f32[32,1,128]{2,1,0:T(1,128)S(1)} async-done(((f32[32,1,128]{2,1,0:T(1,128)}), f32[32,1,128]{2,1,0:T(1,128)S(1)}, u32[]{:S(2)}, u32[]{:S(2)}) %all-to-all-start) | async-done | bytes 16416 | tf_op jit(solution)/shard_map/all_to_all | solution.py:513
  41.0 0.6 %dynamic-slice_multiply_fusion = f32[3]{0:T(128)} fusion(f32[128]{0:T(128)S(1)} %reduce_sum.9, s32[]{:T(128)S(6)} %select_n.3), kind=kLoop, calls=%fused_computation.1 | loop fusion | flops 3 | bytes 28 | tf_op jit(solution)/shard_map/mul | solution.py:518
  (17 shorter events, 0.2 us)
Async XLA Ops:
  0.6 1.1 %copy-start = (bf16[5,36864]{1,0:T(8,128)(2,1)S(1)}, bf16[5,36864]{1,0:T(8,128)(2,1)}, u32[]{:S(2)}) copy-start(bf16[5,36864]{1,0:T(8,128)(2,1)} %green_ref.3) | copy-start | bytes 1105924
  2.0 15.2 %collective-permute-start = (bf16[128,1536]{1,0:T(8,128)(2,1)S(1)}, bf16[128,1536]{1,0:T(8,128)(2,1)S(1)}, u32[]{:S(2)}, u32[]{:S(2)}) collective-permute-start(bf16[128,1536]{1,0:T(8,128)(2,1)S(1)} %pack.1.own_ref.refs_0_), channel_id=1, source_target_pairs={{0,8},{4,12},{8,0},{12,4},{16,24},{20,28},{24,16},{28,20},{1,9},{5... | collective-permute-start | bytes 1179656 | tf_op jit(solution)/shard_map/ppermute | solution.py:388
  5.0 12.2 %collective-permute-start.1 = (bf16[128,1536]{1,0:T(8,128)(2,1)S(1)}, bf16[128,1536]{1,0:T(8,128)(2,1)S(1)}, u32[]{:S(2)}, u32[]{:S(2)}) collective-permute-start(bf16[128,1536]{1,0:T(8,128)(2,1)S(1)} %pack.1.own_ref.refs_0_), channel_id=1, source_target_pairs={{0,16},{4,20},{8,24},{12,28},{16,0},{20,4},{24,8},{28,12},{1,17},{... | collective-permute-start | bytes 1179656 | tf_op jit(solution)/shard_map/ppermute | solution.py:388
  8.6 7.0 %collective-permute-start.2 = (bf16[24,1536]{1,0:T(8,128)(2,1)S(1)}, bf16[24,1536]{1,0:T(8,128)(2,1)S(1)}, u32[]{:S(2)}, u32[]{:S(2)}) collective-permute-start(bf16[24,1536]{1,0:T(8,128)(2,1)S(1)} %get-tuple-element.19), channel_id=1, source_target_pairs={{0,1},{1,2},{2,3},{3,0},{4,5},{5,6},{6,7},{7,4},{8,9},{9,10},{10,1... | collective-permute-start | bytes 221192 | tf_op jit(solution)/shard_map/ppermute | solution.py:429
  10.3 6.9 %collective-permute-start.3 = (bf16[24,1536]{1,0:T(8,128)(2,1)S(1)}, bf16[24,1536]{1,0:T(8,128)(2,1)S(1)}, u32[]{:S(2)}, u32[]{:S(2)}) collective-permute-start(bf16[24,1536]{1,0:T(8,128)(2,1)S(1)} %get-tuple-element.20), channel_id=1, source_target_pairs={{0,2},{1,3},{2,0},{3,1},{4,6},{5,7},{6,4},{7,5},{8,10},{9,11},{10,... | collective-permute-start | bytes 221192 | tf_op jit(solution)/shard_map/ppermute | solution.py:429
  12.8 6.0 %collective-permute-start.7 = (bf16[128,1536]{1,0:T(8,128)(2,1)S(1)}, bf16[128,1536]{1,0:T(8,128)(2,1)S(1)}, u32[]{:S(2)}, u32[]{:S(2)}) collective-permute-start(bf16[128,1536]{1,0:T(8,128)(2,1)S(1)} %pack.1.own_ref.refs_0_), channel_id=1, source_target_pairs={{0,4},{4,0},{8,12},{12,8},{16,20},{20,16},{24,28},{28,24},{1,5},{5... | collective-permute-start | bytes 1179656 | tf_op jit(solution)/shard_map/ppermute | solution.py:388
  17.2 1.7 %collective-permute-start.8 = (bf16[128,1536]{1,0:T(8,128)(2,1)S(1)}, bf16[128,1536]{1,0:T(8,128)(2,1)S(1)}, u32[]{:S(2)}, u32[]{:S(2)}) collective-permute-start(bf16[128,1536]{1,0:T(8,128)(2,1)S(1)} %collective-permute-done.refs_2_), channel_id=1, source_target_pairs={{0,4},{4,0},{8,12},{12,8},{16,20},{20,16},{24,28},{28,24},{1,5},{5... | collective-permute-start | bytes 1179656 | tf_op jit(solution)/shard_map/ppermute | solution.py:388
  17.2 2.3 %collective-permute-start.9 = (bf16[128,1536]{1,0:T(8,128)(2,1)S(1)}, bf16[128,1536]{1,0:T(8,128)(2,1)S(1)}, u32[]{:S(2)}, u32[]{:S(2)}) collective-permute-start(bf16[128,1536]{1,0:T(8,128)(2,1)S(1)} %collective-permute-done.1.refs_4_), channel_id=1, source_target_pairs={{0,4},{4,0},{8,12},{12,8},{16,20},{20,16},{24,28},{28,24},{1,5},{5... | collective-permute-start | bytes 1179656 | tf_op jit(solution)/shard_map/ppermute | solution.py:388
  17.7 6.9 %collective-permute-start.5 = (bf16[128,768]{1,0:T(8,128)(2,1)S(1)}, bf16[128,768]{1,0:T(8,128)(2,1)S(1)}, u32[]{:S(2)}, u32[]{:S(2)}) collective-permute-start(bf16[128,768]{1,0:T(8,128)(2,1)S(1)} %slice.6), channel_id=1, source_target_pairs={{0,8},{4,12},{8,0},{12,4},{16,24},{20,28},{24,16},{28,20},{1,9},{5... | collective-permute-start | bytes 589832 | tf_op jit(solution)/shard_map/ppermute | solution.py:388
  18.3 6.6 %collective-permute-start.6 = (bf16[128,768]{1,0:T(8,128)(2,1)S(1)}, bf16[128,768]{1,0:T(8,128)(2,1)S(1)}, u32[]{:S(2)}, u32[]{:S(2)}) collective-permute-start(bf16[128,768]{1,0:T(8,128)(2,1)S(1)} %slice.7), channel_id=1, source_target_pairs={{0,16},{4,20},{8,24},{12,28},{16,0},{20,4},{24,8},{28,12},{1,17},{... | collective-permute-start | bytes 589832 | tf_op jit(solution)/shard_map/ppermute | solution.py:388
  24.2 9.7 %copy-start.1 = (bf16[5,36864]{1,0:T(8,128)(2,1)S(1)}, bf16[5,36864]{1,0:T(8,128)(2,1)}, u32[]{:S(2)}) copy-start(bf16[5,36864]{1,0:T(8,128)(2,1)} %green_ref.3) | copy-start | bytes 1105924
  24.9 2.5 %collective-permute-start.10 = (bf16[128,768]{1,0:T(8,128)(2,1)S(1)}, bf16[128,768]{1,0:T(8,128)(2,1)S(1)}, u32[]{:S(2)}, u32[]{:S(2)}) collective-permute-start(bf16[128,768]{1,0:T(8,128)(2,1)S(1)} %collective-permute-done.5.refs_0_), channel_id=1, source_target_pairs={{0,4},{4,0},{8,12},{12,8},{16,20},{20,16},{24,28},{28,24},{1,5},{5... | collective-permute-start | bytes 589832 | tf_op jit(solution)/shard_map/ppermute | solution.py:388
  24.9 2.5 %collective-permute-start.11 = (bf16[128,768]{1,0:T(8,128)(2,1)S(1)}, bf16[128,768]{1,0:T(8,128)(2,1)S(1)}, u32[]{:S(2)}, u32[]{:S(2)}) collective-permute-start(bf16[128,768]{1,0:T(8,128)(2,1)S(1)} %collective-permute-done.6.refs_1_), channel_id=1, source_target_pairs={{0,4},{4,0},{8,12},{12,8},{16,20},{20,16},{24,28},{28,24},{1,5},{5... | collective-permute-start | bytes 589832 | tf_op jit(solution)/shard_map/ppermute | solution.py:388
  25.4 8.4 %collective-permute-start.4 = (bf16[24,1536]{1,0:T(8,128)(2,1)S(1)}, bf16[24,1536]{1,0:T(8,128)(2,1)S(1)}, u32[]{:S(2)}, u32[]{:S(2)}) collective-permute-start(bf16[24,1536]{1,0:T(8,128)(2,1)S(1)} %get-tuple-element.23), channel_id=1, source_target_pairs={{0,3},{1,0},{2,1},{3,2},{4,7},{5,4},{6,5},{7,6},{8,11},{9,8},{10,9... | collective-permute-start | bytes 221192 | tf_op jit(solution)/shard_map/ppermute | solution.py:429
  30.4 10.6 %all-to-all-start = ((f32[32,1,128]{2,1,0:T(1,128)}), f32[32,1,128]{2,1,0:T(1,128)S(1)}, u32[]{:S(2)}, u32[]{:S(2)}) async-start(f32[32,1,128]{2,1,0:T(1,128)} %bitcast.6), calls=%async_computation | async-start | bytes 32768 | tf_op jit(solution)/shard_map/all_to_all | solution.py:513

commit v2 on v1

--- a/solution.py
+++ b/solution.py
@@ -141,40 +141,6 @@
         for move in range(self.moves):
             target = jnp.where(self.slot(own, move) == slot, self.dest(own, move), target)
         return target
-
-
-def leave_kernel(dims, ident_ref, table_ref, own_ref, *refs):
-    slots, share_rows, orb_count, walkers, moves, keep = dims
-    leave_refs, place_ref, wide = refs[:-2], refs[-2], refs[-1]
-    table = Moves(table_ref, moves)
-    wide[...] = own_ref[...].astype(jnp.float32)
-    own = ident_ref[0]
-    for shift in range(1, walkers):
-        target = lax.rem(own + shift, walkers)
-        chosen = jnp.int32(0)
-        for move in range(moves):
-            hit = (table.dest(own, move) == target) & (table.slot(own, move) >= 0)
-            chosen = jnp.where(hit, table.slot(own, move), chosen)
-        start = pl.multiple_of(chosen * share_rows, ROWS)
-        leave_refs[shift - 1][...] = wide[pl.ds(start, share_rows), :].astype(jnp.bfloat16)
-    rank = jnp.int32(0)
-    for slot in range(slots):
-        live = slot < table.count(own)
-        gone_to = table.goes_to(own, slot)
-        stays = live & (gone_to < 0)
-        there = jnp.maximum(gone_to, 0)
-        ahead = table.staying(there)
-        for device in range(walkers):
-            for move in range(moves):
-                hit = (
-                    (device < own)
-                    & (table.dest(device, move) == there)
-                    & (table.slot(device, move) >= 0)
-                )
-                ahead = ahead + jnp.where(hit, 1, 0)
-        place = jnp.where(stays, own * keep + rank, there * keep + ahead)
-        place_ref[slot] = jnp.where(live, place, -1)
-        rank = rank + jnp.where(stays, 1, 0)
 
 
 def assemble_kernel(dims, ident_ref, table_ref, green_ref, *refs):
@@ -226,20 +192,66 @@
             ].astype(jnp.bfloat16)
 
 
-def order_kernel(dims, ident_ref, chol_ref, own_ref, out_ref, sems):
-    del own_ref
-    group, groups, chip_rows = dims
-    chip = ident_ref[0] // 2
+def times(left, right):
+    return lax.dot_general(
+        left, right, (((1,), (1,)), ((), ())), preferred_element_type=jnp.float32
+    )
+
+
+def find_places(dims, own, table, place_ref):
+    slots, walkers, moves, keep = dims
+    rank = jnp.int32(0)
+    for slot in range(slots):
+        live = slot < table.count(own)
+        gone_to = table.goes_to(own, slot)
+        stays = live & (gone_to < 0)
+        there = jnp.maximum(gone_to, 0)
+        ahead = table.staying(there)
+        for device in range(walkers):
+            for move in range(moves):
+                hit = (
+                    (device < own)
+                    & (table.dest(device, move) == there)
+                    & (table.slot(device, move) >= 0)
+                )
+                ahead = ahead + jnp.where(hit, 1, 0)
+        place = jnp.where(stays, own * keep + rank, there * keep + ahead)
+        place_ref[slot] = jnp.where(live, place, -1)
+        rank = rank + jnp.where(stays, 1, 0)
+
+
+def leave_kernel(dims, walker_ref, table_ref, own_ref, *refs):
+    share_rows, walkers, moves = dims
+    leave_refs, wide = refs[:-1], refs[-1]
+    table = Moves(table_ref, moves)
+    own = walker_ref[0]
+    wide[...] = own_ref[...].astype(jnp.float32)
+    for shift in range(1, walkers):
+        target = lax.rem(own + shift, walkers)
+        chosen = jnp.int32(0)
+        for move in range(moves):
+            hit = (table.dest(own, move) == target) & (table.slot(own, move) >= 0)
+            chosen = jnp.where(hit, table.slot(own, move), chosen)
+        start = pl.multiple_of(chosen * share_rows, ROWS)
+        leave_refs[shift - 1][...] = wide[pl.ds(start, share_rows), :].astype(jnp.bfloat16)
+
+
+def home_kernel(dims, ident_ref, walker_ref, table_ref, chol_ref, own_ref, core_ref, *refs):
+    slots, share_rows, group, groups, chip_rows, walkers, moves, keep = dims
+    weight_ref, home_ref, place_ref = refs[:3]
+    sems = refs[3]
+    chip, core = ident_ref[0] // 2, lax.rem(ident_ref[0], 2)
     edge = LANES - 2 * chip_rows
     rest = 2 * chip_rows - edge
+    size = group * 4 * chip_rows
     copies = []
 
-    def add(vec, distance, start, size, place):
+    def add(vec, distance, start, count, place):
         row = pl.multiple_of(jnp.bitwise_xor(chip, distance) * chip_rows + start, 16)
         copies.append(
             pltpu.make_async_copy(
-                chol_ref.at[vec, pl.ds(row, size), :],
-                out_ref.at[pl.ds(place, size), :],
+                chol_ref.at[vec, pl.ds(row, count), :],
+                weight_ref.at[pl.ds(place, count), :],
                 sems.at[len(copies)],
             )
         )
@@ -247,36 +259,47 @@
     for index in range(groups):
         for item in range(group):
             vec = index * group + item
-            place = index * group * 4 * chip_rows + item * LANES
+            place = index * size + item * LANES
             add(vec, 0, 0, chip_rows, place)
             add(vec, 1, 0, chip_rows, place + chip_rows)
             add(vec, 2, 0, edge, place + 2 * chip_rows)
-            place = index * group * 4 * chip_rows + group * LANES + item * rest
+            place = index * size + group * LANES + item * rest
             add(vec, 2, edge, chip_rows - edge, place)
             add(vec, 3, 0, chip_rows, place + chip_rows - edge)
     for copy in copies:
         copy.start()
-    for copy in copies:
-        copy.wait()
-
-
-def times(left, right):
-    return lax.dot_general(
-        left, right, (((1,), (1,)), ((), ())), preferred_element_type=jnp.float32
-    )
-
-
-def near_kernel(dims, ident_ref, weight_ref, *refs):
+
+    table = Moves(table_ref, moves)
+    own = walker_ref[0]
+    find_places((slots, walkers, moves, keep), own, table, place_ref)
+
+    pad_rows = own_ref.shape[0]
+    left = jnp.concatenate([own_ref[...], core_ref[...]], axis=0)
+    per_group = len(copies) // groups
+    for index in range(groups):
+        for copy in copies[index * per_group : (index + 1) * per_group]:
+            copy.wait()
+        cols = slice(index * size, (index + 1) * size)
+        result = times(left, weight_ref[cols, :])
+        for piece in range(2):
+            source = jnp.bitwise_xor(core, piece)
+            for slot in range(slots):
+                start = piece * pad_rows + slot * share_rows
+                place = pl.multiple_of(slot * chip_rows + source * share_rows, ROWS)
+                home_ref[pl.ds(place, share_rows), cols] = result[start : start + share_rows, :]
+
+
+def near_kernel(dims, ident_ref, weight_ref, home_ref, *refs):
     slots, share_rows, group, groups, chip_rows = dims
-    piece_refs = refs[:6]
-    sum_ref, late_ref = refs[6:8]
-    trans_refs = refs[8:]
+    piece_refs = refs[:4]
+    sum_ref, late_ref = refs[4:6]
+    trans_refs = refs[6:]
     own = ident_ref[0]
     core = lax.rem(own, 2)
     pad_rows = piece_refs[0].shape[0]
-    near = 3 * chip_rows
+    away = 2 * chip_rows
     size = 4 * chip_rows * group
-    edge = near - LANES
+    edge = 3 * chip_rows - LANES
     half = LANES // 2
     left = jnp.concatenate([ref[...] for ref in piece_refs], axis=0)
     lane = lax.broadcasted_iota(jnp.int32, (1, LANES), 1)
@@ -290,29 +313,38 @@
     for index in range(groups):
         trans = trans_refs[index]
         result = times(left, weight_ref[index * size : (index + 1) * size, :])
-        for piece in range(6):
+        for piece in range(4):
             source = jnp.bitwise_xor(core, piece % 2)
             for slot in range(slots):
                 start = piece * pad_rows + slot * share_rows
-                place = slot * near + (piece // 2) * chip_rows + source * share_rows
+                place = slot * away + (piece // 2) * chip_rows + source * share_rows
                 trans[pl.ds(pl.multiple_of(place, ROWS), share_rows), :] = result[
                     start : start + share_rows, :
                 ]
         for slot in range(slots):
-            base = slot * near
             late = slice(slot * chip_rows, (slot + 1) * chip_rows)
+
+            def head(col):
+                first = home_ref[late, index * size + col : index * size + col + LANES]
+                second = trans[slot * away : slot * away + LANES - chip_rows, col : col + LANES]
+                return jnp.concatenate([first, second], axis=0)
+
+            def tail(col):
+                base = (slot + 1) * away
+                return trans[base - edge : base, col : col + LANES]
+
             acc = sums[slot]
             for pair in range(group // 2):
                 col = (group + pair) * LANES
-                top = trans[base : base + LANES, col : col + LANES].T
-                edge_rows = trans[base + LANES : base + near, col : col + LANES]
+                top = head(col).T
+                edge_rows = tail(col)
                 gap = jnp.zeros((half - edge, LANES), jnp.float32)
                 bottom = jnp.concatenate([edge_rows, gap, edge_rows, gap], axis=0).T
                 for side in range(2):
                     vec = 2 * pair + side
-                    high = trans[base : base + LANES, vec * LANES : (vec + 1) * LANES]
+                    high = head(vec * LANES)
                     acc = acc + fold(high * high.T)
-                    across = trans[base + LANES : base + near, vec * LANES : (vec + 1) * LANES]
+                    across = tail(vec * LANES)
                     acc = acc + 2.0 * fold(across * top[side * half : side * half + edge, :])
                     late_ref[
                         late, (index * (group + group // 2) + vec) * LANES : (
@@ -414,50 +446,54 @@
         compiler_params=limit,
         name="pack",
     )(green)
-    move_dims = (slots, share_rows, orb_count, walkers, moves, keep)
-    *leaving, place = pl.pallas_call(
-        functools.partial(leave_kernel, move_dims),
-        out_shape=[jax.ShapeDtypeStruct((share_rows, orb_count), jnp.bfloat16)] * (walkers - 1)
-        + [jax.ShapeDtypeStruct((slots,), jnp.int32)],
+    leaving = pl.pallas_call(
+        functools.partial(leave_kernel, (share_rows, walkers, moves)),
+        out_shape=[jax.ShapeDtypeStruct((share_rows, orb_count), jnp.bfloat16)] * (walkers - 1),
         in_specs=[smem, smem, vmem],
-        out_specs=[vmem] * (walkers - 1) + [smem],
+        out_specs=[vmem] * (walkers - 1),
         scratch_shapes=[pltpu.VMEM((pad_rows, orb_count), jnp.float32)],
         compiler_params=limit,
         name="leave",
     )(walker_index, table, own_rows)
+    core, near_x, near_y = 1, 2, 4
+    from_x = swap(own_rows, near_x, blocks)
+    from_y = swap(own_rows, near_y, blocks)
+    from_core = swap(own_rows, core, blocks)
+    group = 4
+    groups = vectors // group
+    chip_rows = 2 * share_rows
+    anywhere = pl.BlockSpec(memory_space=pl.ANY)
+    home_dims = (slots, share_rows, group, groups, chip_rows, walkers, moves, keep)
+    weights, home, place = pl.pallas_call(
+        functools.partial(home_kernel, home_dims),
+        out_shape=[
+            jax.ShapeDtypeStruct((vectors * occ_count, orb_count), jnp.bfloat16),
+            jax.ShapeDtypeStruct((slots * chip_rows, vectors * occ_count), jnp.float32),
+            jax.ShapeDtypeStruct((slots,), jnp.int32),
+        ],
+        in_specs=[smem] * 3 + [anywhere] + [vmem] * 2,
+        out_specs=[vmem] * 2 + [smem],
+        scratch_shapes=[pltpu.SemaphoreType.DMA((5 * vectors,))],
+        compiler_params=pltpu.CompilerParams(vmem_limit_bytes=46 * 1024 * 1024),
+        cost_estimate=pl.CostEstimate(
+            flops=4 * vectors * occ_count * orb_count * pad_rows,
+            bytes_accessed=4 * chol.size,
+            transcendentals=0,
+        ),
+        name="home",
+    )(block_index, walker_index, table, chol, own_rows, from_core)
     coming = [
         lax.ppermute(
             leaving[shift - 1], "walker", [(z, (z + shift) % walkers) for z in range(walkers)]
         )
         for shift in range(1, walkers)
     ]
-
-    group = 4
-    groups = vectors // group
-    chip_rows = 2 * share_rows
-    weights = pl.pallas_call(
-        functools.partial(order_kernel, (group, groups, chip_rows)),
-        out_shape=jax.ShapeDtypeStruct((vectors * occ_count, orb_count), jnp.bfloat16),
-        in_specs=[smem] + [pl.BlockSpec(memory_space=pl.ANY)] * 2,
-        out_specs=vmem,
-        scratch_shapes=[pltpu.SemaphoreType.DMA((5 * vectors,))],
-        compiler_params=pltpu.CompilerParams(vmem_limit_bytes=48 * 1024 * 1024),
-        cost_estimate=pl.CostEstimate(
-            flops=0, bytes_accessed=4 * chol.size, transcendentals=0
-        ),
-        name="order",
-    )(block_index, chol, own_rows)
-
-    core, near_x, near_y = 1, 2, 4
-    from_x = swap(own_rows, near_x, blocks)
-    from_y = swap(own_rows, near_y, blocks)
-    from_core = swap(own_rows, core, blocks)
     width = orb_count // 2
     from_x, from_y, weights, coming[:2] = lax.optimization_barrier(
         (from_x, from_y, weights, coming[:2])
     )
     far = [swap(from_y[:, :width], near_x, blocks), swap(from_x[:, width:], near_y, blocks)]
-    near_pieces = [own_rows, from_core]
+    near_pieces = []
     for piece in (from_x, from_y):
         near_pieces += [piece, swap(piece, core, blocks)]
 
@@ -469,16 +505,16 @@
             jax.ShapeDtypeStruct((slots * ROWS, LANES), jnp.float32),
             jax.ShapeDtypeStruct((slots * chip_rows, vectors * occ_count), jnp.float32),
         ],
-        in_specs=[smem] + [vmem] * 7,
+        in_specs=[smem] + [vmem] * 6,
         out_specs=[vmem] * 2,
-        scratch_shapes=[pltpu.VMEM((slots * 3 * chip_rows, group * occ_count), jnp.float32)]
+        scratch_shapes=[pltpu.VMEM((slots * 2 * chip_rows, group * occ_count), jnp.float32)]
         * groups,
         compiler_params=limit,
         cost_estimate=pl.CostEstimate(
-            flops=6 * work, bytes_accessed=2 * chol.size, transcendentals=0
+            flops=4 * work, bytes_accessed=2 * chol.size, transcendentals=0
         ),
         name="near",
-    )(block_index, weights, *near_pieces)
+    )(block_index, weights, home, *near_pieces)
     far, near_sums = lax.optimization_barrier((far, near_sums))
     far_pieces = far + [swap(piece, core, blocks) for piece in far]
     all_sums = pl.pallas_call(
@@ -496,7 +532,9 @@
 
     coming, _ = lax.optimization_barrier((coming, all_sums))
     new_green = pl.pallas_call(
-        functools.partial(assemble_kernel, move_dims),
+        functools.partial(
+            assemble_kernel, (slots, share_rows, orb_count, walkers, moves, keep)
+        ),
         out_shape=jax.ShapeDtypeStruct((keep, share_width), jnp.bfloat16),
         in_specs=[smem] * 2 + [vmem] * walkers,
         out_specs=vmem,

time: 41.9 us -> 42.5 us (1.014)
  starting transfers between devices: 16.3 us -> 17.2 us
    ppermute x3, waiting for transfers between devices: 1.53 us -> 0.18 us  [body(): lax.ppermute(leaving[shift - 1], 'walker', [(z, (z + shift) % walkers) fo...]
    pallas_call x1, Pallas kernels: 4.71 us -> 3.46 us  [body(): pl.pallas_call(functools.partial(near_kernel, dims), out_shape=[jax.Shape...]
    pallas_call x3, Pallas kernels: 6.1 us -> 7.32 us  [the longest x1 4.72 us: body(): pl.pallas_call(functools.partial(home_kernel, home_dims), out_shape=[jax....]
    ppermute x9, waiting for transfers between devices: 1.38 us -> 2.48 us  [swap(): lax.ppermute(value, 'block', [(index, index ^ mask) for index in range(bl...]
    ppermute x3, starting transfers between devices: 6.15 us -> 6.89 us  [body(): lax.ppermute(leaving[shift - 1], 'walker', [(z, (z + shift) % walkers) fo...]
  transfers between devices with their start and end apart: 13 -> 13, of which waited for: 6 -> 5; matrix products, arithmetic and copies ran while one was open for 2% -> 2% of each run, Pallas kernels for 33% -> 33%
where the time goes in v2:
time: 42.5 us; the launch traced here: 42.3 us
  starting transfers between devices  17.2 us (40%)
  Pallas kernels  14.1 us (33%)
  waiting for transfers between devices  7.88 us (19%)
  other arithmetic  1.34 us (3%)
  local copies, waits for them, and re-layouts  1.09 us (3%)
  between operations  0.73 us (2%)
    ppermute x3, starting transfers between devices, body(): lax.ppermute(leaving[shift - 1], 'walker', [(z, (z + shift) % walkers) fo...  6.89 us
    ppermute x9, starting transfers between devices, swap(): lax.ppermute(value, 'block', [(index, index ^ mask) for index in range(bl...  6.87 us
    all_to_all x1, waiting for transfers between devices, body(): lax.all_to_all(all_sums, ('block', 'walker'), split_axis=0, concat_axis=0...  5.22 us
    pallas_call x1, Pallas kernels, body(): pl.pallas_call(functools.partial(home_kernel, home_dims), out_shape=[jax....  4.72 us
    pallas_call x1, Pallas kernels, body(): pl.pallas_call(functools.partial(near_kernel, dims), out_shape=[jax.Shape...  3.46 us
    all_to_all x1, starting transfers between devices, body(): lax.all_to_all(all_sums, ('block', 'walker'), split_axis=0, concat_axis=0...  3.45 us
    pallas_call x1, Pallas kernels, body(): pl.pallas_call(functools.partial(far_kernel, dims), out_shape=jax.ShapeDt...  3.01 us
    ppermute x9, waiting for transfers between devices, swap(): lax.ppermute(value, 'block', [(index, index ^ mask) for index in range(bl...  2.48 us
  transfers between devices with their start and end apart: 13, of which 5 were waited for; matrix products, arithmetic and copies ran while one was open for 2% of the time, Pallas kernels for 33%

profile of v2, /device:TPU:0, one launch (start us, length us, event | category | flops | bytes accessed | tf_op | source)
XLA Modules:
  0.0 42.3 jit_solution(2088730092791166914)
XLA Ops:
  0.6 1.1 %copy-done = bf16[5,36864]{1,0:T(8,128)(2,1)S(1)} copy-done((bf16[5,36864]{1,0:T(8,128)(2,1)S(1)}, bf16[5,36864]{1,0:T(8,128)(2,1)}, u32[]{:S(2)}) %copy-start) | copy-done | bytes 368664
  1.7 0.3 pack.1.own_ref
  2.0 0.5 %collective-permute-start.2 = (bf16[128,1536]{1,0:T(8,128)(2,1)S(1)}, bf16[128,1536]{1,0:T(8,128)(2,1)S(1)}, u32[]{:S(2)}, u32[]{:S(2)}) collective-permute-start(bf16[128,1536]{1,0:T(8,128)(2,1)S(1)} %pack.1.own_ref), channel_id=1, source_target_pairs={{0,4},{4,0},{8,12},{12,8},{16,20},{20,16},{24,28},{28,24},{1,5},{5... | collective-permute-start | bytes 1179656 | tf_op jit(solution)/shard_map/ppermute | solution.py:420
  2.5 2.6 %collective-permute-start = (bf16[128,1536]{1,0:T(8,128)(2,1)S(1)}, bf16[128,1536]{1,0:T(8,128)(2,1)S(1)}, u32[]{:S(2)}, u32[]{:S(2)}) collective-permute-start(bf16[128,1536]{1,0:T(8,128)(2,1)S(1)} %pack.1.own_ref), channel_id=1, source_target_pairs={{0,8},{4,12},{8,0},{12,4},{16,24},{20,28},{24,16},{28,20},{1,9},{5... | collective-permute-start | bytes 1179656 | tf_op jit(solution)/shard_map/ppermute | solution.py:420
  5.1 1.5 %collective-permute-start.1 = (bf16[128,1536]{1,0:T(8,128)(2,1)S(1)}, bf16[128,1536]{1,0:T(8,128)(2,1)S(1)}, u32[]{:S(2)}, u32[]{:S(2)}) collective-permute-start(bf16[128,1536]{1,0:T(8,128)(2,1)S(1)} %pack.1.own_ref), channel_id=1, source_target_pairs={{0,16},{4,20},{8,24},{12,28},{16,0},{20,4},{24,8},{28,12},{1,17},{... | collective-permute-start | bytes 1179656 | tf_op jit(solution)/shard_map/ppermute | solution.py:420
  6.6 0.7 %pad_add_fusion.table_ref = s32[5,4]{1,0:T(8,128)S(1)} fusion(s32[2,4]{1,0:T(2,128)} %bitcast.8, s32[2,4]{1,0:T(2,128)} %bitcast.9, s32[1,4]{1,0:T(1,128)} %bitcast.10), kind=kLoop, calls=%fused_computation | loop fusion | flops 40 | bytes 160 | tf_op jit(solution)/shard_map/concatenate | solution.py:432
  7.3 0.7 %leave.1 = (bf16[24,1536]{1,0:T(8,128)(2,1)S(1)}, bf16[24,1536]{1,0:T(8,128)(2,1)S(1)}, bf16[24,1536]{1,0:T(8,128)(2,1)S(1)}) custom-call(s32[1]{0:T(128)} %bitcast.walker_ref.ident_ref, s32[5,4]{1,0:T(8,128)S(1)} %pad_add_fusion.table_ref, bf16[128,1536]{1,0:T(8,128)(2,1)S(1)} %pack.1.own_ref), custom_call_target="tpu_custom_call" | custom-call | tf_op jit(solution)/shard_map/leave/pallas_call | solution.py:449
  8.0 1.6 %collective-permute-start.3 = (bf16[24,1536]{1,0:T(8,128)(2,1)S(1)}, bf16[24,1536]{1,0:T(8,128)(2,1)S(1)}, u32[]{:S(2)}, u32[]{:S(2)}) collective-permute-start(bf16[24,1536]{1,0:T(8,128)(2,1)S(1)} %get-tuple-element.22), channel_id=1, source_target_pairs={{0,1},{1,2},{2,3},{3,0},{4,5},{5,6},{6,7},{7,4},{8,9},{9,10},{10,1... | collective-permute-start | bytes 221192 | tf_op jit(solution)/shard_map/ppermute | solution.py:486
  9.6 2.6 %collective-permute-start.4 = (bf16[24,1536]{1,0:T(8,128)(2,1)S(1)}, bf16[24,1536]{1,0:T(8,128)(2,1)S(1)}, u32[]{:S(2)}, u32[]{:S(2)}) collective-permute-start(bf16[24,1536]{1,0:T(8,128)(2,1)S(1)} %get-tuple-element.23), channel_id=1, source_target_pairs={{0,2},{1,3},{2,0},{3,1},{4,6},{5,7},{6,4},{7,5},{8,10},{9,11},{10,... | collective-permute-start | bytes 221192 | tf_op jit(solution)/shard_map/ppermute | solution.py:486
  12.2 4.7 %home.1 = (bf16[1536,1536]{1,0:T(8,128)(2,1)S(1)}, f32[240,1536]{1,0:T(8,128)S(1)}, s32[5]{0:T(128)S(1)}) custom-call(s32[1]{0:T(128)} %bitcast.4.ident_ref, s32[1]{0:T(128)} %bitcast.walker_ref.ident_ref, s32[5,4]{1,0:T(8,128)S(1)} %pad_add_fusion.table_ref, bf16[8,192,1536]{2,1,0:T(8,128)(2,1)} %chol_ref.1, bf16[128,1536]{1,0:T(8,128)(2,1)S(1)} %pack.1.own_ref, ...), custom_call_target="tpu_custom_call" | custom-call | flops 1207959552 | bytes 9437184 | tf_op jit(solution)/shard_map/home/pallas_call | solution.py:467
  17.1 0.5 %collective-permute-start.9 = (bf16[128,1536]{1,0:T(8,128)(2,1)S(1)}, bf16[128,1536]{1,0:T(8,128)(2,1)S(1)}, u32[]{:S(2)}, u32[]{:S(2)}) collective-permute-start(bf16[128,1536]{1,0:T(8,128)(2,1)S(1)} %collective-permute-done.1.refs_2_), channel_id=1, source_target_pairs={{0,4},{4,0},{8,12},{12,8},{16,20},{20,16},{24,28},{28,24},{1,5},{5... | collective-permute-start | bytes 1179656 | tf_op jit(solution)/shard_map/ppermute | solution.py:420
  17.7 0.6 %collective-permute-start.6 = (bf16[128,768]{1,0:T(8,128)(2,1)S(1)}, bf16[128,768]{1,0:T(8,128)(2,1)S(1)}, u32[]{:S(2)}, u32[]{:S(2)}) collective-permute-start(bf16[128,768]{1,0:T(8,128)(2,1)S(1)} %slice.6), channel_id=1, source_target_pairs={{0,8},{4,12},{8,0},{12,4},{16,24},{20,28},{24,16},{28,20},{1,9},{5... | collective-permute-start | bytes 589832 | tf_op jit(solution)/shard_map/ppermute | solution.py:420
  18.3 0.7 %collective-permute-start.7 = (bf16[128,768]{1,0:T(8,128)(2,1)S(1)}, bf16[128,768]{1,0:T(8,128)(2,1)S(1)}, u32[]{:S(2)}, u32[]{:S(2)}) collective-permute-start(bf16[128,768]{1,0:T(8,128)(2,1)S(1)} %slice.7), channel_id=1, source_target_pairs={{0,16},{4,20},{8,24},{12,28},{16,0},{20,4},{24,8},{28,12},{1,17},{... | collective-permute-start | bytes 589832 | tf_op jit(solution)/shard_map/ppermute | solution.py:420
  18.9 0.5 %collective-permute-done.9.refs_3_ = bf16[128,1536]{1,0:T(8,128)(2,1)S(1)} collective-permute-done((bf16[128,1536]{1,0:T(8,128)(2,1)S(1)}, bf16[128,1536]{1,0:T(8,128)(2,1)S(1)}, u32[]{:S(2)}, u32[]{:S(2)}) %collective-permute-start.9) | collective-permute-done | bytes 393248 | tf_op jit(solution)/shard_map/ppermute | solution.py:420
  19.4 3.5 %near.1 = (f32[40,128]{1,0:T(8,128)S(1)}, f32[240,1536]{1,0:T(8,128)S(1)}) custom-call(s32[1]{0:T(128)} %bitcast.4.ident_ref, bf16[1536,1536]{1,0:T(8,128)(2,1)S(1)} %get-tuple-element.28.weight_ref, f32[240,1536]{1,0:T(8,128)S(1)} %get-tuple-element.31.home_ref, bf16[128,1536]{1,0:T(8,128)(2,1)S(1)} %collective-permute-done.refs_0_, ...), custom_call_target="tpu_custom_call" | custom-call | flops 2415919104 | bytes 4718592 | tf_op jit(solution)/shard_map/near/pallas_call | solution.py:502
  22.9 1.7 %collective-permute-done.6.refs_0_ = bf16[128,768]{1,0:T(8,128)(2,1)S(1)} collective-permute-done((bf16[128,768]{1,0:T(8,128)(2,1)S(1)}, bf16[128,768]{1,0:T(8,128)(2,1)S(1)}, u32[]{:S(2)}, u32[]{:S(2)}) %collective-permute-start.6) | collective-permute-done | bytes 196640 | tf_op jit(solution)/shard_map/ppermute | solution.py:420
  24.6 0.3 collective-permute-done.7.refs_1_
  24.9 0.5 %collective-permute-start.11 = (bf16[128,768]{1,0:T(8,128)(2,1)S(1)}, bf16[128,768]{1,0:T(8,128)(2,1)S(1)}, u32[]{:S(2)}, u32[]{:S(2)}) collective-permute-start(bf16[128,768]{1,0:T(8,128)(2,1)S(1)} %collective-permute-done.7.refs_1_), channel_id=1, source_target_pairs={{0,4},{4,0},{8,12},{12,8},{16,20},{20,16},{24,28},{28,24},{1,5},{5... | collective-permute-start | bytes 589832 | tf_op jit(solution)/shard_map/ppermute | solution.py:420
  25.4 2.7 %collective-permute-start.5 = (bf16[24,1536]{1,0:T(8,128)(2,1)S(1)}, bf16[24,1536]{1,0:T(8,128)(2,1)S(1)}, u32[]{:S(2)}, u32[]{:S(2)}) collective-permute-start(bf16[24,1536]{1,0:T(8,128)(2,1)S(1)} %get-tuple-element.26), channel_id=1, source_target_pairs={{0,3},{1,0},{2,1},{3,2},{4,7},{5,4},{6,5},{7,6},{8,11},{9,8},{10,9... | collective-permute-start | bytes 221192 | tf_op jit(solution)/shard_map/ppermute | solution.py:486
  28.1 3.0 %far.1 = f32[32,128]{1,0:T(8,128)} custom-call(s32[1]{0:T(128)} %bitcast.4.ident_ref, s32[5]{0:T(128)S(1)} %get-tuple-element.27.place_ref, bf16[1536,1536]{1,0:T(8,128)(2,1)S(1)} %get-tuple-element.28.weight_ref, f32[40,128]{1,0:T(8,128)S(1)} %get-tuple-element.33.near_sum_ref, f32[240,1536]{1,0:T(8,128)S(1)} %get-tuple-element.34.late_ref, ...), custom_call_target="tpu_custom_call" | custom-call | flops 1207959552 | bytes 4718592 | tf_op jit(solution)/shard_map/far/pallas_call | solution.py:520
  31.1 3.5 %all-to-all-start = ((f32[32,1,128]{2,1,0:T(1,128)}), f32[32,1,128]{2,1,0:T(1,128)S(1)}, u32[]{:S(2)}, u32[]{:S(2)}) async-start(f32[32,1,128]{2,1,0:T(1,128)} %bitcast.6), calls=%async_computation | async-start | bytes 32768 | tf_op jit(solution)/shard_map/all_to_all | solution.py:551
  34.5 1.9 %assemble.1 = bf16[3,36864]{1,0:T(4,128)(2,1)} custom-call(s32[1]{0:T(128)} %bitcast.walker_ref.ident_ref, s32[5,4]{1,0:T(8,128)S(1)} %pad_add_fusion.table_ref, bf16[5,36864]{1,0:T(8,128)(2,1)S(1)} %copy-done.1, bf16[24,1536]{1,0:T(8,128)(2,1)S(1)} %collective-permute-done.3.refs_0_, bf16[24,1536]{1,0:T(8,128)(2,1)S(1)} %collective-permute-done.4.refs_1_, ...), custom_call_target="tpu_custom_call" | custom-call | tf_op jit(solution)/shard_map/assemble/pallas_call | solution.py:534
  36.5 5.2 %all-to-all-done = f32[32,1,128]{2,1,0:T(1,128)S(1)} async-done(((f32[32,1,128]{2,1,0:T(1,128)}), f32[32,1,128]{2,1,0:T(1,128)S(1)}, u32[]{:S(2)}, u32[]{:S(2)}) %all-to-all-start) | async-done | bytes 16416 | tf_op jit(solution)/shard_map/all_to_all | solution.py:551
  41.7 0.6 %dynamic-slice_multiply_fusion = f32[3]{0:T(128)} fusion(f32[128]{0:T(128)S(1)} %reduce_sum.9, s32[]{:T(128)S(6)} %select_n.3), kind=kLoop, calls=%fused_computation.1 | loop fusion | flops 3 | bytes 28 | tf_op jit(solution)/shard_map/mul | solution.py:556
  (17 shorter events, 0.3 us)
Async XLA Ops:
  0.6 1.1 %copy-start = (bf16[5,36864]{1,0:T(8,128)(2,1)S(1)}, bf16[5,36864]{1,0:T(8,128)(2,1)}, u32[]{:S(2)}) copy-start(bf16[5,36864]{1,0:T(8,128)(2,1)} %green_ref.3) | copy-start | bytes 1105924
  2.0 10.2 %collective-permute-start.2 = (bf16[128,1536]{1,0:T(8,128)(2,1)S(1)}, bf16[128,1536]{1,0:T(8,128)(2,1)S(1)}, u32[]{:S(2)}, u32[]{:S(2)}) collective-permute-start(bf16[128,1536]{1,0:T(8,128)(2,1)S(1)} %pack.1.own_ref), channel_id=1, source_target_pairs={{0,4},{4,0},{8,12},{12,8},{16,20},{20,16},{24,28},{28,24},{1,5},{5... | collective-permute-start | bytes 1179656 | tf_op jit(solution)/shard_map/ppermute | solution.py:420
  2.5 14.6 %collective-permute-start = (bf16[128,1536]{1,0:T(8,128)(2,1)S(1)}, bf16[128,1536]{1,0:T(8,128)(2,1)S(1)}, u32[]{:S(2)}, u32[]{:S(2)}) collective-permute-start(bf16[128,1536]{1,0:T(8,128)(2,1)S(1)} %pack.1.own_ref), channel_id=1, source_target_pairs={{0,8},{4,12},{8,0},{12,4},{16,24},{20,28},{24,16},{28,20},{1,9},{5... | collective-permute-start | bytes 1179656 | tf_op jit(solution)/shard_map/ppermute | solution.py:420
  5.1 12.0 %collective-permute-start.1 = (bf16[128,1536]{1,0:T(8,128)(2,1)S(1)}, bf16[128,1536]{1,0:T(8,128)(2,1)S(1)}, u32[]{:S(2)}, u32[]{:S(2)}) collective-permute-start(bf16[128,1536]{1,0:T(8,128)(2,1)S(1)} %pack.1.own_ref), channel_id=1, source_target_pairs={{0,16},{4,20},{8,24},{12,28},{16,0},{20,4},{24,8},{28,12},{1,17},{... | collective-permute-start | bytes 1179656 | tf_op jit(solution)/shard_map/ppermute | solution.py:420
  8.0 9.0 %collective-permute-start.3 = (bf16[24,1536]{1,0:T(8,128)(2,1)S(1)}, bf16[24,1536]{1,0:T(8,128)(2,1)S(1)}, u32[]{:S(2)}, u32[]{:S(2)}) collective-permute-start(bf16[24,1536]{1,0:T(8,128)(2,1)S(1)} %get-tuple-element.22), channel_id=1, source_target_pairs={{0,1},{1,2},{2,3},{3,0},{4,5},{5,6},{6,7},{7,4},{8,9},{9,10},{10,1... | collective-permute-start | bytes 221192 | tf_op jit(solution)/shard_map/ppermute | solution.py:486
  9.6 7.5 %collective-permute-start.4 = (bf16[24,1536]{1,0:T(8,128)(2,1)S(1)}, bf16[24,1536]{1,0:T(8,128)(2,1)S(1)}, u32[]{:S(2)}, u32[]{:S(2)}) collective-permute-start(bf16[24,1536]{1,0:T(8,128)(2,1)S(1)} %get-tuple-element.23), channel_id=1, source_target_pairs={{0,2},{1,3},{2,0},{3,1},{4,6},{5,7},{6,4},{7,5},{8,10},{9,11},{10,... | collective-permute-start | bytes 221192 | tf_op jit(solution)/shard_map/ppermute | solution.py:486
  17.1 1.8 %collective-permute-start.8 = (bf16[128,1536]{1,0:T(8,128)(2,1)S(1)}, bf16[128,1536]{1,0:T(8,128)(2,1)S(1)}, u32[]{:S(2)}, u32[]{:S(2)}) collective-permute-start(bf16[128,1536]{1,0:T(8,128)(2,1)S(1)} %collective-permute-done.refs_0_), channel_id=1, source_target_pairs={{0,4},{4,0},{8,12},{12,8},{16,20},{20,16},{24,28},{28,24},{1,5},{5... | collective-permute-start | bytes 1179656 | tf_op jit(solution)/shard_map/ppermute | solution.py:420
  17.1 2.3 %collective-permute-start.9 = (bf16[128,1536]{1,0:T(8,128)(2,1)S(1)}, bf16[128,1536]{1,0:T(8,128)(2,1)S(1)}, u32[]{:S(2)}, u32[]{:S(2)}) collective-permute-start(bf16[128,1536]{1,0:T(8,128)(2,1)S(1)} %collective-permute-done.1.refs_2_), channel_id=1, source_target_pairs={{0,4},{4,0},{8,12},{12,8},{16,20},{20,16},{24,28},{28,24},{1,5},{5... | collective-permute-start | bytes 1179656 | tf_op jit(solution)/shard_map/ppermute | solution.py:420
  17.7 6.9 %collective-permute-start.6 = (bf16[128,768]{1,0:T(8,128)(2,1)S(1)}, bf16[128,768]{1,0:T(8,128)(2,1)S(1)}, u32[]{:S(2)}, u32[]{:S(2)}) collective-permute-start(bf16[128,768]{1,0:T(8,128)(2,1)S(1)} %slice.6), channel_id=1, source_target_pairs={{0,8},{4,12},{8,0},{12,4},{16,24},{20,28},{24,16},{28,20},{1,9},{5... | collective-permute-start | bytes 589832 | tf_op jit(solution)/shard_map/ppermute | solution.py:420
  18.3 6.6 %collective-permute-start.7 = (bf16[128,768]{1,0:T(8,128)(2,1)S(1)}, bf16[128,768]{1,0:T(8,128)(2,1)S(1)}, u32[]{:S(2)}, u32[]{:S(2)}) collective-permute-start(bf16[128,768]{1,0:T(8,128)(2,1)S(1)} %slice.7), channel_id=1, source_target_pairs={{0,16},{4,20},{8,24},{12,28},{16,0},{20,4},{24,8},{28,12},{1,17},{... | collective-permute-start | bytes 589832 | tf_op jit(solution)/shard_map/ppermute | solution.py:420
  22.9 11.7 %copy-start.1 = (bf16[5,36864]{1,0:T(8,128)(2,1)S(1)}, bf16[5,36864]{1,0:T(8,128)(2,1)}, u32[]{:S(2)}) copy-start(bf16[5,36864]{1,0:T(8,128)(2,1)} %green_ref.3) | copy-start | bytes 1105924
  24.9 3.2 %collective-permute-start.10 = (bf16[128,768]{1,0:T(8,128)(2,1)S(1)}, bf16[128,768]{1,0:T(8,128)(2,1)S(1)}, u32[]{:S(2)}, u32[]{:S(2)}) collective-permute-start(bf16[128,768]{1,0:T(8,128)(2,1)S(1)} %collective-permute-done.6.refs_0_), channel_id=1, source_target_pairs={{0,4},{4,0},{8,12},{12,8},{16,20},{20,16},{24,28},{28,24},{1,5},{5... | collective-permute-start | bytes 589832 | tf_op jit(solution)/shard_map/ppermute | solution.py:420
  24.9 3.2 %collective-permute-start.11 = (bf16[128,768]{1,0:T(8,128)(2,1)S(1)}, bf16[128,768]{1,0:T(8,128)(2,1)S(1)}, u32[]{:S(2)}, u32[]{:S(2)}) collective-permute-start(bf16[128,768]{1,0:T(8,128)(2,1)S(1)} %collective-permute-done.7.refs_1_), channel_id=1, source_target_pairs={{0,4},{4,0},{8,12},{12,8},{16,20},{20,16},{24,28},{28,24},{1,5},{5... | collective-permute-start | bytes 589832 | tf_op jit(solution)/shard_map/ppermute | solution.py:420
  25.4 9.1 %collective-permute-start.5 = (bf16[24,1536]{1,0:T(8,128)(2,1)S(1)}, bf16[24,1536]{1,0:T(8,128)(2,1)S(1)}, u32[]{:S(2)}, u32[]{:S(2)}) collective-permute-start(bf16[24,1536]{1,0:T(8,128)(2,1)S(1)} %get-tuple-element.26), channel_id=1, source_target_pairs={{0,3},{1,0},{2,1},{3,2},{4,7},{5,4},{6,5},{7,6},{8,11},{9,8},{10,9... | collective-permute-start | bytes 221192 | tf_op jit(solution)/shard_map/ppermute | solution.py:486
  31.1 10.6 %all-to-all-start = ((f32[32,1,128]{2,1,0:T(1,128)}), f32[32,1,128]{2,1,0:T(1,128)S(1)}, u32[]{:S(2)}, u32[]{:S(2)}) async-start(f32[32,1,128]{2,1,0:T(1,128)} %bitcast.6), calls=%async_computation | async-start | bytes 32768 | tf_op jit(solution)/shard_map/all_to_all | solution.py:551

commit v3 on v1

--- a/solution.py
+++ b/solution.py
@@ -483,7 +483,7 @@
     far_pieces = far + [swap(piece, core, blocks) for piece in far]
     all_sums = pl.pallas_call(
         functools.partial(far_kernel, dims),
-        out_shape=jax.ShapeDtypeStruct((blocks * walkers, LANES), jnp.float32),
+        out_shape=jax.ShapeDtypeStruct((blocks * walkers // 2, LANES), jnp.float32),
         in_specs=[smem] * 2 + [vmem] * 7,
         out_specs=vmem,
         scratch_shapes=[pltpu.VMEM((slots * chip_rows, group * occ_count), jnp.float32)] * groups,
@@ -494,6 +494,7 @@
         name="far",
     )(block_index, place, weights, near_sums, late, *far_pieces)
 
+    all_sums = all_sums + swap(all_sums, core, blocks)
     coming, _ = lax.optimization_barrier((coming, all_sums))
     new_green = pl.pallas_call(
         functools.partial(assemble_kernel, move_dims),
@@ -510,8 +511,17 @@
     )(walker_index, table, green, *coming)
 
     energy_scale = 0.5 / (occ_count * math.sqrt(vectors * blocks))
+    peers = [
+        [block * walkers + walker for block in range(side, blocks, 2) for walker in range(walkers)]
+        for side in range(2)
+    ]
     got = lax.all_to_all(
-        all_sums, ("block", "walker"), split_axis=0, concat_axis=0, tiled=True
+        all_sums,
+        ("block", "walker"),
+        split_axis=0,
+        concat_axis=0,
+        axis_index_groups=peers,
+        tiled=True,
     )
     got_sums = jnp.sum(got, axis=0)
     own_sums = lax.dynamic_slice(got_sums, (walker_index[0] * keep,), (keep,))

time: 41.9 us -> 44.2 us (1.055)
  waiting for transfers between devices: 8.12 us -> 9.38 us
  starting transfers between devices: 16.3 us -> 17.3 us
  Pallas kernels: 14.1 us -> 13.5 us
  other arithmetic: 1.34 us -> 1.93 us
    ppermute x9 -> x10, waiting for transfers between devices: 1.38 us -> 2.54 us  [swap(): lax.ppermute(value, 'block', [(index, index ^ mask) for index in range(bl...]
    all_to_all x1, starting transfers between devices: 3.45 us -> 4.47 us  [body(): lax.all_to_all(all_sums, ('block', 'walker'), split_axis=0, concat_axis=0...]
    pallas_call x1, Pallas kernels: 3.01 us -> 2.41 us  [body(): pl.pallas_call(functools.partial(far_kernel, dims), out_shape=jax.ShapeDt...]
    add x0 -> x1, other arithmetic: none -> 0.6 us  [body(): all_sums = all_sums + swap(all_sums, core, blocks)]
    ppermute x9 -> x10, starting transfers between devices: 6.65 us -> 6.72 us  [swap(): lax.ppermute(value, 'block', [(index, index ^ mask) for index in range(bl...]
  transfers between devices with their start and end apart: 13 -> 14, of which waited for: 6 -> 7; matrix products, arithmetic and copies ran while one was open for 2% -> 3% of each run, Pallas kernels for 33% -> 30%
where the time goes in v3:
time: 44.2 us; the launch traced here: 44 us
  starting transfers between devices  17.3 us (39%)
  Pallas kernels  13.5 us (31%)
  waiting for transfers between devices  9.38 us (21%)
  other arithmetic  1.93 us (4%)
  local copies, waits for them, and re-layouts  1.09 us (2%)
  between operations  0.75 us (2%)
    ppermute x10, starting transfers between devices, swap(): lax.ppermute(value, 'block', [(index, index ^ mask) for index in range(bl...  6.72 us
    ppermute x3, starting transfers between devices, body(): lax.ppermute(leaving[shift - 1], 'walker', [(z, (z + shift) % walkers) fo...  6.15 us
    all_to_all x1, waiting for transfers between devices, body(): lax.all_to_all(all_sums, ('block', 'walker'), split_axis=0, concat_axis=0...  5.31 us
    pallas_call x1, Pallas kernels, body(): pl.pallas_call(functools.partial(near_kernel, dims), out_shape=[jax.Shape...  4.71 us
    all_to_all x1, starting transfers between devices, body(): lax.all_to_all(all_sums, ('block', 'walker'), split_axis=0, concat_axis=0...  4.47 us
    pallas_call x1, Pallas kernels, body(): pl.pallas_call(functools.partial(order_kernel, (group, groups, chip_rows)...  2.76 us
    ppermute x10, waiting for transfers between devices, swap(): lax.ppermute(value, 'block', [(index, index ^ mask) for index in range(bl...  2.54 us
    pallas_call x1, Pallas kernels, body(): pl.pallas_call(functools.partial(far_kernel, dims), out_shape=jax.ShapeDt...  2.41 us
  transfers between devices with their start and end apart: 14, of which 7 were waited for; matrix products, arithmetic and copies ran while one was open for 3% of the time, Pallas kernels for 30%

profile of v3, /device:TPU:0, one launch (start us, length us, event | category | flops | bytes accessed | tf_op | source)
XLA Modules:
  0.0 44.0 jit_solution(7592128249326686979)
XLA Ops:
  0.6 1.1 %copy-done = bf16[5,36864]{1,0:T(8,128)(2,1)S(1)} copy-done((bf16[5,36864]{1,0:T(8,128)(2,1)S(1)}, bf16[5,36864]{1,0:T(8,128)(2,1)}, u32[]{:S(2)}) %copy-start) | copy-done | bytes 368664
  2.0 3.0 %collective-permute-start = (bf16[128,1536]{1,0:T(8,128)(2,1)S(1)}, bf16[128,1536]{1,0:T(8,128)(2,1)S(1)}, u32[]{:S(2)}, u32[]{:S(2)}) collective-permute-start(bf16[128,1536]{1,0:T(8,128)(2,1)S(1)} %pack.1.own_ref.refs_0_), channel_id=1, source_target_pairs={{0,8},{4,12},{8,0},{12,4},{16,24},{20,28},{24,16},{28,20},{1,9},{5... | collective-permute-start | bytes 1179656 | tf_op jit(solution)/shard_map/ppermute | solution.py:388
  5.0 1.5 %collective-permute-start.1 = (bf16[128,1536]{1,0:T(8,128)(2,1)S(1)}, bf16[128,1536]{1,0:T(8,128)(2,1)S(1)}, u32[]{:S(2)}, u32[]{:S(2)}) collective-permute-start(bf16[128,1536]{1,0:T(8,128)(2,1)S(1)} %pack.1.own_ref.refs_0_), channel_id=1, source_target_pairs={{0,16},{4,20},{8,24},{12,28},{16,0},{20,4},{24,8},{28,12},{1,17},{... | collective-permute-start | bytes 1179656 | tf_op jit(solution)/shard_map/ppermute | solution.py:388
  6.5 0.7 %pad_add_fusion.table_ref = s32[5,4]{1,0:T(8,128)S(1)} fusion(s32[2,4]{1,0:T(2,128)} %bitcast.8, s32[2,4]{1,0:T(2,128)} %bitcast.9, s32[1,4]{1,0:T(1,128)} %bitcast.10), kind=kLoop, calls=%fused_computation | loop fusion | flops 40 | bytes 160 | tf_op jit(solution)/shard_map/concatenate | solution.py:400
  7.2 1.4 %leave.1 = (bf16[24,1536]{1,0:T(8,128)(2,1)S(1)}, bf16[24,1536]{1,0:T(8,128)(2,1)S(1)}, bf16[24,1536]{1,0:T(8,128)(2,1)S(1)}, s32[5]{0:T(128)S(1)}) custom-call(s32[1]{0:T(128)} %bitcast.ident_ref, s32[5,4]{1,0:T(8,128)S(1)} %pad_add_fusion.table_ref, bf16[128,1536]{1,0:T(8,128)(2,1)S(1)} %pack.1.own_ref.refs_0_), custom_call_target="tpu_custom_call" | custom-call | tf_op jit(solution)/shard_map/leave/pallas_call | solution.py:418
  8.6 1.6 %collective-permute-start.2 = (bf16[24,1536]{1,0:T(8,128)(2,1)S(1)}, bf16[24,1536]{1,0:T(8,128)(2,1)S(1)}, u32[]{:S(2)}, u32[]{:S(2)}) collective-permute-start(bf16[24,1536]{1,0:T(8,128)(2,1)S(1)} %get-tuple-element.19), channel_id=1, source_target_pairs={{0,1},{1,2},{2,3},{3,0},{4,5},{5,6},{6,7},{7,4},{8,9},{9,10},{10,1... | collective-permute-start | bytes 221192 | tf_op jit(solution)/shard_map/ppermute | solution.py:429
  10.3 2.6 %collective-permute-start.3 = (bf16[24,1536]{1,0:T(8,128)(2,1)S(1)}, bf16[24,1536]{1,0:T(8,128)(2,1)S(1)}, u32[]{:S(2)}, u32[]{:S(2)}) collective-permute-start(bf16[24,1536]{1,0:T(8,128)(2,1)S(1)} %get-tuple-element.20), channel_id=1, source_target_pairs={{0,2},{1,3},{2,0},{3,1},{4,6},{5,7},{6,4},{7,5},{8,10},{9,11},{10,... | collective-permute-start | bytes 221192 | tf_op jit(solution)/shard_map/ppermute | solution.py:429
  12.9 2.8 %order.1.weight_ref = bf16[1536,1536]{1,0:T(8,128)(2,1)S(1)} custom-call(s32[1]{0:T(128)} %bitcast.4.ident_ref, bf16[8,192,1536]{2,1,0:T(8,128)(2,1)} %chol_ref.1, bf16[128,1536]{1,0:T(8,128)(2,1)S(1)} %pack.1.own_ref.refs_0_), custom_call_target="tpu_custom_call" | custom-call | bytes 9437184 | tf_op jit(solution)/shard_map/order/pallas_call | solution.py:438
  15.6 1.5 %collective-permute-done.3.refs_1_ = bf16[24,1536]{1,0:T(8,128)(2,1)S(1)} collective-permute-done((bf16[24,1536]{1,0:T(8,128)(2,1)S(1)}, bf16[24,1536]{1,0:T(8,128)(2,1)S(1)}, u32[]{:S(2)}, u32[]{:S(2)}) %collective-permute-start.3) | collective-permute-done | bytes 73760 | tf_op jit(solution)/shard_map/ppermute | solution.py:429
  17.2 0.5 %collective-permute-start.9 = (bf16[128,1536]{1,0:T(8,128)(2,1)S(1)}, bf16[128,1536]{1,0:T(8,128)(2,1)S(1)}, u32[]{:S(2)}, u32[]{:S(2)}) collective-permute-start(bf16[128,1536]{1,0:T(8,128)(2,1)S(1)} %collective-permute-done.1.refs_4_), channel_id=1, source_target_pairs={{0,4},{4,0},{8,12},{12,8},{16,20},{20,16},{24,28},{28,24},{1,5},{5... | collective-permute-start | bytes 1179656 | tf_op jit(solution)/shard_map/ppermute | solution.py:388
  17.7 0.6 %collective-permute-start.5 = (bf16[128,768]{1,0:T(8,128)(2,1)S(1)}, bf16[128,768]{1,0:T(8,128)(2,1)S(1)}, u32[]{:S(2)}, u32[]{:S(2)}) collective-permute-start(bf16[128,768]{1,0:T(8,128)(2,1)S(1)} %slice.6), channel_id=1, source_target_pairs={{0,8},{4,12},{8,0},{12,4},{16,24},{20,28},{24,16},{28,20},{1,9},{5... | collective-permute-start | bytes 589832 | tf_op jit(solution)/shard_map/ppermute | solution.py:388
  18.3 0.5 %collective-permute-start.6 = (bf16[128,768]{1,0:T(8,128)(2,1)S(1)}, bf16[128,768]{1,0:T(8,128)(2,1)S(1)}, u32[]{:S(2)}, u32[]{:S(2)}) collective-permute-start(bf16[128,768]{1,0:T(8,128)(2,1)S(1)} %slice.7), channel_id=1, source_target_pairs={{0,16},{4,20},{8,24},{12,28},{16,0},{20,4},{24,8},{28,12},{1,17},{... | collective-permute-start | bytes 589832 | tf_op jit(solution)/shard_map/ppermute | solution.py:388
  18.9 0.6 %collective-permute-done.9.refs_5_ = bf16[128,1536]{1,0:T(8,128)(2,1)S(1)} collective-permute-done((bf16[128,1536]{1,0:T(8,128)(2,1)S(1)}, bf16[128,1536]{1,0:T(8,128)(2,1)S(1)}, u32[]{:S(2)}, u32[]{:S(2)}) %collective-permute-start.9) | collective-permute-done | bytes 393248 | tf_op jit(solution)/shard_map/ppermute | solution.py:388
  19.4 4.7 %near.1 = (f32[40,128]{1,0:T(8,128)S(1)}, f32[240,1536]{1,0:T(8,128)S(1)}) custom-call(s32[1]{0:T(128)} %bitcast.4.ident_ref, bf16[1536,1536]{1,0:T(8,128)(2,1)S(1)} %order.1.weight_ref, bf16[128,1536]{1,0:T(8,128)(2,1)S(1)} %pack.1.own_ref.refs_0_, bf16[128,1536]{1,0:T(8,128)(2,1)S(1)} %collective-permute-done.7.refs_1_, ...), custom_call_target="tpu_custom_call" | custom-call | flops 3623878656 | bytes 4718592 | tf_op jit(solution)/shard_map/near/pallas_call | solution.py:466
  24.2 0.5 %collective-permute-done.5.refs_0_ = bf16[128,768]{1,0:T(8,128)(2,1)S(1)} collective-permute-done((bf16[128,768]{1,0:T(8,128)(2,1)S(1)}, bf16[128,768]{1,0:T(8,128)(2,1)S(1)}, u32[]{:S(2)}, u32[]{:S(2)}) %collective-permute-start.5) | collective-permute-done | bytes 196640 | tf_op jit(solution)/shard_map/ppermute | solution.py:388
  24.9 0.5 %collective-permute-start.11 = (bf16[128,768]{1,0:T(8,128)(2,1)S(1)}, bf16[128,768]{1,0:T(8,128)(2,1)S(1)}, u32[]{:S(2)}, u32[]{:S(2)}) collective-permute-start(bf16[128,768]{1,0:T(8,128)(2,1)S(1)} %collective-permute-done.6.refs_1_), channel_id=1, source_target_pairs={{0,4},{4,0},{8,12},{12,8},{16,20},{20,16},{24,28},{28,24},{1,5},{5... | collective-permute-start | bytes 589832 | tf_op jit(solution)/shard_map/ppermute | solution.py:388
  25.4 1.9 %collective-permute-start.4 = (bf16[24,1536]{1,0:T(8,128)(2,1)S(1)}, bf16[24,1536]{1,0:T(8,128)(2,1)S(1)}, u32[]{:S(2)}, u32[]{:S(2)}) collective-permute-start(bf16[24,1536]{1,0:T(8,128)(2,1)S(1)} %get-tuple-element.23), channel_id=1, source_target_pairs={{0,3},{1,0},{2,1},{3,2},{4,7},{5,4},{6,5},{7,6},{8,11},{9,8},{10,9... | collective-permute-start | bytes 221192 | tf_op jit(solution)/shard_map/ppermute | solution.py:429
  27.4 2.4 %far.1 = f32[16,128]{1,0:T(8,128)S(1)} custom-call(s32[1]{0:T(128)} %bitcast.4.ident_ref, s32[5]{0:T(128)S(1)} %get-tuple-element.24.place_ref, bf16[1536,1536]{1,0:T(8,128)(2,1)S(1)} %order.1.weight_ref, f32[40,128]{1,0:T(8,128)S(1)} %get-tuple-element.29.near_sum_ref, f32[240,1536]{1,0:T(8,128)S(1)} %get-tuple-element.30.late_ref, ...), custom_call_target="tpu_custom_call" | custom-call | flops 1207959552 | bytes 4718592 | tf_op jit(solution)/shard_map/far/pallas_call | solution.py:484
  29.9 1.2 %collective-permute-done.12 = f32[16,128]{1,0:T(8,128)S(1)} collective-permute-done((f32[16,128]{1,0:T(8,128)S(1)}, f32[16,128]{1,0:T(8,128)S(1)}, u32[]{:S(2)}, u32[]{:S(2)}) %collective-permute-start.12) | collective-permute-done | bytes 8224 | tf_op jit(solution)/shard_map/ppermute | solution.py:388
  31.0 0.6 %add.6 = f32[16,128]{1,0:T(8,128)} add(f32[16,128]{1,0:T(8,128)S(1)} %far.1, f32[16,128]{1,0:T(8,128)S(1)} %collective-permute-done.12) | non-fusion elementwise | flops 2048 | bytes 24576 | tf_op jit(solution)/shard_map/add | solution.py:497
  31.6 4.5 %all-to-all-start = ((f32[16,1,128]{2,1,0:T(1,128)}), f32[16,1,128]{2,1,0:T(1,128)S(1)}, u32[]{:S(2)}, u32[]{:S(2)}) async-start(f32[16,1,128]{2,1,0:T(1,128)} %bitcast.6), calls=%async_computation | async-start | bytes 16384 | tf_op jit(solution)/shard_map/all_to_all | solution.py:518
  36.1 1.9 %assemble.1 = bf16[3,36864]{1,0:T(4,128)(2,1)} custom-call(s32[1]{0:T(128)} %bitcast.ident_ref, s32[5,4]{1,0:T(8,128)S(1)} %pad_add_fusion.table_ref, bf16[5,36864]{1,0:T(8,128)(2,1)S(1)} %copy-done.1, bf16[24,1536]{1,0:T(8,128)(2,1)S(1)} %collective-permute-done.2.refs_0_, bf16[24,1536]{1,0:T(8,128)(2,1)S(1)} %collective-permute-done.3.refs_1_, ...), custom_call_target="tpu_custom_call" | custom-call | tf_op jit(solution)/shard_map/assemble/pallas_call | solution.py:499
  38.0 5.3 %all-to-all-done = f32[16,1,128]{2,1,0:T(1,128)S(1)} async-done(((f32[16,1,128]{2,1,0:T(1,128)}), f32[16,1,128]{2,1,0:T(1,128)S(1)}, u32[]{:S(2)}, u32[]{:S(2)}) %all-to-all-start) | async-done | bytes 8224 | tf_op jit(solution)/shard_map/all_to_all | solution.py:518
  43.4 0.6 %dynamic-slice_multiply_fusion = f32[3]{0:T(128)} fusion(f32[128]{0:T(128)S(1)} %reduce_sum.9, s32[]{:T(128)S(6)} %select_n.3), kind=kLoop, calls=%fused_computation.1 | loop fusion | flops 3 | bytes 28 | tf_op jit(solution)/shard_map/mul | solution.py:528
  (20 shorter events, 0.8 us)
Async XLA Ops:
  0.6 1.1 %copy-start = (bf16[5,36864]{1,0:T(8,128)(2,1)S(1)}, bf16[5,36864]{1,0:T(8,128)(2,1)}, u32[]{:S(2)}) copy-start(bf16[5,36864]{1,0:T(8,128)(2,1)} %green_ref.3) | copy-start | bytes 1105924
  2.0 15.2 %collective-permute-start = (bf16[128,1536]{1,0:T(8,128)(2,1)S(1)}, bf16[128,1536]{1,0:T(8,128)(2,1)S(1)}, u32[]{:S(2)}, u32[]{:S(2)}) collective-permute-start(bf16[128,1536]{1,0:T(8,128)(2,1)S(1)} %pack.1.own_ref.refs_0_), channel_id=1, source_target_pairs={{0,8},{4,12},{8,0},{12,4},{16,24},{20,28},{24,16},{28,20},{1,9},{5... | collective-permute-start | bytes 1179656 | tf_op jit(solution)/shard_map/ppermute | solution.py:388
  5.0 12.2 %collective-permute-start.1 = (bf16[128,1536]{1,0:T(8,128)(2,1)S(1)}, bf16[128,1536]{1,0:T(8,128)(2,1)S(1)}, u32[]{:S(2)}, u32[]{:S(2)}) collective-permute-start(bf16[128,1536]{1,0:T(8,128)(2,1)S(1)} %pack.1.own_ref.refs_0_), channel_id=1, source_target_pairs={{0,16},{4,20},{8,24},{12,28},{16,0},{20,4},{24,8},{28,12},{1,17},{... | collective-permute-start | bytes 1179656 | tf_op jit(solution)/shard_map/ppermute | solution.py:388
  8.6 7.0 %collective-permute-start.2 = (bf16[24,1536]{1,0:T(8,128)(2,1)S(1)}, bf16[24,1536]{1,0:T(8,128)(2,1)S(1)}, u32[]{:S(2)}, u32[]{:S(2)}) collective-permute-start(bf16[24,1536]{1,0:T(8,128)(2,1)S(1)} %get-tuple-element.19), channel_id=1, source_target_pairs={{0,1},{1,2},{2,3},{3,0},{4,5},{5,6},{6,7},{7,4},{8,9},{9,10},{10,1... | collective-permute-start | bytes 221192 | tf_op jit(solution)/shard_map/ppermute | solution.py:429
  10.3 6.9 %collective-permute-start.3 = (bf16[24,1536]{1,0:T(8,128)(2,1)S(1)}, bf16[24,1536]{1,0:T(8,128)(2,1)S(1)}, u32[]{:S(2)}, u32[]{:S(2)}) collective-permute-start(bf16[24,1536]{1,0:T(8,128)(2,1)S(1)} %get-tuple-element.20), channel_id=1, source_target_pairs={{0,2},{1,3},{2,0},{3,1},{4,6},{5,7},{6,4},{7,5},{8,10},{9,11},{10,... | collective-permute-start | bytes 221192 | tf_op jit(solution)/shard_map/ppermute | solution.py:429
  12.8 6.0 %collective-permute-start.7 = (bf16[128,1536]{1,0:T(8,128)(2,1)S(1)}, bf16[128,1536]{1,0:T(8,128)(2,1)S(1)}, u32[]{:S(2)}, u32[]{:S(2)}) collective-permute-start(bf16[128,1536]{1,0:T(8,128)(2,1)S(1)} %pack.1.own_ref.refs_0_), channel_id=1, source_target_pairs={{0,4},{4,0},{8,12},{12,8},{16,20},{20,16},{24,28},{28,24},{1,5},{5... | collective-permute-start | bytes 1179656 | tf_op jit(solution)/shard_map/ppermute | solution.py:388
  17.2 1.7 %collective-permute-start.8 = (bf16[128,1536]{1,0:T(8,128)(2,1)S(1)}, bf16[128,1536]{1,0:T(8,128)(2,1)S(1)}, u32[]{:S(2)}, u32[]{:S(2)}) collective-permute-start(bf16[128,1536]{1,0:T(8,128)(2,1)S(1)} %collective-permute-done.refs_2_), channel_id=1, source_target_pairs={{0,4},{4,0},{8,12},{12,8},{16,20},{20,16},{24,28},{28,24},{1,5},{5... | collective-permute-start | bytes 1179656 | tf_op jit(solution)/shard_map/ppermute | solution.py:388
  17.2 2.3 %collective-permute-start.9 = (bf16[128,1536]{1,0:T(8,128)(2,1)S(1)}, bf16[128,1536]{1,0:T(8,128)(2,1)S(1)}, u32[]{:S(2)}, u32[]{:S(2)}) collective-permute-start(bf16[128,1536]{1,0:T(8,128)(2,1)S(1)} %collective-permute-done.1.refs_4_), channel_id=1, source_target_pairs={{0,4},{4,0},{8,12},{12,8},{16,20},{20,16},{24,28},{28,24},{1,5},{5... | collective-permute-start | bytes 1179656 | tf_op jit(solution)/shard_map/ppermute | solution.py:388
  17.7 6.9 %collective-permute-start.5 = (bf16[128,768]{1,0:T(8,128)(2,1)S(1)}, bf16[128,768]{1,0:T(8,128)(2,1)S(1)}, u32[]{:S(2)}, u32[]{:S(2)}) collective-permute-start(bf16[128,768]{1,0:T(8,128)(2,1)S(1)} %slice.6), channel_id=1, source_target_pairs={{0,8},{4,12},{8,0},{12,4},{16,24},{20,28},{24,16},{28,20},{1,9},{5... | collective-permute-start | bytes 589832 | tf_op jit(solution)/shard_map/ppermute | solution.py:388
  18.3 6.6 %collective-permute-start.6 = (bf16[128,768]{1,0:T(8,128)(2,1)S(1)}, bf16[128,768]{1,0:T(8,128)(2,1)S(1)}, u32[]{:S(2)}, u32[]{:S(2)}) collective-permute-start(bf16[128,768]{1,0:T(8,128)(2,1)S(1)} %slice.7), channel_id=1, source_target_pairs={{0,16},{4,20},{8,24},{12,28},{16,0},{20,4},{24,8},{28,12},{1,17},{... | collective-permute-start | bytes 589832 | tf_op jit(solution)/shard_map/ppermute | solution.py:388
  24.2 12.0 %copy-start.1 = (bf16[5,36864]{1,0:T(8,128)(2,1)S(1)}, bf16[5,36864]{1,0:T(8,128)(2,1)}, u32[]{:S(2)}) copy-start(bf16[5,36864]{1,0:T(8,128)(2,1)} %green_ref.3) | copy-start | bytes 1105924
  24.9 2.5 %collective-permute-start.10 = (bf16[128,768]{1,0:T(8,128)(2,1)S(1)}, bf16[128,768]{1,0:T(8,128)(2,1)S(1)}, u32[]{:S(2)}, u32[]{:S(2)}) collective-permute-start(bf16[128,768]{1,0:T(8,128)(2,1)S(1)} %collective-permute-done.5.refs_0_), channel_id=1, source_target_pairs={{0,4},{4,0},{8,12},{12,8},{16,20},{20,16},{24,28},{28,24},{1,5},{5... | collective-permute-start | bytes 589832 | tf_op jit(solution)/shard_map/ppermute | solution.py:388
  24.9 2.5 %collective-permute-start.11 = (bf16[128,768]{1,0:T(8,128)(2,1)S(1)}, bf16[128,768]{1,0:T(8,128)(2,1)S(1)}, u32[]{:S(2)}, u32[]{:S(2)}) collective-permute-start(bf16[128,768]{1,0:T(8,128)(2,1)S(1)} %collective-permute-done.6.refs_1_), channel_id=1, source_target_pairs={{0,4},{4,0},{8,12},{12,8},{16,20},{20,16},{24,28},{28,24},{1,5},{5... | collective-permute-start | bytes 589832 | tf_op jit(solution)/shard_map/ppermute | solution.py:388
  25.4 10.7 %collective-permute-start.4 = (bf16[24,1536]{1,0:T(8,128)(2,1)S(1)}, bf16[24,1536]{1,0:T(8,128)(2,1)S(1)}, u32[]{:S(2)}, u32[]{:S(2)}) collective-permute-start(bf16[24,1536]{1,0:T(8,128)(2,1)S(1)} %get-tuple-element.23), channel_id=1, source_target_pairs={{0,3},{1,0},{2,1},{3,2},{4,7},{5,4},{6,5},{7,6},{8,11},{9,8},{10,9... | collective-permute-start | bytes 221192 | tf_op jit(solution)/shard_map/ppermute | solution.py:429
  29.8 1.2 %collective-permute-start.12 = (f32[16,128]{1,0:T(8,128)S(1)}, f32[16,128]{1,0:T(8,128)S(1)}, u32[]{:S(2)}, u32[]{:S(2)}) collective-permute-start(f32[16,128]{1,0:T(8,128)S(1)} %far.1), channel_id=1, source_target_pairs={{0,4},{4,0},{8,12},{12,8},{16,20},{20,16},{24,28},{28,24},{1,5},{5... | collective-permute-start | bytes 24584 | tf_op jit(solution)/shard_map/ppermute | solution.py:388
  31.6 11.7 %all-to-all-start = ((f32[16,1,128]{2,1,0:T(1,128)}), f32[16,1,128]{2,1,0:T(1,128)S(1)}, u32[]{:S(2)}, u32[]{:S(2)}) async-start(f32[16,1,128]{2,1,0:T(1,128)} %bitcast.6), calls=%async_computation | async-start | bytes 16384 | tf_op jit(solution)/shard_map/all_to_all | solution.py:518

commit v4 on v0

--- a/solution.py
+++ b/solution.py
@@ -388,6 +388,11 @@
     return lax.ppermute(value, "block", [(index, index ^ mask) for index in range(blocks)])
 
 
+def turn(value, shift, walkers):
+    pairs = [(index, (index + shift) % walkers) for index in range(walkers)]
+    return lax.ppermute(value, "walker", pairs)
+
+
 def body(green, chol, counts, move_slot, move_dest):
     walkers = lax.axis_size("walker")
     blocks = lax.axis_size("block")
@@ -425,12 +430,7 @@
         compiler_params=limit,
         name="leave",
     )(walker_index, table, own_rows)
-    coming = [
-        lax.ppermute(
-            leaving[shift - 1], "walker", [(z, (z + shift) % walkers) for z in range(walkers)]
-        )
-        for shift in range(1, walkers)
-    ]
+    coming = [turn(leaving[shift - 1], shift, walkers) for shift in range(1, walkers)]
 
     group = 4
     groups = vectors // group
@@ -495,6 +495,14 @@
     )(block_index, place, weights, near_sums, late, *far_pieces)
 
     coming, _ = lax.optimization_barrier((coming, all_sums))
+    energy_scale = 0.5 / (occ_count * math.sqrt(vectors * blocks))
+    all_sums = all_sums + swap(all_sums, core, blocks)
+    all_sums, coming[2:] = lax.optimization_barrier((all_sums, coming[2:]))
+    others = [swap(all_sums, mask, blocks) for mask in (near_x, near_y, near_x | near_y)]
+    all_sums = (all_sums + others[0]) + (others[1] + others[2])
+    others = [turn(all_sums, shift, walkers) for shift in range(1, walkers)]
+    all_sums = functools.reduce(jnp.add, others, all_sums)
+    own_sums = lax.dynamic_slice(all_sums[0], (walker_index[0] * keep,), (keep,))
     new_green = pl.pallas_call(
         functools.partial(assemble_kernel, move_dims),
         out_shape=jax.ShapeDtypeStruct((keep, share_width), jnp.bfloat16),
@@ -509,15 +517,6 @@
         name="assemble",
     )(walker_index, table, green, *coming)
 
-    energy_scale = 0.5 / (occ_count * math.sqrt(vectors * blocks))
-    for mask in (core, near_x, near_y):
-        all_sums = all_sums + swap(all_sums, mask, blocks)
-    mask = 1
-    while mask < walkers:
-        pairs = [(index, index ^ mask) for index in range(walkers)]
-        all_sums = all_sums + lax.ppermute(all_sums, "walker", pairs)
-        mask *= 2
-    own_sums = lax.dynamic_slice(all_sums[0], (walker_index[0] * keep,), (keep,))
     return (new_green, -energy_scale * own_sums)
 
 

time: 46.8 us -> 45.9 us (0.981)
  waiting for transfers between devices: 13.7 us -> 8.85 us
  starting transfers between devices: 16.3 us -> 20.2 us
    ppermute x5 -> x6, waiting for transfers between devices: 7.19 us -> 2.42 us  [turn(): return lax.ppermute(value, 'walker', pairs)]
    ppermute x5 -> x6, starting transfers between devices: 6.54 us -> 9.98 us  [turn(): return lax.ppermute(value, 'walker', pairs)]
    ppermute x12 -> x13, starting transfers between devices: 9.73 us -> 10.2 us  [swap(): lax.ppermute(value, 'block', [(index, index ^ mask) for index in range(bl...]
    ppermute x12 -> x13, waiting for transfers between devices: 6.56 us -> 6.43 us  [swap(): lax.ppermute(value, 'block', [(index, index ^ mask) for index in range(bl...]
  transfers between devices with their start and end apart: 17 -> 19, of which waited for: 10 -> 10; matrix products, arithmetic and copies ran while one was open for 2% -> 2% of each run, Pallas kernels for 28% -> 29%
where the time goes in v4:
time: 45.9 us; the launch traced here: 45.7 us
  starting transfers between devices  20.2 us (44%)
  Pallas kernels  13.5 us (29%)
  waiting for transfers between devices  8.85 us (19%)
  other arithmetic  1.3 us (3%)
  local copies, waits for them, and re-layouts  1.09 us (2%)
  between operations  0.74 us (2%)
    ppermute x13, starting transfers between devices, swap(): lax.ppermute(value, 'block', [(index, index ^ mask) for index in range(bl...  10.2 us
    ppermute x6, starting transfers between devices, turn(): return lax.ppermute(value, 'walker', pairs)  9.98 us
    ppermute x13, waiting for transfers between devices, swap(): lax.ppermute(value, 'block', [(index, index ^ mask) for index in range(bl...  6.43 us
    pallas_call x1, Pallas kernels, body(): pl.pallas_call(functools.partial(near_kernel, dims), out_shape=[jax.Shape...  4.71 us
    pallas_call x1, Pallas kernels, body(): pl.pallas_call(functools.partial(order_kernel, (group, groups, chip_rows)...  2.76 us
    ppermute x6, waiting for transfers between devices, turn(): return lax.ppermute(value, 'walker', pairs)  2.42 us
    pallas_call x1, Pallas kernels, body(): pl.pallas_call(functools.partial(far_kernel, dims), out_shape=jax.ShapeDt...  2.41 us
    pallas_call x1, Pallas kernels, body(): pl.pallas_call(functools.partial(assemble_kernel, move_dims), out_shape=j...  1.93 us
  transfers between devices with their start and end apart: 19, of which 10 were waited for; matrix products, arithmetic and copies ran while one was open for 2% of the time, Pallas kernels for 29%

profile of v4, /device:TPU:0, one launch (start us, length us, event | category | flops | bytes accessed | tf_op | source)
XLA Modules:
  0.0 45.7 jit_solution(4360392433674717895)
XLA Ops:
  0.6 1.1 %copy-done = bf16[5,36864]{1,0:T(8,128)(2,1)S(1)} copy-done((bf16[5,36864]{1,0:T(8,128)(2,1)S(1)}, bf16[5,36864]{1,0:T(8,128)(2,1)}, u32[]{:S(2)}) %copy-start) | copy-done | bytes 368664
  2.0 3.0 %collective-permute-start = (bf16[128,1536]{1,0:T(8,128)(2,1)S(1)}, bf16[128,1536]{1,0:T(8,128)(2,1)S(1)}, u32[]{:S(2)}, u32[]{:S(2)}) collective-permute-start(bf16[128,1536]{1,0:T(8,128)(2,1)S(1)} %pack.1.own_ref.refs_0_), channel_id=1, source_target_pairs={{0,8},{4,12},{8,0},{12,4},{16,24},{20,28},{24,16},{28,20},{1,9},{5... | collective-permute-start | bytes 1179656 | tf_op jit(solution)/shard_map/ppermute | solution.py:388
  5.0 1.5 %collective-permute-start.1 = (bf16[128,1536]{1,0:T(8,128)(2,1)S(1)}, bf16[128,1536]{1,0:T(8,128)(2,1)S(1)}, u32[]{:S(2)}, u32[]{:S(2)}) collective-permute-start(bf16[128,1536]{1,0:T(8,128)(2,1)S(1)} %pack.1.own_ref.refs_0_), channel_id=1, source_target_pairs={{0,16},{4,20},{8,24},{12,28},{16,0},{20,4},{24,8},{28,12},{1,17},{... | collective-permute-start | bytes 1179656 | tf_op jit(solution)/shard_map/ppermute | solution.py:388
  6.5 0.7 %pad_add_fusion.table_ref = s32[5,4]{1,0:T(8,128)S(1)} fusion(s32[2,4]{1,0:T(2,128)} %bitcast.7, s32[2,4]{1,0:T(2,128)} %bitcast.8, s32[1,4]{1,0:T(1,128)} %bitcast.9), kind=kLoop, calls=%fused_computation | loop fusion | flops 40 | bytes 160 | tf_op jit(solution)/shard_map/concatenate | solution.py:405
  7.2 1.4 %leave.1 = (bf16[24,1536]{1,0:T(8,128)(2,1)S(1)}, bf16[24,1536]{1,0:T(8,128)(2,1)S(1)}, bf16[24,1536]{1,0:T(8,128)(2,1)S(1)}, s32[5]{0:T(128)S(1)}) custom-call(s32[1]{0:T(128)} %bitcast.ident_ref, s32[5,4]{1,0:T(8,128)S(1)} %pad_add_fusion.table_ref, bf16[128,1536]{1,0:T(8,128)(2,1)S(1)} %pack.1.own_ref.refs_0_), custom_call_target="tpu_custom_call" | custom-call | tf_op jit(solution)/shard_map/leave/pallas_call | solution.py:423
  8.6 1.6 %collective-permute-start.2 = (bf16[24,1536]{1,0:T(8,128)(2,1)S(1)}, bf16[24,1536]{1,0:T(8,128)(2,1)S(1)}, u32[]{:S(2)}, u32[]{:S(2)}) collective-permute-start(bf16[24,1536]{1,0:T(8,128)(2,1)S(1)} %get-tuple-element.21), channel_id=1, source_target_pairs={{0,1},{1,2},{2,3},{3,0},{4,5},{5,6},{6,7},{7,4},{8,9},{9,10},{10,1... | collective-permute-start | bytes 221192 | tf_op jit(solution)/shard_map/ppermute | solution.py:393
  10.3 2.6 %collective-permute-start.3 = (bf16[24,1536]{1,0:T(8,128)(2,1)S(1)}, bf16[24,1536]{1,0:T(8,128)(2,1)S(1)}, u32[]{:S(2)}, u32[]{:S(2)}) collective-permute-start(bf16[24,1536]{1,0:T(8,128)(2,1)S(1)} %get-tuple-element.22), channel_id=1, source_target_pairs={{0,2},{1,3},{2,0},{3,1},{4,6},{5,7},{6,4},{7,5},{8,10},{9,11},{10,... | collective-permute-start | bytes 221192 | tf_op jit(solution)/shard_map/ppermute | solution.py:393
  12.9 2.8 %order.1.weight_ref = bf16[1536,1536]{1,0:T(8,128)(2,1)S(1)} custom-call(s32[1]{0:T(128)} %bitcast.4.ident_ref, bf16[8,192,1536]{2,1,0:T(8,128)(2,1)} %chol_ref.1, bf16[128,1536]{1,0:T(8,128)(2,1)S(1)} %pack.1.own_ref.refs_0_), custom_call_target="tpu_custom_call" | custom-call | bytes 9437184 | tf_op jit(solution)/shard_map/order/pallas_call | solution.py:438
  15.6 1.5 %collective-permute-done.3.refs_1_ = bf16[24,1536]{1,0:T(8,128)(2,1)S(1)} collective-permute-done((bf16[24,1536]{1,0:T(8,128)(2,1)S(1)}, bf16[24,1536]{1,0:T(8,128)(2,1)S(1)}, u32[]{:S(2)}, u32[]{:S(2)}) %collective-permute-start.3) | collective-permute-done | bytes 73760 | tf_op jit(solution)/shard_map/ppermute | solution.py:393
  17.7 0.6 %collective-permute-start.5 = (bf16[128,768]{1,0:T(8,128)(2,1)S(1)}, bf16[128,768]{1,0:T(8,128)(2,1)S(1)}, u32[]{:S(2)}, u32[]{:S(2)}) collective-permute-start(bf16[128,768]{1,0:T(8,128)(2,1)S(1)} %slice.6), channel_id=1, source_target_pairs={{0,8},{4,12},{8,0},{12,4},{16,24},{20,28},{24,16},{28,20},{1,9},{5... | collective-permute-start | bytes 589832 | tf_op jit(solution)/shard_map/ppermute | solution.py:388
  18.9 0.6 %collective-permute-done.9.refs_5_ = bf16[128,1536]{1,0:T(8,128)(2,1)S(1)} collective-permute-done((bf16[128,1536]{1,0:T(8,128)(2,1)S(1)}, bf16[128,1536]{1,0:T(8,128)(2,1)S(1)}, u32[]{:S(2)}, u32[]{:S(2)}) %collective-permute-start.9) | collective-permute-done | bytes 393248 | tf_op jit(solution)/shard_map/ppermute | solution.py:388
  19.4 4.7 %near.1 = (f32[40,128]{1,0:T(8,128)S(1)}, f32[240,1536]{1,0:T(8,128)S(1)}) custom-call(s32[1]{0:T(128)} %bitcast.4.ident_ref, bf16[1536,1536]{1,0:T(8,128)(2,1)S(1)} %order.1.weight_ref, bf16[128,1536]{1,0:T(8,128)(2,1)S(1)} %pack.1.own_ref.refs_0_, bf16[128,1536]{1,0:T(8,128)(2,1)S(1)} %collective-permute-done.7.refs_1_, ...), custom_call_target="tpu_custom_call" | custom-call | flops 3623878656 | bytes 4718592 | tf_op jit(solution)/shard_map/near/pallas_call | solution.py:466
  25.4 1.9 %collective-permute-start.4 = (bf16[24,1536]{1,0:T(8,128)(2,1)S(1)}, bf16[24,1536]{1,0:T(8,128)(2,1)S(1)}, u32[]{:S(2)}, u32[]{:S(2)}) collective-permute-start(bf16[24,1536]{1,0:T(8,128)(2,1)S(1)} %get-tuple-element.25), channel_id=1, source_target_pairs={{0,3},{1,0},{2,1},{3,2},{4,7},{5,4},{6,5},{7,6},{8,11},{9,8},{10,9... | collective-permute-start | bytes 221192 | tf_op jit(solution)/shard_map/ppermute | solution.py:393
  27.4 2.4 %far.1 = f32[1,128]{1,0:T(1,128)S(1)} custom-call(s32[1]{0:T(128)} %bitcast.4.ident_ref, s32[5]{0:T(128)S(1)} %get-tuple-element.26.place_ref, bf16[1536,1536]{1,0:T(8,128)(2,1)S(1)} %order.1.weight_ref, f32[40,128]{1,0:T(8,128)S(1)} %get-tuple-element.31.near_sum_ref, f32[240,1536]{1,0:T(8,128)S(1)} %get-tuple-element.32.late_ref, ...), custom_call_target="tpu_custom_call" | custom-call | flops 1207959552 | bytes 4718592 | tf_op jit(solution)/shard_map/far/pallas_call | solution.py:484
  29.9 1.1 %collective-permute-done.12 = f32[1,128]{1,0:T(1,128)S(1)} collective-permute-done((f32[1,128]{1,0:T(1,128)S(1)}, f32[1,128]{1,0:T(1,128)S(1)}, u32[]{:S(2)}, u32[]{:S(2)}) %collective-permute-start.12) | collective-permute-done | bytes 544 | tf_op jit(solution)/shard_map/ppermute | solution.py:388
  31.0 1.5 %collective-permute-start.13 = (f32[1,128]{1,0:T(1,128)S(1)}, f32[1,128]{1,0:T(1,128)S(1)}, u32[]{:S(2)}, u32[]{:S(2)}) collective-permute-start(f32[1,128]{1,0:T(1,128)S(1)} %add.24), channel_id=1, source_target_pairs={{0,8},{4,12},{8,0},{12,4},{16,24},{20,28},{24,16},{28,20},{1,9},{5... | collective-permute-start | bytes 1544 | tf_op jit(solution)/shard_map/ppermute | solution.py:388
  32.5 1.5 %collective-permute-start.14 = (f32[1,128]{1,0:T(1,128)S(1)}, f32[1,128]{1,0:T(1,128)S(1)}, u32[]{:S(2)}, u32[]{:S(2)}) collective-permute-start(f32[1,128]{1,0:T(1,128)S(1)} %add.24), channel_id=1, source_target_pairs={{0,16},{4,20},{8,24},{12,28},{16,0},{20,4},{24,8},{28,12},{1,17},{... | collective-permute-start | bytes 1544 | tf_op jit(solution)/shard_map/ppermute | solution.py:388
  34.5 1.5 %collective-permute-done.14 = f32[1,128]{1,0:T(1,128)S(1)} collective-permute-done((f32[1,128]{1,0:T(1,128)S(1)}, f32[1,128]{1,0:T(1,128)S(1)}, u32[]{:S(2)}, u32[]{:S(2)}) %collective-permute-start.14) | collective-permute-done | bytes 544 | tf_op jit(solution)/shard_map/ppermute | solution.py:388
  36.0 2.4 %collective-permute-done.15 = f32[1,128]{1,0:T(1,128)S(1)} collective-permute-done((f32[1,128]{1,0:T(1,128)S(1)}, f32[1,128]{1,0:T(1,128)S(1)}, u32[]{:S(2)}, u32[]{:S(2)}) %collective-permute-start.15) | collective-permute-done | bytes 544 | tf_op jit(solution)/shard_map/ppermute | solution.py:388
  38.4 3.1 %collective-permute-start.17 = (f32[1,128]{1,0:T(1,128)S(1)}, f32[1,128]{1,0:T(1,128)S(1)}, u32[]{:S(2)}, u32[]{:S(2)}) collective-permute-start(f32[1,128]{1,0:T(1,128)S(1)} %add_add_fusion.1), channel_id=1, source_target_pairs={{0,2},{1,3},{2,0},{3,1},{4,6},{5,7},{6,4},{7,5},{8,10},{9,11},{10,... | collective-permute-start | bytes 1544 | tf_op jit(solution)/shard_map/ppermute | solution.py:393
  41.5 0.7 %collective-permute-start.18 = (f32[1,128]{1,0:T(1,128)S(1)}, f32[1,128]{1,0:T(1,128)S(1)}, u32[]{:S(2)}, u32[]{:S(2)}) collective-permute-start(f32[1,128]{1,0:T(1,128)S(1)} %add_add_fusion.1), channel_id=1, source_target_pairs={{0,3},{1,0},{2,1},{3,2},{4,7},{5,4},{6,5},{7,6},{8,11},{9,8},{10,9... | collective-permute-start | bytes 1544 | tf_op jit(solution)/shard_map/ppermute | solution.py:393
  42.3 1.9 %assemble.1 = bf16[3,36864]{1,0:T(4,128)(2,1)} custom-call(s32[1]{0:T(128)} %bitcast.ident_ref, s32[5,4]{1,0:T(8,128)S(1)} %pad_add_fusion.table_ref, bf16[5,36864]{1,0:T(8,128)(2,1)S(1)} %copy-done.1, bf16[24,1536]{1,0:T(8,128)(2,1)S(1)} %collective-permute-done.2.refs_0_, bf16[24,1536]{1,0:T(8,128)(2,1)S(1)} %collective-permute-done.3.refs_1_, ...), custom_call_target="tpu_custom_call" | custom-call | tf_op jit(solution)/shard_map/assemble/pallas_call | solution.py:506
  44.2 0.9 %collective-permute-done.18 = f32[1,128]{1,0:T(1,128)S(1)} collective-permute-done((f32[1,128]{1,0:T(1,128)S(1)}, f32[1,128]{1,0:T(1,128)S(1)}, u32[]{:S(2)}, u32[]{:S(2)}) %collective-permute-start.18) | collective-permute-done | bytes 544 | tf_op jit(solution)/shard_map/ppermute | solution.py:393
  45.1 0.6 %multiply_bitcast_fusion = f32[3]{0:T(128)} fusion(f32[1,128]{1,0:T(1,128)S(1)} %add_add_fusion, s32[]{:T(128)S(6)} %select_n.3), kind=kLoop, calls=%fused_computation.1 | loop fusion | flops 3 | bytes 28 | tf_op jit(solution)/shard_map/mul | solution.py:520
  (31 shorter events, 3.3 us)
Async XLA Ops:
  0.6 1.1 %copy-start = (bf16[5,36864]{1,0:T(8,128)(2,1)S(1)}, bf16[5,36864]{1,0:T(8,128)(2,1)}, u32[]{:S(2)}) copy-start(bf16[5,36864]{1,0:T(8,128)(2,1)} %green_ref.3) | copy-start | bytes 1105924
  2.0 15.2 %collective-permute-start = (bf16[128,1536]{1,0:T(8,128)(2,1)S(1)}, bf16[128,1536]{1,0:T(8,128)(2,1)S(1)}, u32[]{:S(2)}, u32[]{:S(2)}) collective-permute-start(bf16[128,1536]{1,0:T(8,128)(2,1)S(1)} %pack.1.own_ref.refs_0_), channel_id=1, source_target_pairs={{0,8},{4,12},{8,0},{12,4},{16,24},{20,28},{24,16},{28,20},{1,9},{5... | collective-permute-start | bytes 1179656 | tf_op jit(solution)/shard_map/ppermute | solution.py:388
  5.0 12.2 %collective-permute-start.1 = (bf16[128,1536]{1,0:T(8,128)(2,1)S(1)}, bf16[128,1536]{1,0:T(8,128)(2,1)S(1)}, u32[]{:S(2)}, u32[]{:S(2)}) collective-permute-start(bf16[128,1536]{1,0:T(8,128)(2,1)S(1)} %pack.1.own_ref.refs_0_), channel_id=1, source_target_pairs={{0,16},{4,20},{8,24},{12,28},{16,0},{20,4},{24,8},{28,12},{1,17},{... | collective-permute-start | bytes 1179656 | tf_op jit(solution)/shard_map/ppermute | solution.py:388
  8.6 7.0 %collective-permute-start.2 = (bf16[24,1536]{1,0:T(8,128)(2,1)S(1)}, bf16[24,1536]{1,0:T(8,128)(2,1)S(1)}, u32[]{:S(2)}, u32[]{:S(2)}) collective-permute-start(bf16[24,1536]{1,0:T(8,128)(2,1)S(1)} %get-tuple-element.21), channel_id=1, source_target_pairs={{0,1},{1,2},{2,3},{3,0},{4,5},{5,6},{6,7},{7,4},{8,9},{9,10},{10,1... | collective-permute-start | bytes 221192 | tf_op jit(solution)/shard_map/ppermute | solution.py:393
  10.3 6.9 %collective-permute-start.3 = (bf16[24,1536]{1,0:T(8,128)(2,1)S(1)}, bf16[24,1536]{1,0:T(8,128)(2,1)S(1)}, u32[]{:S(2)}, u32[]{:S(2)}) collective-permute-start(bf16[24,1536]{1,0:T(8,128)(2,1)S(1)} %get-tuple-element.22), channel_id=1, source_target_pairs={{0,2},{1,3},{2,0},{3,1},{4,6},{5,7},{6,4},{7,5},{8,10},{9,11},{10,... | collective-permute-start | bytes 221192 | tf_op jit(solution)/shard_map/ppermute | solution.py:393
  12.8 6.0 %collective-permute-start.7 = (bf16[128,1536]{1,0:T(8,128)(2,1)S(1)}, bf16[128,1536]{1,0:T(8,128)(2,1)S(1)}, u32[]{:S(2)}, u32[]{:S(2)}) collective-permute-start(bf16[128,1536]{1,0:T(8,128)(2,1)S(1)} %pack.1.own_ref.refs_0_), channel_id=1, source_target_pairs={{0,4},{4,0},{8,12},{12,8},{16,20},{20,16},{24,28},{28,24},{1,5},{5... | collective-permute-start | bytes 1179656 | tf_op jit(solution)/shard_map/ppermute | solution.py:388
  17.2 1.7 %collective-permute-start.8 = (bf16[128,1536]{1,0:T(8,128)(2,1)S(1)}, bf16[128,1536]{1,0:T(8,128)(2,1)S(1)}, u32[]{:S(2)}, u32[]{:S(2)}) collective-permute-start(bf16[128,1536]{1,0:T(8,128)(2,1)S(1)} %collective-permute-done.refs_2_), channel_id=1, source_target_pairs={{0,4},{4,0},{8,12},{12,8},{16,20},{20,16},{24,28},{28,24},{1,5},{5... | collective-permute-start | bytes 1179656 | tf_op jit(solution)/shard_map/ppermute | solution.py:388
  17.2 2.3 %collective-permute-start.9 = (bf16[128,1536]{1,0:T(8,128)(2,1)S(1)}, bf16[128,1536]{1,0:T(8,128)(2,1)S(1)}, u32[]{:S(2)}, u32[]{:S(2)}) collective-permute-start(bf16[128,1536]{1,0:T(8,128)(2,1)S(1)} %collective-permute-done.1.refs_4_), channel_id=1, source_target_pairs={{0,4},{4,0},{8,12},{12,8},{16,20},{20,16},{24,28},{28,24},{1,5},{5... | collective-permute-start | bytes 1179656 | tf_op jit(solution)/shard_map/ppermute | solution.py:388
  17.7 6.9 %collective-permute-start.5 = (bf16[128,768]{1,0:T(8,128)(2,1)S(1)}, bf16[128,768]{1,0:T(8,128)(2,1)S(1)}, u32[]{:S(2)}, u32[]{:S(2)}) collective-permute-start(bf16[128,768]{1,0:T(8,128)(2,1)S(1)} %slice.6), channel_id=1, source_target_pairs={{0,8},{4,12},{8,0},{12,4},{16,24},{20,28},{24,16},{28,20},{1,9},{5... | collective-permute-start | bytes 589832 | tf_op jit(solution)/shard_map/ppermute | solution.py:388
  18.3 6.6 %collective-permute-start.6 = (bf16[128,768]{1,0:T(8,128)(2,1)S(1)}, bf16[128,768]{1,0:T(8,128)(2,1)S(1)}, u32[]{:S(2)}, u32[]{:S(2)}) collective-permute-start(bf16[128,768]{1,0:T(8,128)(2,1)S(1)} %slice.7), channel_id=1, source_target_pairs={{0,16},{4,20},{8,24},{12,28},{16,0},{20,4},{24,8},{28,12},{1,17},{... | collective-permute-start | bytes 589832 | tf_op jit(solution)/shard_map/ppermute | solution.py:388
  24.2 18.1 %copy-start.1 = (bf16[5,36864]{1,0:T(8,128)(2,1)S(1)}, bf16[5,36864]{1,0:T(8,128)(2,1)}, u32[]{:S(2)}) copy-start(bf16[5,36864]{1,0:T(8,128)(2,1)} %green_ref.3) | copy-start | bytes 1105924
  24.9 2.5 %collective-permute-start.10 = (bf16[128,768]{1,0:T(8,128)(2,1)S(1)}, bf16[128,768]{1,0:T(8,128)(2,1)S(1)}, u32[]{:S(2)}, u32[]{:S(2)}) collective-permute-start(bf16[128,768]{1,0:T(8,128)(2,1)S(1)} %collective-permute-done.5.refs_0_), channel_id=1, source_target_pairs={{0,4},{4,0},{8,12},{12,8},{16,20},{20,16},{24,28},{28,24},{1,5},{5... | collective-permute-start | bytes 589832 | tf_op jit(solution)/shard_map/ppermute | solution.py:388
  24.9 2.5 %collective-permute-start.11 = (bf16[128,768]{1,0:T(8,128)(2,1)S(1)}, bf16[128,768]{1,0:T(8,128)(2,1)S(1)}, u32[]{:S(2)}, u32[]{:S(2)}) collective-permute-start(bf16[128,768]{1,0:T(8,128)(2,1)S(1)} %collective-permute-done.6.refs_1_), channel_id=1, source_target_pairs={{0,4},{4,0},{8,12},{12,8},{16,20},{20,16},{24,28},{28,24},{1,5},{5... | collective-permute-start | bytes 589832 | tf_op jit(solution)/shard_map/ppermute | solution.py:388
  25.4 4.4 %collective-permute-start.4 = (bf16[24,1536]{1,0:T(8,128)(2,1)S(1)}, bf16[24,1536]{1,0:T(8,128)(2,1)S(1)}, u32[]{:S(2)}, u32[]{:S(2)}) collective-permute-start(bf16[24,1536]{1,0:T(8,128)(2,1)S(1)} %get-tuple-element.25), channel_id=1, source_target_pairs={{0,3},{1,0},{2,1},{3,2},{4,7},{5,4},{6,5},{7,6},{8,11},{9,8},{10,9... | collective-permute-start | bytes 221192 | tf_op jit(solution)/shard_map/ppermute | solution.py:393
  29.8 1.2 %collective-permute-start.12 = (f32[1,128]{1,0:T(1,128)S(1)}, f32[1,128]{1,0:T(1,128)S(1)}, u32[]{:S(2)}, u32[]{:S(2)}) collective-permute-start(f32[1,128]{1,0:T(1,128)S(1)} %far.1), channel_id=1, source_target_pairs={{0,4},{4,0},{8,12},{12,8},{16,20},{20,16},{24,28},{28,24},{1,5},{5... | collective-permute-start | bytes 1544 | tf_op jit(solution)/shard_map/ppermute | solution.py:388
  31.0 3.5 %collective-permute-start.13 = (f32[1,128]{1,0:T(1,128)S(1)}, f32[1,128]{1,0:T(1,128)S(1)}, u32[]{:S(2)}, u32[]{:S(2)}) collective-permute-start(f32[1,128]{1,0:T(1,128)S(1)} %add.24), channel_id=1, source_target_pairs={{0,8},{4,12},{8,0},{12,4},{16,24},{20,28},{24,16},{28,20},{1,9},{5... | collective-permute-start | bytes 1544 | tf_op jit(solution)/shard_map/ppermute | solution.py:388
  32.5 3.5 %collective-permute-start.14 = (f32[1,128]{1,0:T(1,128)S(1)}, f32[1,128]{1,0:T(1,128)S(1)}, u32[]{:S(2)}, u32[]{:S(2)}) collective-permute-start(f32[1,128]{1,0:T(1,128)S(1)} %add.24), channel_id=1, source_target_pairs={{0,16},{4,20},{8,24},{12,28},{16,0},{20,4},{24,8},{28,12},{1,17},{... | collective-permute-start | bytes 1544 | tf_op jit(solution)/shard_map/ppermute | solution.py:388
  34.0 4.4 %collective-permute-start.15 = (f32[1,128]{1,0:T(1,128)S(1)}, f32[1,128]{1,0:T(1,128)S(1)}, u32[]{:S(2)}, u32[]{:S(2)}) collective-permute-start(f32[1,128]{1,0:T(1,128)S(1)} %add.24), channel_id=1, source_target_pairs={{0,24},{4,28},{8,16},{12,20},{16,8},{20,12},{24,0},{28,4},{1,25},{... | collective-permute-start | bytes 1544 | tf_op jit(solution)/shard_map/ppermute | solution.py:388
  38.4 5.8 %collective-permute-start.16 = (f32[1,128]{1,0:T(1,128)S(1)}, f32[1,128]{1,0:T(1,128)S(1)}, u32[]{:S(2)}, u32[]{:S(2)}) collective-permute-start(f32[1,128]{1,0:T(1,128)S(1)} %add_add_fusion.1), channel_id=1, source_target_pairs={{0,1},{1,2},{2,3},{3,0},{4,5},{5,6},{6,7},{7,4},{8,9},{9,10},{10,1... | collective-permute-start | bytes 1544 | tf_op jit(solution)/shard_map/ppermute | solution.py:393
  38.4 5.8 %collective-permute-start.17 = (f32[1,128]{1,0:T(1,128)S(1)}, f32[1,128]{1,0:T(1,128)S(1)}, u32[]{:S(2)}, u32[]{:S(2)}) collective-permute-start(f32[1,128]{1,0:T(1,128)S(1)} %add_add_fusion.1), channel_id=1, source_target_pairs={{0,2},{1,3},{2,0},{3,1},{4,6},{5,7},{6,4},{7,5},{8,10},{9,11},{10,... | collective-permute-start | bytes 1544 | tf_op jit(solution)/shard_map/ppermute | solution.py:393
  41.5 3.5 %collective-permute-start.18 = (f32[1,128]{1,0:T(1,128)S(1)}, f32[1,128]{1,0:T(1,128)S(1)}, u32[]{:S(2)}, u32[]{:S(2)}) collective-permute-start(f32[1,128]{1,0:T(1,128)S(1)} %add_add_fusion.1), channel_id=1, source_target_pairs={{0,3},{1,0},{2,1},{3,2},{4,7},{5,4},{6,5},{7,6},{8,11},{9,8},{10,9... | collective-permute-start | bytes 1544 | tf_op jit(solution)/shard_map/ppermute | solution.py:393

commit v5 on v1

--- a/solution.py
+++ b/solution.py
@@ -107,12 +107,10 @@
 
 
 def pack_kernel(dims, green_ref, own_ref, spread):
-    slots, share_rows, orb_count, pad_rows = dims
+    slots, share_rows, orb_count = dims
     spread_slots(green_ref, spread, share_rows)
     for tile in range(orb_count // LANES):
         dense = [spread[tile, pl.ds(slot, share_rows, stride=ROWS), :] for slot in range(slots)]
-        if pad_rows > slots * share_rows:
-            dense.append(jnp.zeros((pad_rows - slots * share_rows, LANES), jnp.float32))
         packed = jnp.concatenate(dense, axis=0).astype(jnp.bfloat16)
         own_ref[:, tile * LANES : (tile + 1) * LANES] = packed
 
@@ -260,6 +258,20 @@
         copy.wait()
 
 
+def padded(rows):
+    return -(-rows // 16) * 16
+
+
+def stacked(refs):
+    values = []
+    for ref in refs:
+        rows, width = ref.shape
+        values.append(ref[...])
+        if padded(rows) > rows:
+            values.append(jnp.zeros((padded(rows) - rows, width), jnp.bfloat16))
+    return jnp.concatenate(values, axis=0)
+
+
 def times(left, right):
     return lax.dot_general(
         left, right, (((1,), (1,)), ((), ())), preferred_element_type=jnp.float32
@@ -273,12 +285,12 @@
     trans_refs = refs[8:]
     own = ident_ref[0]
     core = lax.rem(own, 2)
-    pad_rows = piece_refs[0].shape[0]
+    pad_rows = padded(piece_refs[0].shape[0])
     near = 3 * chip_rows
     size = 4 * chip_rows * group
     edge = near - LANES
     half = LANES // 2
-    left = jnp.concatenate([ref[...] for ref in piece_refs], axis=0)
+    left = stacked(piece_refs)
     lane = lax.broadcasted_iota(jnp.int32, (1, LANES), 1)
     low_half = lane < half
     in_edge = jnp.where(low_half, lane, lane - half) < edge
@@ -335,17 +347,15 @@
     trans_refs = refs[5:]
     own = ident_ref[0]
     core = lax.rem(own, 2)
-    pad_rows, width = piece_refs[0].shape
+    pack_rows, width = piece_refs[0].shape
+    pad_rows = padded(pack_rows)
     half = LANES // 2
     edge = half - chip_rows
     size = 4 * chip_rows * group
     lane = lax.broadcasted_iota(jnp.int32, (1, LANES), 1)
     low_half = lane < half
     in_rest = jnp.where(low_half, lane, lane - half) >= edge
-    lefts = [
-        jnp.concatenate([piece_refs[part][...], piece_refs[2 + part][...]], axis=0)
-        for part in range(2)
-    ]
+    lefts = [stacked(piece_refs[part::2]) for part in range(2)]
     twice = [jnp.zeros((ROWS, LANES), jnp.float32) for _ in range(slots)]
     once = [near_sum_ref[slot * ROWS : (slot + 1) * ROWS, :] for slot in range(slots)]
 
@@ -396,7 +406,7 @@
     moves = move_slot.shape[1]
     keep = slots - moves
     share_rows = share_width // orb_count
-    pad_rows = -(-slots * share_rows // 16) * 16
+    pack_rows = slots * share_rows
     table = jnp.concatenate([counts[None, :], move_slot.T, move_dest.T], axis=0)
     walker_index = lax.axis_index("walker").astype(jnp.int32).reshape(1)
     block_index = lax.axis_index("block").astype(jnp.int32).reshape(1)
@@ -406,8 +416,8 @@
 
     spread = pltpu.VMEM((orb_count // LANES, share_rows * ROWS, LANES), jnp.float32)
     own_rows = pl.pallas_call(
-        functools.partial(pack_kernel, (slots, share_rows, orb_count, pad_rows)),
-        out_shape=jax.ShapeDtypeStruct((pad_rows, orb_count), jnp.bfloat16),
+        functools.partial(pack_kernel, (slots, share_rows, orb_count)),
+        out_shape=jax.ShapeDtypeStruct((pack_rows, orb_count), jnp.bfloat16),
         in_specs=[vmem],
         out_specs=vmem,
         scratch_shapes=[spread],
@@ -421,7 +431,7 @@
         + [jax.ShapeDtypeStruct((slots,), jnp.int32)],
         in_specs=[smem, smem, vmem],
         out_specs=[vmem] * (walkers - 1) + [smem],
-        scratch_shapes=[pltpu.VMEM((pad_rows, orb_count), jnp.float32)],
+        scratch_shapes=[pltpu.VMEM((pack_rows, orb_count), jnp.float32)],
         compiler_params=limit,
         name="leave",
     )(walker_index, table, own_rows)
@@ -462,7 +472,7 @@
         near_pieces += [piece, swap(piece, core, blocks)]
 
     dims = (slots, share_rows, group, groups, chip_rows)
-    work = 2 * vectors * occ_count * orb_count * pad_rows
+    work = 2 * vectors * occ_count * orb_count * pack_rows
     near_sums, late = pl.pallas_call(
         functools.partial(near_kernel, dims),
         out_shape=[

time: 41.9 us -> 41 us (0.979)
  starting transfers between devices: 16.3 us -> 15.7 us
    ppermute x3, starting transfers between devices: 6.15 us -> 5.72 us  [body(): lax.ppermute(leaving[shift - 1], 'walker', [(z, (z + shift) % walkers) fo...]
  transfers between devices with their start and end apart: 13 -> 13, of which waited for: 6 -> 5; matrix products, arithmetic and copies ran while one was open for 2% -> 2% of each run, Pallas kernels for 33% -> 34%
where the time goes in v5:
time: 41 us; the launch traced here: 40.8 us
  starting transfers between devices  15.7 us (38%)
  Pallas kernels  14.1 us (34%)
  waiting for transfers between devices  7.85 us (19%)
  other arithmetic  1.34 us (3%)
  local copies, waits for them, and re-layouts  1.09 us (3%)
  between operations  0.74 us (2%)
    ppermute x9, starting transfers between devices, swap(): lax.ppermute(value, 'block', [(index, index ^ mask) for index in range(bl...  6.65 us
    ppermute x3, starting transfers between devices, body(): lax.ppermute(leaving[shift - 1], 'walker', [(z, (z + shift) % walkers) fo...  5.72 us
    all_to_all x1, waiting for transfers between devices, body(): lax.all_to_all(all_sums, ('block', 'walker'), split_axis=0, concat_axis=0...  5.21 us
    pallas_call x1, Pallas kernels, body(): pl.pallas_call(functools.partial(near_kernel, dims), out_shape=[jax.Shape...  4.71 us
    all_to_all x1, starting transfers between devices, body(): lax.all_to_all(all_sums, ('block', 'walker'), split_axis=0, concat_axis=0...  3.33 us
    pallas_call x1, Pallas kernels, body(): pl.pallas_call(functools.partial(far_kernel, dims), out_shape=jax.ShapeDt...  3.02 us
    pallas_call x1, Pallas kernels, body(): pl.pallas_call(functools.partial(order_kernel, (group, groups, chip_rows)...  2.76 us
    pallas_call x1, Pallas kernels, body(): pl.pallas_call(functools.partial(assemble_kernel, move_dims), out_shape=j...  1.93 us
  transfers between devices with their start and end apart: 13, of which 5 were waited for; matrix products, arithmetic and copies ran while one was open for 2% of the time, Pallas kernels for 34%

profile of v5, /device:TPU:0, one launch (start us, length us, event | category | flops | bytes accessed | tf_op | source)
XLA Modules:
  0.0 40.8 jit_solution(2816833813279067973)
XLA Ops:
  0.6 1.1 %copy-done = bf16[5,36864]{1,0:T(8,128)(2,1)S(1)} copy-done((bf16[5,36864]{1,0:T(8,128)(2,1)S(1)}, bf16[5,36864]{1,0:T(8,128)(2,1)}, u32[]{:S(2)}) %copy-start) | copy-done | bytes 368664
  1.7 0.3 pack.1.own_ref.refs_0_
  2.0 3.0 %collective-permute-start = (bf16[120,1536]{1,0:T(8,128)(2,1)S(1)}, bf16[120,1536]{1,0:T(8,128)(2,1)S(1)}, u32[]{:S(2)}, u32[]{:S(2)}) collective-permute-start(bf16[120,1536]{1,0:T(8,128)(2,1)S(1)} %pack.1.own_ref.refs_0_), channel_id=1, source_target_pairs={{0,8},{4,12},{8,0},{12,4},{16,24},{20,28},{24,16},{28,20},{1,9},{5... | collective-permute-start | bytes 1105928 | tf_op jit(solution)/shard_map/ppermute | solution.py:398
  5.0 1.5 %collective-permute-start.1 = (bf16[120,1536]{1,0:T(8,128)(2,1)S(1)}, bf16[120,1536]{1,0:T(8,128)(2,1)S(1)}, u32[]{:S(2)}, u32[]{:S(2)}) collective-permute-start(bf16[120,1536]{1,0:T(8,128)(2,1)S(1)} %pack.1.own_ref.refs_0_), channel_id=1, source_target_pairs={{0,16},{4,20},{8,24},{12,28},{16,0},{20,4},{24,8},{28,12},{1,17},{... | collective-permute-start | bytes 1105928 | tf_op jit(solution)/shard_map/ppermute | solution.py:398
  6.5 0.7 %pad_add_fusion.table_ref = s32[5,4]{1,0:T(8,128)S(1)} fusion(s32[2,4]{1,0:T(2,128)} %bitcast.8, s32[2,4]{1,0:T(2,128)} %bitcast.9, s32[1,4]{1,0:T(1,128)} %bitcast.10), kind=kLoop, calls=%fused_computation | loop fusion | flops 40 | bytes 160 | tf_op jit(solution)/shard_map/concatenate | solution.py:410
  7.2 1.4 %leave.1 = (bf16[24,1536]{1,0:T(8,128)(2,1)S(1)}, bf16[24,1536]{1,0:T(8,128)(2,1)S(1)}, bf16[24,1536]{1,0:T(8,128)(2,1)S(1)}, s32[5]{0:T(128)S(1)}) custom-call(s32[1]{0:T(128)} %bitcast.ident_ref, s32[5,4]{1,0:T(8,128)S(1)} %pad_add_fusion.table_ref, bf16[120,1536]{1,0:T(8,128)(2,1)S(1)} %pack.1.own_ref.refs_0_), custom_call_target="tpu_custom_call" | custom-call | tf_op jit(solution)/shard_map/leave/pallas_call | solution.py:428
  8.6 1.6 %collective-permute-start.2 = (bf16[24,1536]{1,0:T(8,128)(2,1)S(1)}, bf16[24,1536]{1,0:T(8,128)(2,1)S(1)}, u32[]{:S(2)}, u32[]{:S(2)}) collective-permute-start(bf16[24,1536]{1,0:T(8,128)(2,1)S(1)} %get-tuple-element.19), channel_id=1, source_target_pairs={{0,1},{1,2},{2,3},{3,0},{4,5},{5,6},{6,7},{7,4},{8,9},{9,10},{10,1... | collective-permute-start | bytes 221192 | tf_op jit(solution)/shard_map/ppermute | solution.py:439
  10.3 2.6 %collective-permute-start.3 = (bf16[24,1536]{1,0:T(8,128)(2,1)S(1)}, bf16[24,1536]{1,0:T(8,128)(2,1)S(1)}, u32[]{:S(2)}, u32[]{:S(2)}) collective-permute-start(bf16[24,1536]{1,0:T(8,128)(2,1)S(1)} %get-tuple-element.20), channel_id=1, source_target_pairs={{0,2},{1,3},{2,0},{3,1},{4,6},{5,7},{6,4},{7,5},{8,10},{9,11},{10,... | collective-permute-start | bytes 221192 | tf_op jit(solution)/shard_map/ppermute | solution.py:439
  12.8 2.8 %order.1.weight_ref = bf16[1536,1536]{1,0:T(8,128)(2,1)S(1)} custom-call(s32[1]{0:T(128)} %bitcast.4.ident_ref, bf16[8,192,1536]{2,1,0:T(8,128)(2,1)} %chol_ref.1, bf16[120,1536]{1,0:T(8,128)(2,1)S(1)} %pack.1.own_ref.refs_0_), custom_call_target="tpu_custom_call" | custom-call | bytes 9437184 | tf_op jit(solution)/shard_map/order/pallas_call | solution.py:448
  15.6 1.5 %collective-permute-done.3.refs_1_ = bf16[24,1536]{1,0:T(8,128)(2,1)S(1)} collective-permute-done((bf16[24,1536]{1,0:T(8,128)(2,1)S(1)}, bf16[24,1536]{1,0:T(8,128)(2,1)S(1)}, u32[]{:S(2)}, u32[]{:S(2)}) %collective-permute-start.3) | collective-permute-done | bytes 73760 | tf_op jit(solution)/shard_map/ppermute | solution.py:439
  17.2 0.5 %collective-permute-start.9 = (bf16[120,1536]{1,0:T(8,128)(2,1)S(1)}, bf16[120,1536]{1,0:T(8,128)(2,1)S(1)}, u32[]{:S(2)}, u32[]{:S(2)}) collective-permute-start(bf16[120,1536]{1,0:T(8,128)(2,1)S(1)} %collective-permute-done.1.refs_4_), channel_id=1, source_target_pairs={{0,4},{4,0},{8,12},{12,8},{16,20},{20,16},{24,28},{28,24},{1,5},{5... | collective-permute-start | bytes 1105928 | tf_op jit(solution)/shard_map/ppermute | solution.py:398
  17.7 0.6 %collective-permute-start.5 = (bf16[120,768]{1,0:T(8,128)(2,1)S(1)}, bf16[120,768]{1,0:T(8,128)(2,1)S(1)}, u32[]{:S(2)}, u32[]{:S(2)}) collective-permute-start(bf16[120,768]{1,0:T(8,128)(2,1)S(1)} %slice.6), channel_id=1, source_target_pairs={{0,8},{4,12},{8,0},{12,4},{16,24},{20,28},{24,16},{28,20},{1,9},{5... | collective-permute-start | bytes 552968 | tf_op jit(solution)/shard_map/ppermute | solution.py:398
  18.3 0.5 %collective-permute-start.6 = (bf16[120,768]{1,0:T(8,128)(2,1)S(1)}, bf16[120,768]{1,0:T(8,128)(2,1)S(1)}, u32[]{:S(2)}, u32[]{:S(2)}) collective-permute-start(bf16[120,768]{1,0:T(8,128)(2,1)S(1)} %slice.7), channel_id=1, source_target_pairs={{0,16},{4,20},{8,24},{12,28},{16,0},{20,4},{24,8},{28,12},{1,17},{... | collective-permute-start | bytes 552968 | tf_op jit(solution)/shard_map/ppermute | solution.py:398
  18.8 0.5 %collective-permute-done.9.refs_5_ = bf16[120,1536]{1,0:T(8,128)(2,1)S(1)} collective-permute-done((bf16[120,1536]{1,0:T(8,128)(2,1)S(1)}, bf16[120,1536]{1,0:T(8,128)(2,1)S(1)}, u32[]{:S(2)}, u32[]{:S(2)}) %collective-permute-start.9) | collective-permute-done | bytes 368672 | tf_op jit(solution)/shard_map/ppermute | solution.py:398
  19.4 4.7 %near.1 = (f32[40,128]{1,0:T(8,128)S(1)}, f32[240,1536]{1,0:T(8,128)S(1)}) custom-call(s32[1]{0:T(128)} %bitcast.4.ident_ref, bf16[1536,1536]{1,0:T(8,128)(2,1)S(1)} %order.1.weight_ref, bf16[120,1536]{1,0:T(8,128)(2,1)S(1)} %pack.1.own_ref.refs_0_, bf16[120,1536]{1,0:T(8,128)(2,1)S(1)} %collective-permute-done.7.refs_1_, ...), custom_call_target="tpu_custom_call" | custom-call | flops 3397386240 | bytes 4718592 | tf_op jit(solution)/shard_map/near/pallas_call | solution.py:476
  24.1 0.3 collective-permute-done.5.refs_0_
  24.4 0.3 collective-permute-done.6.refs_1_
  24.6 0.5 %collective-permute-start.11 = (bf16[120,768]{1,0:T(8,128)(2,1)S(1)}, bf16[120,768]{1,0:T(8,128)(2,1)S(1)}, u32[]{:S(2)}, u32[]{:S(2)}) collective-permute-start(bf16[120,768]{1,0:T(8,128)(2,1)S(1)} %collective-permute-done.6.refs_1_), channel_id=1, source_target_pairs={{0,4},{4,0},{8,12},{12,8},{16,20},{20,16},{24,28},{28,24},{1,5},{5... | collective-permute-start | bytes 552968 | tf_op jit(solution)/shard_map/ppermute | solution.py:398
  25.2 1.5 %collective-permute-start.4 = (bf16[24,1536]{1,0:T(8,128)(2,1)S(1)}, bf16[24,1536]{1,0:T(8,128)(2,1)S(1)}, u32[]{:S(2)}, u32[]{:S(2)}) collective-permute-start(bf16[24,1536]{1,0:T(8,128)(2,1)S(1)} %get-tuple-element.23), channel_id=1, source_target_pairs={{0,3},{1,0},{2,1},{3,2},{4,7},{5,4},{6,5},{7,6},{8,11},{9,8},{10,9... | collective-permute-start | bytes 221192 | tf_op jit(solution)/shard_map/ppermute | solution.py:439
  26.7 3.0 %far.1 = f32[32,128]{1,0:T(8,128)} custom-call(s32[1]{0:T(128)} %bitcast.4.ident_ref, s32[5]{0:T(128)S(1)} %get-tuple-element.24.place_ref, bf16[1536,1536]{1,0:T(8,128)(2,1)S(1)} %order.1.weight_ref, f32[40,128]{1,0:T(8,128)S(1)} %get-tuple-element.29.near_sum_ref, f32[240,1536]{1,0:T(8,128)S(1)} %get-tuple-element.30.late_ref, ...), custom_call_target="tpu_custom_call" | custom-call | flops 1132462080 | bytes 4718592 | tf_op jit(solution)/shard_map/far/pallas_call | solution.py:494
  29.7 3.3 %all-to-all-start = ((f32[32,1,128]{2,1,0:T(1,128)}), f32[32,1,128]{2,1,0:T(1,128)S(1)}, u32[]{:S(2)}, u32[]{:S(2)}) async-start(f32[32,1,128]{2,1,0:T(1,128)} %bitcast.6), calls=%async_computation | async-start | bytes 32768 | tf_op jit(solution)/shard_map/all_to_all | solution.py:523
  33.0 1.9 %assemble.1 = bf16[3,36864]{1,0:T(4,128)(2,1)} custom-call(s32[1]{0:T(128)} %bitcast.ident_ref, s32[5,4]{1,0:T(8,128)S(1)} %pad_add_fusion.table_ref, bf16[5,36864]{1,0:T(8,128)(2,1)S(1)} %copy-done.1, bf16[24,1536]{1,0:T(8,128)(2,1)S(1)} %collective-permute-done.2.refs_0_, bf16[24,1536]{1,0:T(8,128)(2,1)S(1)} %collective-permute-done.3.refs_1_, ...), custom_call_target="tpu_custom_call" | custom-call | tf_op jit(solution)/shard_map/assemble/pallas_call | solution.py:508
  35.0 5.2 %all-to-all-done = f32[32,1,128]{2,1,0:T(1,128)S(1)} async-done(((f32[32,1,128]{2,1,0:T(1,128)}), f32[32,1,128]{2,1,0:T(1,128)S(1)}, u32[]{:S(2)}, u32[]{:S(2)}) %all-to-all-start) | async-done | bytes 16416 | tf_op jit(solution)/shard_map/all_to_all | solution.py:523
  40.2 0.6 %dynamic-slice_multiply_fusion = f32[3]{0:T(128)} fusion(f32[128]{0:T(128)S(1)} %reduce_sum.9, s32[]{:T(128)S(6)} %select_n.3), kind=kLoop, calls=%fused_computation.1 | loop fusion | flops 3 | bytes 28 | tf_op jit(solution)/shard_map/mul | solution.py:528
  (17 shorter events, 0.1 us)
Async XLA Ops:
  0.6 1.1 %copy-start = (bf16[5,36864]{1,0:T(8,128)(2,1)S(1)}, bf16[5,36864]{1,0:T(8,128)(2,1)}, u32[]{:S(2)}) copy-start(bf16[5,36864]{1,0:T(8,128)(2,1)} %green_ref.3) | copy-start | bytes 1105924
  2.0 15.2 %collective-permute-start = (bf16[120,1536]{1,0:T(8,128)(2,1)S(1)}, bf16[120,1536]{1,0:T(8,128)(2,1)S(1)}, u32[]{:S(2)}, u32[]{:S(2)}) collective-permute-start(bf16[120,1536]{1,0:T(8,128)(2,1)S(1)} %pack.1.own_ref.refs_0_), channel_id=1, source_target_pairs={{0,8},{4,12},{8,0},{12,4},{16,24},{20,28},{24,16},{28,20},{1,9},{5... | collective-permute-start | bytes 1105928 | tf_op jit(solution)/shard_map/ppermute | solution.py:398
  5.0 12.2 %collective-permute-start.1 = (bf16[120,1536]{1,0:T(8,128)(2,1)S(1)}, bf16[120,1536]{1,0:T(8,128)(2,1)S(1)}, u32[]{:S(2)}, u32[]{:S(2)}) collective-permute-start(bf16[120,1536]{1,0:T(8,128)(2,1)S(1)} %pack.1.own_ref.refs_0_), channel_id=1, source_target_pairs={{0,16},{4,20},{8,24},{12,28},{16,0},{20,4},{24,8},{28,12},{1,17},{... | collective-permute-start | bytes 1105928 | tf_op jit(solution)/shard_map/ppermute | solution.py:398
  8.6 7.0 %collective-permute-start.2 = (bf16[24,1536]{1,0:T(8,128)(2,1)S(1)}, bf16[24,1536]{1,0:T(8,128)(2,1)S(1)}, u32[]{:S(2)}, u32[]{:S(2)}) collective-permute-start(bf16[24,1536]{1,0:T(8,128)(2,1)S(1)} %get-tuple-element.19), channel_id=1, source_target_pairs={{0,1},{1,2},{2,3},{3,0},{4,5},{5,6},{6,7},{7,4},{8,9},{9,10},{10,1... | collective-permute-start | bytes 221192 | tf_op jit(solution)/shard_map/ppermute | solution.py:439
  10.3 6.9 %collective-permute-start.3 = (bf16[24,1536]{1,0:T(8,128)(2,1)S(1)}, bf16[24,1536]{1,0:T(8,128)(2,1)S(1)}, u32[]{:S(2)}, u32[]{:S(2)}) collective-permute-start(bf16[24,1536]{1,0:T(8,128)(2,1)S(1)} %get-tuple-element.20), channel_id=1, source_target_pairs={{0,2},{1,3},{2,0},{3,1},{4,6},{5,7},{6,4},{7,5},{8,10},{9,11},{10,... | collective-permute-start | bytes 221192 | tf_op jit(solution)/shard_map/ppermute | solution.py:439
  12.8 6.0 %collective-permute-start.7 = (bf16[120,1536]{1,0:T(8,128)(2,1)S(1)}, bf16[120,1536]{1,0:T(8,128)(2,1)S(1)}, u32[]{:S(2)}, u32[]{:S(2)}) collective-permute-start(bf16[120,1536]{1,0:T(8,128)(2,1)S(1)} %pack.1.own_ref.refs_0_), channel_id=1, source_target_pairs={{0,4},{4,0},{8,12},{12,8},{16,20},{20,16},{24,28},{28,24},{1,5},{5... | collective-permute-start | bytes 1105928 | tf_op jit(solution)/shard_map/ppermute | solution.py:398
  17.2 1.7 %collective-permute-start.8 = (bf16[120,1536]{1,0:T(8,128)(2,1)S(1)}, bf16[120,1536]{1,0:T(8,128)(2,1)S(1)}, u32[]{:S(2)}, u32[]{:S(2)}) collective-permute-start(bf16[120,1536]{1,0:T(8,128)(2,1)S(1)} %collective-permute-done.refs_2_), channel_id=1, source_target_pairs={{0,4},{4,0},{8,12},{12,8},{16,20},{20,16},{24,28},{28,24},{1,5},{5... | collective-permute-start | bytes 1105928 | tf_op jit(solution)/shard_map/ppermute | solution.py:398
  17.2 2.2 %collective-permute-start.9 = (bf16[120,1536]{1,0:T(8,128)(2,1)S(1)}, bf16[120,1536]{1,0:T(8,128)(2,1)S(1)}, u32[]{:S(2)}, u32[]{:S(2)}) collective-permute-start(bf16[120,1536]{1,0:T(8,128)(2,1)S(1)} %collective-permute-done.1.refs_4_), channel_id=1, source_target_pairs={{0,4},{4,0},{8,12},{12,8},{16,20},{20,16},{24,28},{28,24},{1,5},{5... | collective-permute-start | bytes 1105928 | tf_op jit(solution)/shard_map/ppermute | solution.py:398
  17.7 6.7 %collective-permute-start.5 = (bf16[120,768]{1,0:T(8,128)(2,1)S(1)}, bf16[120,768]{1,0:T(8,128)(2,1)S(1)}, u32[]{:S(2)}, u32[]{:S(2)}) collective-permute-start(bf16[120,768]{1,0:T(8,128)(2,1)S(1)} %slice.6), channel_id=1, source_target_pairs={{0,8},{4,12},{8,0},{12,4},{16,24},{20,28},{24,16},{28,20},{1,9},{5... | collective-permute-start | bytes 552968 | tf_op jit(solution)/shard_map/ppermute | solution.py:398
  18.3 6.3 %collective-permute-start.6 = (bf16[120,768]{1,0:T(8,128)(2,1)S(1)}, bf16[120,768]{1,0:T(8,128)(2,1)S(1)}, u32[]{:S(2)}, u32[]{:S(2)}) collective-permute-start(bf16[120,768]{1,0:T(8,128)(2,1)S(1)} %slice.7), channel_id=1, source_target_pairs={{0,16},{4,20},{8,24},{12,28},{16,0},{20,4},{24,8},{28,12},{1,17},{... | collective-permute-start | bytes 552968 | tf_op jit(solution)/shard_map/ppermute | solution.py:398
  24.1 8.9 %copy-start.1 = (bf16[5,36864]{1,0:T(8,128)(2,1)S(1)}, bf16[5,36864]{1,0:T(8,128)(2,1)}, u32[]{:S(2)}) copy-start(bf16[5,36864]{1,0:T(8,128)(2,1)} %green_ref.3) | copy-start | bytes 1105924
  24.6 2.0 %collective-permute-start.10 = (bf16[120,768]{1,0:T(8,128)(2,1)S(1)}, bf16[120,768]{1,0:T(8,128)(2,1)S(1)}, u32[]{:S(2)}, u32[]{:S(2)}) collective-permute-start(bf16[120,768]{1,0:T(8,128)(2,1)S(1)} %collective-permute-done.5.refs_0_), channel_id=1, source_target_pairs={{0,4},{4,0},{8,12},{12,8},{16,20},{20,16},{24,28},{28,24},{1,5},{5... | collective-permute-start | bytes 552968 | tf_op jit(solution)/shard_map/ppermute | solution.py:398
  24.6 2.0 %collective-permute-start.11 = (bf16[120,768]{1,0:T(8,128)(2,1)S(1)}, bf16[120,768]{1,0:T(8,128)(2,1)S(1)}, u32[]{:S(2)}, u32[]{:S(2)}) collective-permute-start(bf16[120,768]{1,0:T(8,128)(2,1)S(1)} %collective-permute-done.6.refs_1_), channel_id=1, source_target_pairs={{0,4},{4,0},{8,12},{12,8},{16,20},{20,16},{24,28},{28,24},{1,5},{5... | collective-permute-start | bytes 552968 | tf_op jit(solution)/shard_map/ppermute | solution.py:398
  25.2 7.9 %collective-permute-start.4 = (bf16[24,1536]{1,0:T(8,128)(2,1)S(1)}, bf16[24,1536]{1,0:T(8,128)(2,1)S(1)}, u32[]{:S(2)}, u32[]{:S(2)}) collective-permute-start(bf16[24,1536]{1,0:T(8,128)(2,1)S(1)} %get-tuple-element.23), channel_id=1, source_target_pairs={{0,3},{1,0},{2,1},{3,2},{4,7},{5,4},{6,5},{7,6},{8,11},{9,8},{10,9... | collective-permute-start | bytes 221192 | tf_op jit(solution)/shard_map/ppermute | solution.py:439
  29.7 10.5 %all-to-all-start = ((f32[32,1,128]{2,1,0:T(1,128)}), f32[32,1,128]{2,1,0:T(1,128)S(1)}, u32[]{:S(2)}, u32[]{:S(2)}) async-start(f32[32,1,128]{2,1,0:T(1,128)} %bitcast.6), calls=%async_computation | async-start | bytes 32768 | tf_op jit(solution)/shard_map/all_to_all | solution.py:523

commit v6 on v5

--- a/solution.py
+++ b/solution.py
@@ -143,7 +143,7 @@
 
 def leave_kernel(dims, ident_ref, table_ref, own_ref, *refs):
     slots, share_rows, orb_count, walkers, moves, keep = dims
-    leave_refs, place_ref, wide = refs[:-2], refs[-2], refs[-1]
+    leave_refs, wide = refs[:-1], refs[-1]
     table = Moves(table_ref, moves)
     wide[...] = own_ref[...].astype(jnp.float32)
     own = ident_ref[0]
@@ -155,24 +155,6 @@
             chosen = jnp.where(hit, table.slot(own, move), chosen)
         start = pl.multiple_of(chosen * share_rows, ROWS)
         leave_refs[shift - 1][...] = wide[pl.ds(start, share_rows), :].astype(jnp.bfloat16)
-    rank = jnp.int32(0)
-    for slot in range(slots):
-        live = slot < table.count(own)
-        gone_to = table.goes_to(own, slot)
-        stays = live & (gone_to < 0)
-        there = jnp.maximum(gone_to, 0)
-        ahead = table.staying(there)
-        for device in range(walkers):
-            for move in range(moves):
-                hit = (
-                    (device < own)
-                    & (table.dest(device, move) == there)
-                    & (table.slot(device, move) >= 0)
-                )
-                ahead = ahead + jnp.where(hit, 1, 0)
-        place = jnp.where(stays, own * keep + rank, there * keep + ahead)
-        place_ref[slot] = jnp.where(live, place, -1)
-        rank = rank + jnp.where(stays, 1, 0)
 
 
 def assemble_kernel(dims, ident_ref, table_ref, green_ref, *refs):
@@ -224,9 +206,33 @@
             ].astype(jnp.bfloat16)
 
 
-def order_kernel(dims, ident_ref, chol_ref, own_ref, out_ref, sems):
-    del own_ref
-    group, groups, chip_rows = dims
+def find_places(dims, own, table, place_ref):
+    slots, walkers, moves, keep = dims
+    rank = jnp.int32(0)
+    for slot in range(slots):
+        live = slot < table.count(own)
+        gone_to = table.goes_to(own, slot)
+        stays = live & (gone_to < 0)
+        there = jnp.maximum(gone_to, 0)
+        ahead = table.staying(there)
+        for device in range(walkers):
+            for move in range(moves):
+                hit = (
+                    (device < own)
+                    & (table.dest(device, move) == there)
+                    & (table.slot(device, move) >= 0)
+                )
+                ahead = ahead + jnp.where(hit, 1, 0)
+        place = jnp.where(stays, own * keep + rank, there * keep + ahead)
+        place_ref[slot] = jnp.where(live, place, -1)
+        rank = rank + jnp.where(stays, 1, 0)
+
+
+def order_kernel(
+    dims, ident_ref, walker_ref, table_ref, chol_ref, core_ref, out_ref, place_ref, sems
+):
+    del core_ref
+    group, groups, chip_rows, place_dims = dims
     chip = ident_ref[0] // 2
     edge = LANES - 2 * chip_rows
     rest = 2 * chip_rows - edge
@@ -254,6 +260,7 @@
             add(vec, 3, 0, chip_rows, place + chip_rows - edge)
     for copy in copies:
         copy.start()
+    find_places(place_dims, walker_ref[0], Moves(table_ref, place_dims[2]), place_ref)
     for copy in copies:
         copy.wait()
 
@@ -425,12 +432,11 @@
         name="pack",
     )(green)
     move_dims = (slots, share_rows, orb_count, walkers, moves, keep)
-    *leaving, place = pl.pallas_call(
+    leaving = pl.pallas_call(
         functools.partial(leave_kernel, move_dims),
-        out_shape=[jax.ShapeDtypeStruct((share_rows, orb_count), jnp.bfloat16)] * (walkers - 1)
-        + [jax.ShapeDtypeStruct((slots,), jnp.int32)],
+        out_shape=[jax.ShapeDtypeStruct((share_rows, orb_count), jnp.bfloat16)] * (walkers - 1),
         in_specs=[smem, smem, vmem],
-        out_specs=[vmem] * (walkers - 1) + [smem],
+        out_specs=[vmem] * (walkers - 1),
         scratch_shapes=[pltpu.VMEM((pack_rows, orb_count), jnp.float32)],
         compiler_params=limit,
         name="leave",
@@ -445,23 +451,27 @@
     group = 4
     groups = vectors // group
     chip_rows = 2 * share_rows
-    weights = pl.pallas_call(
-        functools.partial(order_kernel, (group, groups, chip_rows)),
-        out_shape=jax.ShapeDtypeStruct((vectors * occ_count, orb_count), jnp.bfloat16),
-        in_specs=[smem] + [pl.BlockSpec(memory_space=pl.ANY)] * 2,
-        out_specs=vmem,
+    core, near_x, near_y = 1, 2, 4
+    from_x = swap(own_rows, near_x, blocks)
+    from_y = swap(own_rows, near_y, blocks)
+    from_core = swap(own_rows, core, blocks)
+    weights, place = pl.pallas_call(
+        functools.partial(
+            order_kernel, (group, groups, chip_rows, (slots, walkers, moves, keep))
+        ),
+        out_shape=[
+            jax.ShapeDtypeStruct((vectors * occ_count, orb_count), jnp.bfloat16),
+            jax.ShapeDtypeStruct((slots,), jnp.int32),
+        ],
+        in_specs=[smem] * 3 + [pl.BlockSpec(memory_space=pl.ANY)] * 2,
+        out_specs=[vmem, smem],
         scratch_shapes=[pltpu.SemaphoreType.DMA((5 * vectors,))],
         compiler_params=pltpu.CompilerParams(vmem_limit_bytes=48 * 1024 * 1024),
         cost_estimate=pl.CostEstimate(
             flops=0, bytes_accessed=4 * chol.size, transcendentals=0
         ),
         name="order",
-    )(block_index, chol, own_rows)
-
-    core, near_x, near_y = 1, 2, 4
-    from_x = swap(own_rows, near_x, blocks)
-    from_y = swap(own_rows, near_y, blocks)
-    from_core = swap(own_rows, core, blocks)
+    )(block_index, walker_index, table, chol, own_rows)
     width = orb_count // 2
     from_x, from_y, weights, coming[:2] = lax.optimization_barrier(
         (from_x, from_y, weights, coming[:2])

time: 41 us -> 41 us (level)
  waiting for transfers between devices: 7.85 us -> 6.86 us
  Pallas kernels: 14.1 us -> 14.6 us
  starting transfers between devices: 15.7 us -> 16.2 us
    ppermute x3, waiting for transfers between devices: 1.53 us -> 0.33 us  [body(): lax.ppermute(leaving[shift - 1], 'walker', [(z, (z + shift) % walkers) fo...]
    pallas_call x1, Pallas kernels: 2.76 us -> 3.96 us  [body(): pl.pallas_call(functools.partial(order_kernel, (group, groups, chip_rows,...]
    pallas_call x1, Pallas kernels: 1.4 us -> 0.67 us  [body(): pl.pallas_call(functools.partial(leave_kernel, move_dims), out_shape=[jax...]
    ppermute x3, starting transfers between devices: 5.72 us -> 6.24 us  [body(): lax.ppermute(leaving[shift - 1], 'walker', [(z, (z + shift) % walkers) fo...]
  transfers between devices with their start and end apart: 13 -> 13, of which waited for: 5 -> 5; matrix products, arithmetic and copies ran while one was open for 2% -> 2% of each run, Pallas kernels for 34% -> 35%
where the time goes in v6:
time: 41 us; the launch traced here: 40.8 us
  starting transfers between devices  16.2 us (40%)
  Pallas kernels  14.6 us (36%)
  waiting for transfers between devices  6.86 us (17%)
  other arithmetic  1.34 us (3%)
  local copies, waits for them, and re-layouts  1.09 us (3%)
  between operations  0.73 us (2%)
    ppermute x9, starting transfers between devices, swap(): lax.ppermute(value, 'block', [(index, index ^ mask) for index in range(bl...  6.65 us
    ppermute x3, starting transfers between devices, body(): lax.ppermute(leaving[shift - 1], 'walker', [(z, (z + shift) % walkers) fo...  6.24 us
    all_to_all x1, waiting for transfers between devices, body(): lax.all_to_all(all_sums, ('block', 'walker'), split_axis=0, concat_axis=0...  5.22 us
    pallas_call x1, Pallas kernels, body(): pl.pallas_call(functools.partial(near_kernel, dims), out_shape=[jax.Shape...  4.71 us
    pallas_call x1, Pallas kernels, body(): pl.pallas_call(functools.partial(order_kernel, (group, groups, chip_rows,...  3.96 us
    all_to_all x1, starting transfers between devices, body(): lax.all_to_all(all_sums, ('block', 'walker'), split_axis=0, concat_axis=0...  3.33 us
    pallas_call x1, Pallas kernels, body(): pl.pallas_call(functools.partial(far_kernel, dims), out_shape=jax.ShapeDt...  3.01 us
    pallas_call x1, Pallas kernels, body(): pl.pallas_call(functools.partial(assemble_kernel, move_dims), out_shape=j...  1.93 us
  transfers between devices with their start and end apart: 13, of which 5 were waited for; matrix products, arithmetic and copies ran while one was open for 2% of the time, Pallas kernels for 35%

profile of v6, /device:TPU:0, one launch (start us, length us, event | category | flops | bytes accessed | tf_op | source)
XLA Modules:
  0.0 40.8 jit_solution(15644397178719729133)
XLA Ops:
  0.6 1.1 %copy-done = bf16[5,36864]{1,0:T(8,128)(2,1)S(1)} copy-done((bf16[5,36864]{1,0:T(8,128)(2,1)S(1)}, bf16[5,36864]{1,0:T(8,128)(2,1)}, u32[]{:S(2)}) %copy-start) | copy-done | bytes 368664
  1.7 0.3 pack.1.core_ref.own_ref.refs_0_
  2.0 3.0 %collective-permute-start = (bf16[120,1536]{1,0:T(8,128)(2,1)S(1)}, bf16[120,1536]{1,0:T(8,128)(2,1)S(1)}, u32[]{:S(2)}, u32[]{:S(2)}) collective-permute-start(bf16[120,1536]{1,0:T(8,128)(2,1)S(1)} %pack.1.core_ref.own_ref.refs_0_), channel_id=1, source_target_pairs={{0,8},{4,12},{8,0},{12,4},{16,24},{20,28},{24,16},{28,20},{1,9},{5... | collective-permute-start | bytes 1105928 | tf_op jit(solution)/shard_map/ppermute | solution.py:405
  5.0 1.5 %collective-permute-start.1 = (bf16[120,1536]{1,0:T(8,128)(2,1)S(1)}, bf16[120,1536]{1,0:T(8,128)(2,1)S(1)}, u32[]{:S(2)}, u32[]{:S(2)}) collective-permute-start(bf16[120,1536]{1,0:T(8,128)(2,1)S(1)} %pack.1.core_ref.own_ref.refs_0_), channel_id=1, source_target_pairs={{0,16},{4,20},{8,24},{12,28},{16,0},{20,4},{24,8},{28,12},{1,17},{... | collective-permute-start | bytes 1105928 | tf_op jit(solution)/shard_map/ppermute | solution.py:405
  6.5 0.7 %pad_add_fusion.table_ref = s32[5,4]{1,0:T(8,128)S(1)} fusion(s32[2,4]{1,0:T(2,128)} %bitcast.8, s32[2,4]{1,0:T(2,128)} %bitcast.9, s32[1,4]{1,0:T(1,128)} %bitcast.10), kind=kLoop, calls=%fused_computation | loop fusion | flops 40 | bytes 160 | tf_op jit(solution)/shard_map/concatenate | solution.py:417
  7.2 0.7 %leave.1 = (bf16[24,1536]{1,0:T(8,128)(2,1)S(1)}, bf16[24,1536]{1,0:T(8,128)(2,1)S(1)}, bf16[24,1536]{1,0:T(8,128)(2,1)S(1)}) custom-call(s32[1]{0:T(128)} %bitcast.walker_ref.ident_ref, s32[5,4]{1,0:T(8,128)S(1)} %pad_add_fusion.table_ref, bf16[120,1536]{1,0:T(8,128)(2,1)S(1)} %pack.1.core_ref.own_ref.refs_0_), custom_call_target="tpu_custom_call" | custom-call | tf_op jit(solution)/shard_map/leave/pallas_call | solution.py:435
  7.9 1.6 %collective-permute-start.2 = (bf16[24,1536]{1,0:T(8,128)(2,1)S(1)}, bf16[24,1536]{1,0:T(8,128)(2,1)S(1)}, u32[]{:S(2)}, u32[]{:S(2)}) collective-permute-start(bf16[24,1536]{1,0:T(8,128)(2,1)S(1)} %get-tuple-element.21), channel_id=1, source_target_pairs={{0,1},{1,2},{2,3},{3,0},{4,5},{5,6},{6,7},{7,4},{8,9},{9,10},{10,1... | collective-permute-start | bytes 221192 | tf_op jit(solution)/shard_map/ppermute | solution.py:445
  9.5 2.6 %collective-permute-start.3 = (bf16[24,1536]{1,0:T(8,128)(2,1)S(1)}, bf16[24,1536]{1,0:T(8,128)(2,1)S(1)}, u32[]{:S(2)}, u32[]{:S(2)}) collective-permute-start(bf16[24,1536]{1,0:T(8,128)(2,1)S(1)} %get-tuple-element.22), channel_id=1, source_target_pairs={{0,2},{1,3},{2,0},{3,1},{4,6},{5,7},{6,4},{7,5},{8,10},{9,11},{10,... | collective-permute-start | bytes 221192 | tf_op jit(solution)/shard_map/ppermute | solution.py:445
  12.1 4.0 %order.1 = (bf16[1536,1536]{1,0:T(8,128)(2,1)S(1)}, s32[5]{0:T(128)S(1)}) custom-call(s32[1]{0:T(128)} %bitcast.4.ident_ref, s32[1]{0:T(128)} %bitcast.walker_ref.ident_ref, s32[5,4]{1,0:T(8,128)S(1)} %pad_add_fusion.table_ref, bf16[8,192,1536]{2,1,0:T(8,128)(2,1)} %chol_ref.1, bf16[120,1536]{1,0:T(8,128)(2,1)S(1)} %pack.1.core_ref.own_ref.refs_0_), custom_call_target="tpu_custom_call" | custom-call | bytes 9437184 | tf_op jit(solution)/shard_map/order/pallas_call | solution.py:458
  16.1 0.3 collective-permute-done.3.refs_1_
  16.4 0.3 collective-permute-start.8
  17.0 0.6 %collective-permute-start.5 = (bf16[120,768]{1,0:T(8,128)(2,1)S(1)}, bf16[120,768]{1,0:T(8,128)(2,1)S(1)}, u32[]{:S(2)}, u32[]{:S(2)}) collective-permute-start(bf16[120,768]{1,0:T(8,128)(2,1)S(1)} %slice.6), channel_id=1, source_target_pairs={{0,8},{4,12},{8,0},{12,4},{16,24},{20,28},{24,16},{28,20},{1,9},{5... | collective-permute-start | bytes 552968 | tf_op jit(solution)/shard_map/ppermute | solution.py:405
  17.6 0.5 %collective-permute-start.6 = (bf16[120,768]{1,0:T(8,128)(2,1)S(1)}, bf16[120,768]{1,0:T(8,128)(2,1)S(1)}, u32[]{:S(2)}, u32[]{:S(2)}) collective-permute-start(bf16[120,768]{1,0:T(8,128)(2,1)S(1)} %slice.7), channel_id=1, source_target_pairs={{0,16},{4,20},{8,24},{12,28},{16,0},{20,4},{24,8},{28,12},{1,17},{... | collective-permute-start | bytes 552968 | tf_op jit(solution)/shard_map/ppermute | solution.py:405
  18.1 0.5 %collective-permute-done.9.refs_5_ = bf16[120,1536]{1,0:T(8,128)(2,1)S(1)} collective-permute-done((bf16[120,1536]{1,0:T(8,128)(2,1)S(1)}, bf16[120,1536]{1,0:T(8,128)(2,1)S(1)}, u32[]{:S(2)}, u32[]{:S(2)}) %collective-permute-start.9) | collective-permute-done | bytes 368672 | tf_op jit(solution)/shard_map/ppermute | solution.py:405
  18.6 4.7 %near.1 = (f32[40,128]{1,0:T(8,128)S(1)}, f32[240,1536]{1,0:T(8,128)S(1)}) custom-call(s32[1]{0:T(128)} %bitcast.4.ident_ref, bf16[1536,1536]{1,0:T(8,128)(2,1)S(1)} %get-tuple-element.27.weight_ref, bf16[120,1536]{1,0:T(8,128)(2,1)S(1)} %pack.1.core_ref.own_ref.refs_0_, bf16[120,1536]{1,0:T(8,128)(2,1)S(1)} %collective-permute-done.7.refs_1_, ...), custom_call_target="tpu_custom_call" | custom-call | flops 3397386240 | bytes 4718592 | tf_op jit(solution)/shard_map/near/pallas_call | solution.py:486
  23.4 0.5 %collective-permute-done.5.refs_0_ = bf16[120,768]{1,0:T(8,128)(2,1)S(1)} collective-permute-done((bf16[120,768]{1,0:T(8,128)(2,1)S(1)}, bf16[120,768]{1,0:T(8,128)(2,1)S(1)}, u32[]{:S(2)}, u32[]{:S(2)}) %collective-permute-start.5) | collective-permute-done | bytes 184352 | tf_op jit(solution)/shard_map/ppermute | solution.py:405
  23.9 0.3 collective-permute-done.6.refs_1_
  24.1 0.5 %collective-permute-start.11 = (bf16[120,768]{1,0:T(8,128)(2,1)S(1)}, bf16[120,768]{1,0:T(8,128)(2,1)S(1)}, u32[]{:S(2)}, u32[]{:S(2)}) collective-permute-start(bf16[120,768]{1,0:T(8,128)(2,1)S(1)} %collective-permute-done.6.refs_1_), channel_id=1, source_target_pairs={{0,4},{4,0},{8,12},{12,8},{16,20},{20,16},{24,28},{28,24},{1,5},{5... | collective-permute-start | bytes 552968 | tf_op jit(solution)/shard_map/ppermute | solution.py:405
  24.6 2.0 %collective-permute-start.4 = (bf16[24,1536]{1,0:T(8,128)(2,1)S(1)}, bf16[24,1536]{1,0:T(8,128)(2,1)S(1)}, u32[]{:S(2)}, u32[]{:S(2)}) collective-permute-start(bf16[24,1536]{1,0:T(8,128)(2,1)S(1)} %get-tuple-element.25), channel_id=1, source_target_pairs={{0,3},{1,0},{2,1},{3,2},{4,7},{5,4},{6,5},{7,6},{8,11},{9,8},{10,9... | collective-permute-start | bytes 221192 | tf_op jit(solution)/shard_map/ppermute | solution.py:445
  26.7 3.0 %far.1 = f32[32,128]{1,0:T(8,128)} custom-call(s32[1]{0:T(128)} %bitcast.4.ident_ref, s32[5]{0:T(128)S(1)} %get-tuple-element.26.place_ref, bf16[1536,1536]{1,0:T(8,128)(2,1)S(1)} %get-tuple-element.27.weight_ref, f32[40,128]{1,0:T(8,128)S(1)} %get-tuple-element.31.near_sum_ref, f32[240,1536]{1,0:T(8,128)S(1)} %get-tuple-element.32.late_ref, ...), custom_call_target="tpu_custom_call" | custom-call | flops 1132462080 | bytes 4718592 | tf_op jit(solution)/shard_map/far/pallas_call | solution.py:504
  29.7 3.3 %all-to-all-start = ((f32[32,1,128]{2,1,0:T(1,128)}), f32[32,1,128]{2,1,0:T(1,128)S(1)}, u32[]{:S(2)}, u32[]{:S(2)}) async-start(f32[32,1,128]{2,1,0:T(1,128)} %bitcast.6), calls=%async_computation | async-start | bytes 32768 | tf_op jit(solution)/shard_map/all_to_all | solution.py:533
  33.0 1.9 %assemble.1 = bf16[3,36864]{1,0:T(4,128)(2,1)} custom-call(s32[1]{0:T(128)} %bitcast.walker_ref.ident_ref, s32[5,4]{1,0:T(8,128)S(1)} %pad_add_fusion.table_ref, bf16[5,36864]{1,0:T(8,128)(2,1)S(1)} %copy-done.1, bf16[24,1536]{1,0:T(8,128)(2,1)S(1)} %collective-permute-done.2.refs_0_, bf16[24,1536]{1,0:T(8,128)(2,1)S(1)} %collective-permute-done.3.refs_1_, ...), custom_call_target="tpu_custom_call" | custom-call | tf_op jit(solution)/shard_map/assemble/pallas_call | solution.py:518
  35.0 5.2 %all-to-all-done = f32[32,1,128]{2,1,0:T(1,128)S(1)} async-done(((f32[32,1,128]{2,1,0:T(1,128)}), f32[32,1,128]{2,1,0:T(1,128)S(1)}, u32[]{:S(2)}, u32[]{:S(2)}) %all-to-all-start) | async-done | bytes 16416 | tf_op jit(solution)/shard_map/all_to_all | solution.py:533
  40.2 0.6 %dynamic-slice_multiply_fusion = f32[3]{0:T(128)} fusion(f32[128]{0:T(128)S(1)} %reduce_sum.9, s32[]{:T(128)S(6)} %select_n.3), kind=kLoop, calls=%fused_computation.1 | loop fusion | flops 3 | bytes 28 | tf_op jit(solution)/shard_map/mul | solution.py:538
  (17 shorter events, 0.4 us)
Async XLA Ops:
  0.6 1.1 %copy-start = (bf16[5,36864]{1,0:T(8,128)(2,1)S(1)}, bf16[5,36864]{1,0:T(8,128)(2,1)}, u32[]{:S(2)}) copy-start(bf16[5,36864]{1,0:T(8,128)(2,1)} %green_ref.3) | copy-start | bytes 1105924
  2.0 14.4 %collective-permute-start = (bf16[120,1536]{1,0:T(8,128)(2,1)S(1)}, bf16[120,1536]{1,0:T(8,128)(2,1)S(1)}, u32[]{:S(2)}, u32[]{:S(2)}) collective-permute-start(bf16[120,1536]{1,0:T(8,128)(2,1)S(1)} %pack.1.core_ref.own_ref.refs_0_), channel_id=1, source_target_pairs={{0,8},{4,12},{8,0},{12,4},{16,24},{20,28},{24,16},{28,20},{1,9},{5... | collective-permute-start | bytes 1105928 | tf_op jit(solution)/shard_map/ppermute | solution.py:405
  5.0 11.4 %collective-permute-start.1 = (bf16[120,1536]{1,0:T(8,128)(2,1)S(1)}, bf16[120,1536]{1,0:T(8,128)(2,1)S(1)}, u32[]{:S(2)}, u32[]{:S(2)}) collective-permute-start(bf16[120,1536]{1,0:T(8,128)(2,1)S(1)} %pack.1.core_ref.own_ref.refs_0_), channel_id=1, source_target_pairs={{0,16},{4,20},{8,24},{12,28},{16,0},{20,4},{24,8},{28,12},{1,17},{... | collective-permute-start | bytes 1105928 | tf_op jit(solution)/shard_map/ppermute | solution.py:405
  7.9 8.2 %collective-permute-start.2 = (bf16[24,1536]{1,0:T(8,128)(2,1)S(1)}, bf16[24,1536]{1,0:T(8,128)(2,1)S(1)}, u32[]{:S(2)}, u32[]{:S(2)}) collective-permute-start(bf16[24,1536]{1,0:T(8,128)(2,1)S(1)} %get-tuple-element.21), channel_id=1, source_target_pairs={{0,1},{1,2},{2,3},{3,0},{4,5},{5,6},{6,7},{7,4},{8,9},{9,10},{10,1... | collective-permute-start | bytes 221192 | tf_op jit(solution)/shard_map/ppermute | solution.py:445
  9.5 6.9 %collective-permute-start.3 = (bf16[24,1536]{1,0:T(8,128)(2,1)S(1)}, bf16[24,1536]{1,0:T(8,128)(2,1)S(1)}, u32[]{:S(2)}, u32[]{:S(2)}) collective-permute-start(bf16[24,1536]{1,0:T(8,128)(2,1)S(1)} %get-tuple-element.22), channel_id=1, source_target_pairs={{0,2},{1,3},{2,0},{3,1},{4,6},{5,7},{6,4},{7,5},{8,10},{9,11},{10,... | collective-permute-start | bytes 221192 | tf_op jit(solution)/shard_map/ppermute | solution.py:445
  12.1 6.0 %collective-permute-start.7 = (bf16[120,1536]{1,0:T(8,128)(2,1)S(1)}, bf16[120,1536]{1,0:T(8,128)(2,1)S(1)}, u32[]{:S(2)}, u32[]{:S(2)}) collective-permute-start(bf16[120,1536]{1,0:T(8,128)(2,1)S(1)} %pack.1.core_ref.own_ref.refs_0_), channel_id=1, source_target_pairs={{0,4},{4,0},{8,12},{12,8},{16,20},{20,16},{24,28},{28,24},{1,5},{5... | collective-permute-start | bytes 1105928 | tf_op jit(solution)/shard_map/ppermute | solution.py:405
  16.4 1.7 %collective-permute-start.8 = (bf16[120,1536]{1,0:T(8,128)(2,1)S(1)}, bf16[120,1536]{1,0:T(8,128)(2,1)S(1)}, u32[]{:S(2)}, u32[]{:S(2)}) collective-permute-start(bf16[120,1536]{1,0:T(8,128)(2,1)S(1)} %collective-permute-done.refs_2_), channel_id=1, source_target_pairs={{0,4},{4,0},{8,12},{12,8},{16,20},{20,16},{24,28},{28,24},{1,5},{5... | collective-permute-start | bytes 1105928 | tf_op jit(solution)/shard_map/ppermute | solution.py:405
  16.7 1.9 %collective-permute-start.9 = (bf16[120,1536]{1,0:T(8,128)(2,1)S(1)}, bf16[120,1536]{1,0:T(8,128)(2,1)S(1)}, u32[]{:S(2)}, u32[]{:S(2)}) collective-permute-start(bf16[120,1536]{1,0:T(8,128)(2,1)S(1)} %collective-permute-done.1.refs_4_), channel_id=1, source_target_pairs={{0,4},{4,0},{8,12},{12,8},{16,20},{20,16},{24,28},{28,24},{1,5},{5... | collective-permute-start | bytes 1105928 | tf_op jit(solution)/shard_map/ppermute | solution.py:405
  17.0 6.9 %collective-permute-start.5 = (bf16[120,768]{1,0:T(8,128)(2,1)S(1)}, bf16[120,768]{1,0:T(8,128)(2,1)S(1)}, u32[]{:S(2)}, u32[]{:S(2)}) collective-permute-start(bf16[120,768]{1,0:T(8,128)(2,1)S(1)} %slice.6), channel_id=1, source_target_pairs={{0,8},{4,12},{8,0},{12,4},{16,24},{20,28},{24,16},{28,20},{1,9},{5... | collective-permute-start | bytes 552968 | tf_op jit(solution)/shard_map/ppermute | solution.py:405
  17.6 6.5 %collective-permute-start.6 = (bf16[120,768]{1,0:T(8,128)(2,1)S(1)}, bf16[120,768]{1,0:T(8,128)(2,1)S(1)}, u32[]{:S(2)}, u32[]{:S(2)}) collective-permute-start(bf16[120,768]{1,0:T(8,128)(2,1)S(1)} %slice.7), channel_id=1, source_target_pairs={{0,16},{4,20},{8,24},{12,28},{16,0},{20,4},{24,8},{28,12},{1,17},{... | collective-permute-start | bytes 552968 | tf_op jit(solution)/shard_map/ppermute | solution.py:405
  23.4 9.7 %copy-start.1 = (bf16[5,36864]{1,0:T(8,128)(2,1)S(1)}, bf16[5,36864]{1,0:T(8,128)(2,1)}, u32[]{:S(2)}) copy-start(bf16[5,36864]{1,0:T(8,128)(2,1)} %green_ref.3) | copy-start | bytes 1105924
  24.1 2.5 %collective-permute-start.10 = (bf16[120,768]{1,0:T(8,128)(2,1)S(1)}, bf16[120,768]{1,0:T(8,128)(2,1)S(1)}, u32[]{:S(2)}, u32[]{:S(2)}) collective-permute-start(bf16[120,768]{1,0:T(8,128)(2,1)S(1)} %collective-permute-done.5.refs_0_), channel_id=1, source_target_pairs={{0,4},{4,0},{8,12},{12,8},{16,20},{20,16},{24,28},{28,24},{1,5},{5... | collective-permute-start | bytes 552968 | tf_op jit(solution)/shard_map/ppermute | solution.py:405
  24.1 2.5 %collective-permute-start.11 = (bf16[120,768]{1,0:T(8,128)(2,1)S(1)}, bf16[120,768]{1,0:T(8,128)(2,1)S(1)}, u32[]{:S(2)}, u32[]{:S(2)}) collective-permute-start(bf16[120,768]{1,0:T(8,128)(2,1)S(1)} %collective-permute-done.6.refs_1_), channel_id=1, source_target_pairs={{0,4},{4,0},{8,12},{12,8},{16,20},{20,16},{24,28},{28,24},{1,5},{5... | collective-permute-start | bytes 552968 | tf_op jit(solution)/shard_map/ppermute | solution.py:405
  24.6 8.4 %collective-permute-start.4 = (bf16[24,1536]{1,0:T(8,128)(2,1)S(1)}, bf16[24,1536]{1,0:T(8,128)(2,1)S(1)}, u32[]{:S(2)}, u32[]{:S(2)}) collective-permute-start(bf16[24,1536]{1,0:T(8,128)(2,1)S(1)} %get-tuple-element.25), channel_id=1, source_target_pairs={{0,3},{1,0},{2,1},{3,2},{4,7},{5,4},{6,5},{7,6},{8,11},{9,8},{10,9... | collective-permute-start | bytes 221192 | tf_op jit(solution)/shard_map/ppermute | solution.py:445
  29.7 10.5 %all-to-all-start = ((f32[32,1,128]{2,1,0:T(1,128)}), f32[32,1,128]{2,1,0:T(1,128)S(1)}, u32[]{:S(2)}, u32[]{:S(2)}) async-start(f32[32,1,128]{2,1,0:T(1,128)} %bitcast.6), calls=%async_computation | async-start | bytes 32768 | tf_op jit(solution)/shard_map/all_to_all | solution.py:533

commit v7 on v6

--- a/solution.py
+++ b/solution.py
@@ -287,9 +287,10 @@
 
 def near_kernel(dims, ident_ref, weight_ref, *refs):
     slots, share_rows, group, groups, chip_rows = dims
-    piece_refs = refs[:6]
-    sum_ref, late_ref = refs[6:8]
-    trans_refs = refs[8:]
+    own_ref, core_ref, x_ref, y_ref, turned_ref = refs[:5]
+    piece_refs = [own_ref, core_ref, x_ref, turned_ref.at[0], y_ref, turned_ref.at[1]]
+    sum_ref, late_ref = refs[5:7]
+    trans_refs = refs[7:]
     own = ident_ref[0]
     core = lax.rem(own, 2)
     pad_rows = padded(piece_refs[0].shape[0])
@@ -349,12 +350,11 @@
 
 def far_kernel(dims, ident_ref, place_ref, weight_ref, near_sum_ref, late_ref, *refs):
     slots, share_rows, group, groups, chip_rows = dims
-    piece_refs = refs[:4]
-    sum_ref = refs[4]
-    trans_refs = refs[5:]
+    here_ref, there_ref, sum_ref = refs[:3]
+    trans_refs = refs[3:]
     own = ident_ref[0]
     core = lax.rem(own, 2)
-    pack_rows, width = piece_refs[0].shape
+    _, pack_rows, width = here_ref.shape
     pad_rows = padded(pack_rows)
     half = LANES // 2
     edge = half - chip_rows
@@ -362,7 +362,7 @@
     lane = lax.broadcasted_iota(jnp.int32, (1, LANES), 1)
     low_half = lane < half
     in_rest = jnp.where(low_half, lane, lane - half) >= edge
-    lefts = [stacked(piece_refs[part::2]) for part in range(2)]
+    lefts = [stacked([here_ref.at[part], there_ref.at[part]]) for part in range(2)]
     twice = [jnp.zeros((ROWS, LANES), jnp.float32) for _ in range(slots)]
     once = [near_sum_ref[slot * ROWS : (slot + 1) * ROWS, :] for slot in range(slots)]
 
@@ -405,6 +405,23 @@
     return lax.ppermute(value, "block", [(index, index ^ mask) for index in range(blocks)])
 
 
+def pair_kernel(one_ref, two_ref, out_ref):
+    out_ref[0] = one_ref[...]
+    out_ref[1] = two_ref[...]
+
+
+def pair(one, two):
+    vmem = pl.BlockSpec(memory_space=pltpu.VMEM)
+    return pl.pallas_call(
+        pair_kernel,
+        out_shape=jax.ShapeDtypeStruct((2, *one.shape), one.dtype),
+        in_specs=[vmem] * 2,
+        out_specs=vmem,
+        compiler_params=pltpu.CompilerParams(vmem_limit_bytes=16 * 1024 * 1024),
+        name="pair",
+    )(one, two)
+
+
 def body(green, chol, counts, move_slot, move_dest):
     walkers = lax.axis_size("walker")
     blocks = lax.axis_size("block")
@@ -473,13 +490,12 @@
         name="order",
     )(block_index, walker_index, table, chol, own_rows)
     width = orb_count // 2
-    from_x, from_y, weights, coming[:2] = lax.optimization_barrier(
-        (from_x, from_y, weights, coming[:2])
+    from_x, from_y, from_core, weights, coming[:2] = lax.optimization_barrier(
+        (from_x, from_y, from_core, weights, coming[:2])
     )
     far = [swap(from_y[:, :width], near_x, blocks), swap(from_x[:, width:], near_y, blocks)]
-    near_pieces = [own_rows, from_core]
-    for piece in (from_x, from_y):
-        near_pieces += [piece, swap(piece, core, blocks)]
+    turned = swap(pair(from_x, from_y), core, blocks)
+    near_pieces = [own_rows, from_core, from_x, from_y, turned]
 
     dims = (slots, share_rows, group, groups, chip_rows)
     work = 2 * vectors * occ_count * orb_count * pack_rows
@@ -489,7 +505,7 @@
             jax.ShapeDtypeStruct((slots * ROWS, LANES), jnp.float32),
             jax.ShapeDtypeStruct((slots * chip_rows, vectors * occ_count), jnp.float32),
         ],
-        in_specs=[smem] + [vmem] * 7,
+        in_specs=[smem] + [vmem] * 6,
         out_specs=[vmem] * 2,
         scratch_shapes=[pltpu.VMEM((slots * 3 * chip_rows, group * occ_count), jnp.float32)]
         * groups,
@@ -500,11 +516,12 @@
         name="near",
     )(block_index, weights, *near_pieces)
     far, near_sums = lax.optimization_barrier((far, near_sums))
-    far_pieces = far + [swap(piece, core, blocks) for piece in far]
+    here = pair(*far)
+    far_pieces = [here, swap(here, core, blocks)]
     all_sums = pl.pallas_call(
         functools.partial(far_kernel, dims),
         out_shape=jax.ShapeDtypeStruct((blocks * walkers, LANES), jnp.float32),
-        in_specs=[smem] * 2 + [vmem] * 7,
+        in_specs=[smem] * 2 + [vmem] * 5,
         out_specs=vmem,
         scratch_shapes=[pltpu.VMEM((slots * chip_rows, group * occ_count), jnp.float32)] * groups,
         compiler_params=limit,

time: 41 us -> 41.2 us (level)
  waiting for transfers between devices: 6.86 us -> 8.26 us
  starting transfers between devices: 16.2 us -> 14.9 us
    ppermute x3, waiting for transfers between devices: 0.33 us -> 1.56 us  [body(): lax.ppermute(leaving[shift - 1], 'walker', [(z, (z + shift) % walkers) fo...]
    ppermute x9 -> x7, starting transfers between devices: 6.65 us -> 5.81 us  [swap(): lax.ppermute(value, 'block', [(index, index ^ mask) for index in range(bl...]
    ppermute x9 -> x7, waiting for transfers between devices: 1.31 us -> 1.49 us  [swap(): lax.ppermute(value, 'block', [(index, index ^ mask) for index in range(bl...]
  transfers between devices with their start and end apart: 13 -> 11, of which waited for: 5 -> 5; matrix products, arithmetic and copies ran while one was open for 2% -> 2% of each run, Pallas kernels for 35% -> 35%
where the time goes in v7:
time: 41.2 us; the launch traced here: 41 us
  starting transfers between devices  14.9 us (36%)
  Pallas kernels  14.7 us (36%)
  waiting for transfers between devices  8.26 us (20%)
  other arithmetic  1.34 us (3%)
  local copies, waits for them, and re-layouts  1.09 us (3%)
  between operations  0.75 us (2%)
    ppermute x3, starting transfers between devices, body(): lax.ppermute(leaving[shift - 1], 'walker', [(z, (z + shift) % walkers) fo...  5.9 us
    ppermute x7, starting transfers between devices, swap(): lax.ppermute(value, 'block', [(index, index ^ mask) for index in range(bl...  5.81 us
    all_to_all x1, waiting for transfers between devices, body(): lax.all_to_all(all_sums, ('block', 'walker'), split_axis=0, concat_axis=0...  5.21 us
    pallas_call x1, Pallas kernels, body(): pl.pallas_call(functools.partial(near_kernel, dims), out_shape=[jax.Shape...  4.73 us
    pallas_call x1, Pallas kernels, body(): pl.pallas_call(functools.partial(order_kernel, (group, groups, chip_rows,...  3.96 us
    all_to_all x1, starting transfers between devices, body(): lax.all_to_all(all_sums, ('block', 'walker'), split_axis=0, concat_axis=0...  3.21 us
    pallas_call x1, Pallas kernels, body(): pl.pallas_call(functools.partial(far_kernel, dims), out_shape=jax.ShapeDt...  3.01 us
    pallas_call x1, Pallas kernels, body(): pl.pallas_call(functools.partial(assemble_kernel, move_dims), out_shape=j...  1.93 us
  transfers between devices with their start and end apart: 11, of which 5 were waited for; matrix products, arithmetic and copies ran while one was open for 2% of the time, Pallas kernels for 35%

profile of v7, /device:TPU:0, one launch (start us, length us, event | category | flops | bytes accessed | tf_op | source)
XLA Modules:
  0.0 41.0 jit_solution(17485710116204863384)
XLA Ops:
  0.6 1.1 %copy-done = bf16[5,36864]{1,0:T(8,128)(2,1)S(1)} copy-done((bf16[5,36864]{1,0:T(8,128)(2,1)S(1)}, bf16[5,36864]{1,0:T(8,128)(2,1)}, u32[]{:S(2)}) %copy-start) | copy-done | bytes 368664
  1.7 0.3 pack.1.core_ref.own_ref.refs_0_
  2.0 3.0 %collective-permute-start = (bf16[120,1536]{1,0:T(8,128)(2,1)S(1)}, bf16[120,1536]{1,0:T(8,128)(2,1)S(1)}, u32[]{:S(2)}, u32[]{:S(2)}) collective-permute-start(bf16[120,1536]{1,0:T(8,128)(2,1)S(1)} %pack.1.core_ref.own_ref.refs_0_), channel_id=1, source_target_pairs={{0,8},{4,12},{8,0},{12,4},{16,24},{20,28},{24,16},{28,20},{1,9},{5... | collective-permute-start | bytes 1105928 | tf_op jit(solution)/shard_map/ppermute | solution.py:405
  5.0 1.5 %collective-permute-start.1 = (bf16[120,1536]{1,0:T(8,128)(2,1)S(1)}, bf16[120,1536]{1,0:T(8,128)(2,1)S(1)}, u32[]{:S(2)}, u32[]{:S(2)}) collective-permute-start(bf16[120,1536]{1,0:T(8,128)(2,1)S(1)} %pack.1.core_ref.own_ref.refs_0_), channel_id=1, source_target_pairs={{0,16},{4,20},{8,24},{12,28},{16,0},{20,4},{24,8},{28,12},{1,17},{... | collective-permute-start | bytes 1105928 | tf_op jit(solution)/shard_map/ppermute | solution.py:405
  6.5 0.7 %pad_add_fusion.table_ref = s32[5,4]{1,0:T(8,128)S(1)} fusion(s32[2,4]{1,0:T(2,128)} %bitcast.8, s32[2,4]{1,0:T(2,128)} %bitcast.9, s32[1,4]{1,0:T(1,128)} %bitcast.10), kind=kLoop, calls=%fused_computation | loop fusion | flops 40 | bytes 160 | tf_op jit(solution)/shard_map/concatenate | solution.py:434
  7.2 0.7 %leave.1 = (bf16[24,1536]{1,0:T(8,128)(2,1)S(1)}, bf16[24,1536]{1,0:T(8,128)(2,1)S(1)}, bf16[24,1536]{1,0:T(8,128)(2,1)S(1)}) custom-call(s32[1]{0:T(128)} %bitcast.walker_ref.ident_ref, s32[5,4]{1,0:T(8,128)S(1)} %pad_add_fusion.table_ref, bf16[120,1536]{1,0:T(8,128)(2,1)S(1)} %pack.1.core_ref.own_ref.refs_0_), custom_call_target="tpu_custom_call" | custom-call | tf_op jit(solution)/shard_map/leave/pallas_call | solution.py:452
  7.9 1.6 %collective-permute-start.3 = (bf16[24,1536]{1,0:T(8,128)(2,1)S(1)}, bf16[24,1536]{1,0:T(8,128)(2,1)S(1)}, u32[]{:S(2)}, u32[]{:S(2)}) collective-permute-start(bf16[24,1536]{1,0:T(8,128)(2,1)S(1)} %get-tuple-element.22), channel_id=1, source_target_pairs={{0,1},{1,2},{2,3},{3,0},{4,5},{5,6},{6,7},{7,4},{8,9},{9,10},{10,1... | collective-permute-start | bytes 221192 | tf_op jit(solution)/shard_map/ppermute | solution.py:462
  9.5 2.6 %collective-permute-start.4 = (bf16[24,1536]{1,0:T(8,128)(2,1)S(1)}, bf16[24,1536]{1,0:T(8,128)(2,1)S(1)}, u32[]{:S(2)}, u32[]{:S(2)}) collective-permute-start(bf16[24,1536]{1,0:T(8,128)(2,1)S(1)} %get-tuple-element.23), channel_id=1, source_target_pairs={{0,2},{1,3},{2,0},{3,1},{4,6},{5,7},{6,4},{7,5},{8,10},{9,11},{10,... | collective-permute-start | bytes 221192 | tf_op jit(solution)/shard_map/ppermute | solution.py:462
  12.1 4.0 %order.1 = (bf16[1536,1536]{1,0:T(8,128)(2,1)S(1)}, s32[5]{0:T(128)S(1)}) custom-call(s32[1]{0:T(128)} %bitcast.4.ident_ref, s32[1]{0:T(128)} %bitcast.walker_ref.ident_ref, s32[5,4]{1,0:T(8,128)S(1)} %pad_add_fusion.table_ref, bf16[8,192,1536]{2,1,0:T(8,128)(2,1)} %chol_ref.1, bf16[120,1536]{1,0:T(8,128)(2,1)S(1)} %pack.1.core_ref.own_ref.refs_0_), custom_call_target="tpu_custom_call" | custom-call | bytes 9437184 | tf_op jit(solution)/shard_map/order/pallas_call | solution.py:475
  16.1 1.6 %collective-permute-done.4.refs_1_ = bf16[24,1536]{1,0:T(8,128)(2,1)S(1)} collective-permute-done((bf16[24,1536]{1,0:T(8,128)(2,1)S(1)}, bf16[24,1536]{1,0:T(8,128)(2,1)S(1)}, u32[]{:S(2)}, u32[]{:S(2)}) %collective-permute-start.4) | collective-permute-done | bytes 73760 | tf_op jit(solution)/shard_map/ppermute | solution.py:462
  17.7 0.1 collective-permute-start.8
  17.9 0.6 %collective-permute-start.6 = (bf16[120,768]{1,0:T(8,128)(2,1)S(1)}, bf16[120,768]{1,0:T(8,128)(2,1)S(1)}, u32[]{:S(2)}, u32[]{:S(2)}) collective-permute-start(bf16[120,768]{1,0:T(8,128)(2,1)S(1)} %slice.6), channel_id=1, source_target_pairs={{0,8},{4,12},{8,0},{12,4},{16,24},{20,28},{24,16},{28,20},{1,9},{5... | collective-permute-start | bytes 552968 | tf_op jit(solution)/shard_map/ppermute | solution.py:405
  18.5 0.5 %collective-permute-start.7 = (bf16[120,768]{1,0:T(8,128)(2,1)S(1)}, bf16[120,768]{1,0:T(8,128)(2,1)S(1)}, u32[]{:S(2)}, u32[]{:S(2)}) collective-permute-start(bf16[120,768]{1,0:T(8,128)(2,1)S(1)} %slice.7), channel_id=1, source_target_pairs={{0,16},{4,20},{8,24},{12,28},{16,0},{20,4},{24,8},{28,12},{1,17},{... | collective-permute-start | bytes 552968 | tf_op jit(solution)/shard_map/ppermute | solution.py:405
  19.0 1.0 %collective-permute-done.8.refs_4_ = bf16[2,120,1536]{2,1,0:T(8,128)(2,1)S(1)} collective-permute-done((bf16[2,120,1536]{2,1,0:T(8,128)(2,1)S(1)}, bf16[2,120,1536]{2,1,0:T(8,128)(2,1)S(1)}, u32[]{:S(2)}, u32[]{:S(2)}) %collective-permute-start.8) | collective-permute-done | bytes 737312 | tf_op jit(solution)/shard_map/ppermute | solution.py:405
  20.0 4.7 %near.1 = (f32[40,128]{1,0:T(8,128)S(1)}, f32[240,1536]{1,0:T(8,128)S(1)}) custom-call(s32[1]{0:T(128)} %bitcast.4.ident_ref, bf16[1536,1536]{1,0:T(8,128)(2,1)S(1)} %get-tuple-element.28.weight_ref, bf16[120,1536]{1,0:T(8,128)(2,1)S(1)} %pack.1.core_ref.own_ref.refs_0_, bf16[120,1536]{1,0:T(8,128)(2,1)S(1)} %collective-permute-done.2.refs_1_, ...), custom_call_target="tpu_custom_call" | custom-call | flops 3397386240 | bytes 4718592 | tf_op jit(solution)/shard_map/near/pallas_call | solution.py:502
  24.7 0.2 collective-permute-done.6.one_ref
  24.9 0.3 collective-permute-done.7.two_ref
  25.2 0.1 collective-permute-start.9
  25.3 1.7 %collective-permute-start.5 = (bf16[24,1536]{1,0:T(8,128)(2,1)S(1)}, bf16[24,1536]{1,0:T(8,128)(2,1)S(1)}, u32[]{:S(2)}, u32[]{:S(2)}) collective-permute-start(bf16[24,1536]{1,0:T(8,128)(2,1)S(1)} %get-tuple-element.26), channel_id=1, source_target_pairs={{0,3},{1,0},{2,1},{3,2},{4,7},{5,4},{6,5},{7,6},{8,11},{9,8},{10,9... | collective-permute-start | bytes 221192 | tf_op jit(solution)/shard_map/ppermute | solution.py:462
  27.0 3.0 %far.1 = f32[32,128]{1,0:T(8,128)} custom-call(s32[1]{0:T(128)} %bitcast.4.ident_ref, s32[5]{0:T(128)S(1)} %get-tuple-element.27.place_ref, bf16[1536,1536]{1,0:T(8,128)(2,1)S(1)} %get-tuple-element.28.weight_ref, f32[40,128]{1,0:T(8,128)S(1)} %get-tuple-element.33.near_sum_ref, f32[240,1536]{1,0:T(8,128)S(1)} %get-tuple-element.34.late_ref, ...), custom_call_target="tpu_custom_call" | custom-call | flops 1132462080 | bytes 4718592 | tf_op jit(solution)/shard_map/far/pallas_call | solution.py:521
  30.0 3.2 %all-to-all-start = ((f32[32,1,128]{2,1,0:T(1,128)}), f32[32,1,128]{2,1,0:T(1,128)S(1)}, u32[]{:S(2)}, u32[]{:S(2)}) async-start(f32[32,1,128]{2,1,0:T(1,128)} %bitcast.6), calls=%async_computation | async-start | bytes 32768 | tf_op jit(solution)/shard_map/all_to_all | solution.py:550
  33.2 1.9 %assemble.1 = bf16[3,36864]{1,0:T(4,128)(2,1)} custom-call(s32[1]{0:T(128)} %bitcast.walker_ref.ident_ref, s32[5,4]{1,0:T(8,128)S(1)} %pad_add_fusion.table_ref, bf16[5,36864]{1,0:T(8,128)(2,1)S(1)} %copy-done.1, bf16[24,1536]{1,0:T(8,128)(2,1)S(1)} %collective-permute-done.3.refs_0_, bf16[24,1536]{1,0:T(8,128)(2,1)S(1)} %collective-permute-done.4.refs_1_, ...), custom_call_target="tpu_custom_call" | custom-call | tf_op jit(solution)/shard_map/assemble/pallas_call | solution.py:535
  35.2 5.2 %all-to-all-done = f32[32,1,128]{2,1,0:T(1,128)S(1)} async-done(((f32[32,1,128]{2,1,0:T(1,128)}), f32[32,1,128]{2,1,0:T(1,128)S(1)}, u32[]{:S(2)}, u32[]{:S(2)}) %all-to-all-start) | async-done | bytes 16416 | tf_op jit(solution)/shard_map/all_to_all | solution.py:550
  40.4 0.6 %dynamic-slice_multiply_fusion = f32[3]{0:T(128)} fusion(f32[128]{0:T(128)S(1)} %reduce_sum.9, s32[]{:T(128)S(6)} %select_n.3), kind=kLoop, calls=%fused_computation.1 | loop fusion | flops 3 | bytes 28 | tf_op jit(solution)/shard_map/mul | solution.py:555
  (15 shorter events, 0.2 us)
Async XLA Ops:
  0.6 1.1 %copy-start = (bf16[5,36864]{1,0:T(8,128)(2,1)S(1)}, bf16[5,36864]{1,0:T(8,128)(2,1)}, u32[]{:S(2)}) copy-start(bf16[5,36864]{1,0:T(8,128)(2,1)} %green_ref.3) | copy-start | bytes 1105924
  2.0 15.7 %collective-permute-start = (bf16[120,1536]{1,0:T(8,128)(2,1)S(1)}, bf16[120,1536]{1,0:T(8,128)(2,1)S(1)}, u32[]{:S(2)}, u32[]{:S(2)}) collective-permute-start(bf16[120,1536]{1,0:T(8,128)(2,1)S(1)} %pack.1.core_ref.own_ref.refs_0_), channel_id=1, source_target_pairs={{0,8},{4,12},{8,0},{12,4},{16,24},{20,28},{24,16},{28,20},{1,9},{5... | collective-permute-start | bytes 1105928 | tf_op jit(solution)/shard_map/ppermute | solution.py:405
  5.0 12.7 %collective-permute-start.1 = (bf16[120,1536]{1,0:T(8,128)(2,1)S(1)}, bf16[120,1536]{1,0:T(8,128)(2,1)S(1)}, u32[]{:S(2)}, u32[]{:S(2)}) collective-permute-start(bf16[120,1536]{1,0:T(8,128)(2,1)S(1)} %pack.1.core_ref.own_ref.refs_0_), channel_id=1, source_target_pairs={{0,16},{4,20},{8,24},{12,28},{16,0},{20,4},{24,8},{28,12},{1,17},{... | collective-permute-start | bytes 1105928 | tf_op jit(solution)/shard_map/ppermute | solution.py:405
  6.5 11.2 %collective-permute-start.2 = (bf16[120,1536]{1,0:T(8,128)(2,1)S(1)}, bf16[120,1536]{1,0:T(8,128)(2,1)S(1)}, u32[]{:S(2)}, u32[]{:S(2)}) collective-permute-start(bf16[120,1536]{1,0:T(8,128)(2,1)S(1)} %pack.1.core_ref.own_ref.refs_0_), channel_id=1, source_target_pairs={{0,4},{4,0},{8,12},{12,8},{16,20},{20,16},{24,28},{28,24},{1,5},{5... | collective-permute-start | bytes 1105928 | tf_op jit(solution)/shard_map/ppermute | solution.py:405
  7.9 8.2 %collective-permute-start.3 = (bf16[24,1536]{1,0:T(8,128)(2,1)S(1)}, bf16[24,1536]{1,0:T(8,128)(2,1)S(1)}, u32[]{:S(2)}, u32[]{:S(2)}) collective-permute-start(bf16[24,1536]{1,0:T(8,128)(2,1)S(1)} %get-tuple-element.22), channel_id=1, source_target_pairs={{0,1},{1,2},{2,3},{3,0},{4,5},{5,6},{6,7},{7,4},{8,9},{9,10},{10,1... | collective-permute-start | bytes 221192 | tf_op jit(solution)/shard_map/ppermute | solution.py:462
  9.5 8.1 %collective-permute-start.4 = (bf16[24,1536]{1,0:T(8,128)(2,1)S(1)}, bf16[24,1536]{1,0:T(8,128)(2,1)S(1)}, u32[]{:S(2)}, u32[]{:S(2)}) collective-permute-start(bf16[24,1536]{1,0:T(8,128)(2,1)S(1)} %get-tuple-element.23), channel_id=1, source_target_pairs={{0,2},{1,3},{2,0},{3,1},{4,6},{5,7},{6,4},{7,5},{8,10},{9,11},{10,... | collective-permute-start | bytes 221192 | tf_op jit(solution)/shard_map/ppermute | solution.py:462
  17.7 2.3 %collective-permute-start.8 = (bf16[2,120,1536]{2,1,0:T(8,128)(2,1)S(1)}, bf16[2,120,1536]{2,1,0:T(8,128)(2,1)S(1)}, u32[]{:S(2)}, u32[]{:S(2)}) collective-permute-start(bf16[2,120,1536]{2,1,0:T(8,128)(2,1)S(1)} %pair.2), channel_id=1, source_target_pairs={{0,4},{4,0},{8,12},{12,8},{16,20},{20,16},{24,28},{28,24},{1,5},{5... | collective-permute-start | bytes 2211848 | tf_op jit(solution)/shard_map/ppermute | solution.py:405
  17.9 7.1 %collective-permute-start.6 = (bf16[120,768]{1,0:T(8,128)(2,1)S(1)}, bf16[120,768]{1,0:T(8,128)(2,1)S(1)}, u32[]{:S(2)}, u32[]{:S(2)}) collective-permute-start(bf16[120,768]{1,0:T(8,128)(2,1)S(1)} %slice.6), channel_id=1, source_target_pairs={{0,8},{4,12},{8,0},{12,4},{16,24},{20,28},{24,16},{28,20},{1,9},{5... | collective-permute-start | bytes 552968 | tf_op jit(solution)/shard_map/ppermute | solution.py:405
  18.5 6.7 %collective-permute-start.7 = (bf16[120,768]{1,0:T(8,128)(2,1)S(1)}, bf16[120,768]{1,0:T(8,128)(2,1)S(1)}, u32[]{:S(2)}, u32[]{:S(2)}) collective-permute-start(bf16[120,768]{1,0:T(8,128)(2,1)S(1)} %slice.7), channel_id=1, source_target_pairs={{0,16},{4,20},{8,24},{12,28},{16,0},{20,4},{24,8},{28,12},{1,17},{... | collective-permute-start | bytes 552968 | tf_op jit(solution)/shard_map/ppermute | solution.py:405
  24.7 8.5 %copy-start.1 = (bf16[5,36864]{1,0:T(8,128)(2,1)S(1)}, bf16[5,36864]{1,0:T(8,128)(2,1)}, u32[]{:S(2)}) copy-start(bf16[5,36864]{1,0:T(8,128)(2,1)} %green_ref.3) | copy-start | bytes 1105924
  25.2 1.8 %collective-permute-start.9 = (bf16[2,120,768]{2,1,0:T(8,128)(2,1)S(1)}, bf16[2,120,768]{2,1,0:T(8,128)(2,1)S(1)}, u32[]{:S(2)}, u32[]{:S(2)}) collective-permute-start(bf16[2,120,768]{2,1,0:T(8,128)(2,1)S(1)} %pair.3.refs_0_), channel_id=1, source_target_pairs={{0,4},{4,0},{8,12},{12,8},{16,20},{20,16},{24,28},{28,24},{1,5},{5... | collective-permute-start | bytes 1105928 | tf_op jit(solution)/shard_map/ppermute | solution.py:405
  25.3 7.9 %collective-permute-start.5 = (bf16[24,1536]{1,0:T(8,128)(2,1)S(1)}, bf16[24,1536]{1,0:T(8,128)(2,1)S(1)}, u32[]{:S(2)}, u32[]{:S(2)}) collective-permute-start(bf16[24,1536]{1,0:T(8,128)(2,1)S(1)} %get-tuple-element.26), channel_id=1, source_target_pairs={{0,3},{1,0},{2,1},{3,2},{4,7},{5,4},{6,5},{7,6},{8,11},{9,8},{10,9... | collective-permute-start | bytes 221192 | tf_op jit(solution)/shard_map/ppermute | solution.py:462
  30.0 10.4 %all-to-all-start = ((f32[32,1,128]{2,1,0:T(1,128)}), f32[32,1,128]{2,1,0:T(1,128)S(1)}, u32[]{:S(2)}, u32[]{:S(2)}) async-start(f32[32,1,128]{2,1,0:T(1,128)} %bitcast.6), calls=%async_computation | async-start | bytes 32768 | tf_op jit(solution)/shard_map/all_to_all | solution.py:550

commit v8 on v5

--- a/solution.py
+++ b/solution.py
@@ -280,9 +280,10 @@
 
 def near_kernel(dims, ident_ref, weight_ref, *refs):
     slots, share_rows, group, groups, chip_rows = dims
-    piece_refs = refs[:6]
-    sum_ref, late_ref = refs[6:8]
-    trans_refs = refs[8:]
+    own_ref, core_ref, x_ref, y_ref, turned_ref = refs[:5]
+    piece_refs = [own_ref, core_ref, x_ref, turned_ref.at[0], y_ref, turned_ref.at[1]]
+    sum_ref, late_ref = refs[5:7]
+    trans_refs = refs[7:]
     own = ident_ref[0]
     core = lax.rem(own, 2)
     pad_rows = padded(piece_refs[0].shape[0])
@@ -342,12 +343,11 @@
 
 def far_kernel(dims, ident_ref, place_ref, weight_ref, near_sum_ref, late_ref, *refs):
     slots, share_rows, group, groups, chip_rows = dims
-    piece_refs = refs[:4]
-    sum_ref = refs[4]
-    trans_refs = refs[5:]
+    here_ref, there_ref, sum_ref = refs[:3]
+    trans_refs = refs[3:]
     own = ident_ref[0]
     core = lax.rem(own, 2)
-    pack_rows, width = piece_refs[0].shape
+    _, pack_rows, width = here_ref.shape
     pad_rows = padded(pack_rows)
     half = LANES // 2
     edge = half - chip_rows
@@ -355,7 +355,7 @@
     lane = lax.broadcasted_iota(jnp.int32, (1, LANES), 1)
     low_half = lane < half
     in_rest = jnp.where(low_half, lane, lane - half) >= edge
-    lefts = [stacked(piece_refs[part::2]) for part in range(2)]
+    lefts = [stacked([here_ref.at[part], there_ref.at[part]]) for part in range(2)]
     twice = [jnp.zeros((ROWS, LANES), jnp.float32) for _ in range(slots)]
     once = [near_sum_ref[slot * ROWS : (slot + 1) * ROWS, :] for slot in range(slots)]
 
@@ -398,6 +398,23 @@
     return lax.ppermute(value, "block", [(index, index ^ mask) for index in range(blocks)])
 
 
+def pair_kernel(one_ref, two_ref, out_ref):
+    out_ref[0] = one_ref[...]
+    out_ref[1] = two_ref[...]
+
+
+def pair(one, two):
+    vmem = pl.BlockSpec(memory_space=pltpu.VMEM)
+    return pl.pallas_call(
+        pair_kernel,
+        out_shape=jax.ShapeDtypeStruct((2, *one.shape), one.dtype),
+        in_specs=[vmem] * 2,
+        out_specs=vmem,
+        compiler_params=pltpu.CompilerParams(vmem_limit_bytes=16 * 1024 * 1024),
+        name="pair",
+    )(one, two)
+
+
 def body(green, chol, counts, move_slot, move_dest):
     walkers = lax.axis_size("walker")
     blocks = lax.axis_size("block")
@@ -463,13 +480,12 @@
     from_y = swap(own_rows, near_y, blocks)
     from_core = swap(own_rows, core, blocks)
     width = orb_count // 2
-    from_x, from_y, weights, coming[:2] = lax.optimization_barrier(
-        (from_x, from_y, weights, coming[:2])
+    from_x, from_y, from_core, weights, coming[:2] = lax.optimization_barrier(
+        (from_x, from_y, from_core, weights, coming[:2])
     )
     far = [swap(from_y[:, :width], near_x, blocks), swap(from_x[:, width:], near_y, blocks)]
-    near_pieces = [own_rows, from_core]
-    for piece in (from_x, from_y):
-        near_pieces += [piece, swap(piece, core, blocks)]
+    turned = swap(pair(from_x, from_y), core, blocks)
+    near_pieces = [own_rows, from_core, from_x, from_y, turned]
 
     dims = (slots, share_rows, group, groups, chip_rows)
     work = 2 * vectors * occ_count * orb_count * pack_rows
@@ -479,7 +495,7 @@
             jax.ShapeDtypeStruct((slots * ROWS, LANES), jnp.float32),
             jax.ShapeDtypeStruct((slots * chip_rows, vectors * occ_count), jnp.float32),
         ],
-        in_specs=[smem] + [vmem] * 7,
+        in_specs=[smem] + [vmem] * 6,
         out_specs=[vmem] * 2,
         scratch_shapes=[pltpu.VMEM((slots * 3 * chip_rows, group * occ_count), jnp.float32)]
         * groups,
@@ -490,11 +506,12 @@
         name="near",
     )(block_index, weights, *near_pieces)
     far, near_sums = lax.optimization_barrier((far, near_sums))
-    far_pieces = far + [swap(piece, core, blocks) for piece in far]
+    here = pair(*far)
+    far_pieces = [here, swap(here, core, blocks)]
     all_sums = pl.pallas_call(
         functools.partial(far_kernel, dims),
         out_shape=jax.ShapeDtypeStruct((blocks * walkers, LANES), jnp.float32),
-        in_specs=[smem] * 2 + [vmem] * 7,
+        in_specs=[smem] * 2 + [vmem] * 5,
         out_specs=vmem,
         scratch_shapes=[pltpu.VMEM((slots * chip_rows, group * occ_count), jnp.float32)] * groups,
         compiler_params=limit,

time: 41 us -> 41.7 us (1.017)
  waiting for transfers between devices: 7.85 us -> 9.47 us
  starting transfers between devices: 15.7 us -> 14.6 us
    ppermute x3, waiting for transfers between devices: 1.53 us -> 2.77 us  [body(): lax.ppermute(leaving[shift - 1], 'walker', [(z, (z + shift) % walkers) fo...]
    ppermute x9 -> x7, starting transfers between devices: 6.65 us -> 5.81 us  [swap(): lax.ppermute(value, 'block', [(index, index ^ mask) for index in range(bl...]
    all_to_all x1, starting transfers between devices: 3.33 us -> 2.91 us  [body(): lax.all_to_all(all_sums, ('block', 'walker'), split_axis=0, concat_axis=0...]
    ppermute x9 -> x7, waiting for transfers between devices: 1.11 us -> 1.49 us  [swap(): lax.ppermute(value, 'block', [(index, index ^ mask) for index in range(bl...]
  transfers between devices with their start and end apart: 13 -> 11, of which waited for: 5 -> 5; matrix products, arithmetic and copies ran while one was open for 2% -> 2% of each run, Pallas kernels for 34% -> 33%
where the time goes in v8:
time: 41.7 us; the launch traced here: 41.5 us
  starting transfers between devices  14.6 us (35%)
  Pallas kernels  14.2 us (34%)
  waiting for transfers between devices  9.47 us (23%)
  other arithmetic  1.34 us (3%)
  local copies, waits for them, and re-layouts  1.09 us (3%)
  between operations  0.75 us (2%)
    ppermute x3, starting transfers between devices, body(): lax.ppermute(leaving[shift - 1], 'walker', [(z, (z + shift) % walkers) fo...  5.9 us
    ppermute x7, starting transfers between devices, swap(): lax.ppermute(value, 'block', [(index, index ^ mask) for index in range(bl...  5.81 us
    all_to_all x1, waiting for transfers between devices, body(): lax.all_to_all(all_sums, ('block', 'walker'), split_axis=0, concat_axis=0...  5.22 us
    pallas_call x1, Pallas kernels, body(): pl.pallas_call(functools.partial(near_kernel, dims), out_shape=[jax.Shape...  4.73 us
    pallas_call x1, Pallas kernels, body(): pl.pallas_call(functools.partial(far_kernel, dims), out_shape=jax.ShapeDt...  3.02 us
    all_to_all x1, starting transfers between devices, body(): lax.all_to_all(all_sums, ('block', 'walker'), split_axis=0, concat_axis=0...  2.91 us
    ppermute x3, waiting for transfers between devices, body(): lax.ppermute(leaving[shift - 1], 'walker', [(z, (z + shift) % walkers) fo...  2.77 us
    pallas_call x1, Pallas kernels, body(): pl.pallas_call(functools.partial(order_kernel, (group, groups, chip_rows)...  2.76 us
  transfers between devices with their start and end apart: 11, of which 5 were waited for; matrix products, arithmetic and copies ran while one was open for 2% of the time, Pallas kernels for 33%

profile of v8, /device:TPU:0, one launch (start us, length us, event | category | flops | bytes accessed | tf_op | source)
XLA Modules:
  0.0 41.5 jit_solution(8717891402763646050)
XLA Ops:
  0.6 1.1 %copy-done = bf16[5,36864]{1,0:T(8,128)(2,1)S(1)} copy-done((bf16[5,36864]{1,0:T(8,128)(2,1)S(1)}, bf16[5,36864]{1,0:T(8,128)(2,1)}, u32[]{:S(2)}) %copy-start) | copy-done | bytes 368664
  1.7 0.3 pack.1.own_ref.refs_0_
  2.0 3.0 %collective-permute-start = (bf16[120,1536]{1,0:T(8,128)(2,1)S(1)}, bf16[120,1536]{1,0:T(8,128)(2,1)S(1)}, u32[]{:S(2)}, u32[]{:S(2)}) collective-permute-start(bf16[120,1536]{1,0:T(8,128)(2,1)S(1)} %pack.1.own_ref.refs_0_), channel_id=1, source_target_pairs={{0,8},{4,12},{8,0},{12,4},{16,24},{20,28},{24,16},{28,20},{1,9},{5... | collective-permute-start | bytes 1105928 | tf_op jit(solution)/shard_map/ppermute | solution.py:398
  5.0 1.5 %collective-permute-start.1 = (bf16[120,1536]{1,0:T(8,128)(2,1)S(1)}, bf16[120,1536]{1,0:T(8,128)(2,1)S(1)}, u32[]{:S(2)}, u32[]{:S(2)}) collective-permute-start(bf16[120,1536]{1,0:T(8,128)(2,1)S(1)} %pack.1.own_ref.refs_0_), channel_id=1, source_target_pairs={{0,16},{4,20},{8,24},{12,28},{16,0},{20,4},{24,8},{28,12},{1,17},{... | collective-permute-start | bytes 1105928 | tf_op jit(solution)/shard_map/ppermute | solution.py:398
  6.5 0.7 %pad_add_fusion.table_ref = s32[5,4]{1,0:T(8,128)S(1)} fusion(s32[2,4]{1,0:T(2,128)} %bitcast.8, s32[2,4]{1,0:T(2,128)} %bitcast.9, s32[1,4]{1,0:T(1,128)} %bitcast.10), kind=kLoop, calls=%fused_computation | loop fusion | flops 40 | bytes 160 | tf_op jit(solution)/shard_map/concatenate | solution.py:427
  7.2 1.4 %leave.1 = (bf16[24,1536]{1,0:T(8,128)(2,1)S(1)}, bf16[24,1536]{1,0:T(8,128)(2,1)S(1)}, bf16[24,1536]{1,0:T(8,128)(2,1)S(1)}, s32[5]{0:T(128)S(1)}) custom-call(s32[1]{0:T(128)} %bitcast.ident_ref, s32[5,4]{1,0:T(8,128)S(1)} %pad_add_fusion.table_ref, bf16[120,1536]{1,0:T(8,128)(2,1)S(1)} %pack.1.own_ref.refs_0_), custom_call_target="tpu_custom_call" | custom-call | tf_op jit(solution)/shard_map/leave/pallas_call | solution.py:445
  8.6 1.6 %collective-permute-start.3 = (bf16[24,1536]{1,0:T(8,128)(2,1)S(1)}, bf16[24,1536]{1,0:T(8,128)(2,1)S(1)}, u32[]{:S(2)}, u32[]{:S(2)}) collective-permute-start(bf16[24,1536]{1,0:T(8,128)(2,1)S(1)} %get-tuple-element.20), channel_id=1, source_target_pairs={{0,1},{1,2},{2,3},{3,0},{4,5},{5,6},{6,7},{7,4},{8,9},{9,10},{10,1... | collective-permute-start | bytes 221192 | tf_op jit(solution)/shard_map/ppermute | solution.py:456
  10.3 2.6 %collective-permute-start.4 = (bf16[24,1536]{1,0:T(8,128)(2,1)S(1)}, bf16[24,1536]{1,0:T(8,128)(2,1)S(1)}, u32[]{:S(2)}, u32[]{:S(2)}) collective-permute-start(bf16[24,1536]{1,0:T(8,128)(2,1)S(1)} %get-tuple-element.21), channel_id=1, source_target_pairs={{0,2},{1,3},{2,0},{3,1},{4,6},{5,7},{6,4},{7,5},{8,10},{9,11},{10,... | collective-permute-start | bytes 221192 | tf_op jit(solution)/shard_map/ppermute | solution.py:456
  12.8 2.8 %order.1.weight_ref = bf16[1536,1536]{1,0:T(8,128)(2,1)S(1)} custom-call(s32[1]{0:T(128)} %bitcast.4.ident_ref, bf16[8,192,1536]{2,1,0:T(8,128)(2,1)} %chol_ref.1, bf16[120,1536]{1,0:T(8,128)(2,1)S(1)} %pack.1.own_ref.refs_0_), custom_call_target="tpu_custom_call" | custom-call | bytes 9437184 | tf_op jit(solution)/shard_map/order/pallas_call | solution.py:465
  15.6 2.8 %collective-permute-done.4.refs_1_ = bf16[24,1536]{1,0:T(8,128)(2,1)S(1)} collective-permute-done((bf16[24,1536]{1,0:T(8,128)(2,1)S(1)}, bf16[24,1536]{1,0:T(8,128)(2,1)S(1)}, u32[]{:S(2)}, u32[]{:S(2)}) %collective-permute-start.4) | collective-permute-done | bytes 73760 | tf_op jit(solution)/shard_map/ppermute | solution.py:456
  18.5 0.1 collective-permute-start.8
  18.6 0.6 %collective-permute-start.6 = (bf16[120,768]{1,0:T(8,128)(2,1)S(1)}, bf16[120,768]{1,0:T(8,128)(2,1)S(1)}, u32[]{:S(2)}, u32[]{:S(2)}) collective-permute-start(bf16[120,768]{1,0:T(8,128)(2,1)S(1)} %slice.6), channel_id=1, source_target_pairs={{0,8},{4,12},{8,0},{12,4},{16,24},{20,28},{24,16},{28,20},{1,9},{5... | collective-permute-start | bytes 552968 | tf_op jit(solution)/shard_map/ppermute | solution.py:398
  19.2 0.5 %collective-permute-start.7 = (bf16[120,768]{1,0:T(8,128)(2,1)S(1)}, bf16[120,768]{1,0:T(8,128)(2,1)S(1)}, u32[]{:S(2)}, u32[]{:S(2)}) collective-permute-start(bf16[120,768]{1,0:T(8,128)(2,1)S(1)} %slice.7), channel_id=1, source_target_pairs={{0,16},{4,20},{8,24},{12,28},{16,0},{20,4},{24,8},{28,12},{1,17},{... | collective-permute-start | bytes 552968 | tf_op jit(solution)/shard_map/ppermute | solution.py:398
  19.7 1.0 %collective-permute-done.8.refs_4_ = bf16[2,120,1536]{2,1,0:T(8,128)(2,1)S(1)} collective-permute-done((bf16[2,120,1536]{2,1,0:T(8,128)(2,1)S(1)}, bf16[2,120,1536]{2,1,0:T(8,128)(2,1)S(1)}, u32[]{:S(2)}, u32[]{:S(2)}) %collective-permute-start.8) | collective-permute-done | bytes 737312 | tf_op jit(solution)/shard_map/ppermute | solution.py:398
  20.7 4.7 %near.1 = (f32[40,128]{1,0:T(8,128)S(1)}, f32[240,1536]{1,0:T(8,128)S(1)}) custom-call(s32[1]{0:T(128)} %bitcast.4.ident_ref, bf16[1536,1536]{1,0:T(8,128)(2,1)S(1)} %order.1.weight_ref, bf16[120,1536]{1,0:T(8,128)(2,1)S(1)} %pack.1.own_ref.refs_0_, bf16[120,1536]{1,0:T(8,128)(2,1)S(1)} %collective-permute-done.2.refs_1_, ...), custom_call_target="tpu_custom_call" | custom-call | flops 3397386240 | bytes 4718592 | tf_op jit(solution)/shard_map/near/pallas_call | solution.py:492
  25.5 0.2 collective-permute-done.6.one_ref
  25.7 0.3 collective-permute-done.7.two_ref
  26.0 0.1 collective-permute-start.9
  26.0 1.7 %collective-permute-start.5 = (bf16[24,1536]{1,0:T(8,128)(2,1)S(1)}, bf16[24,1536]{1,0:T(8,128)(2,1)S(1)}, u32[]{:S(2)}, u32[]{:S(2)}) collective-permute-start(bf16[24,1536]{1,0:T(8,128)(2,1)S(1)} %get-tuple-element.24), channel_id=1, source_target_pairs={{0,3},{1,0},{2,1},{3,2},{4,7},{5,4},{6,5},{7,6},{8,11},{9,8},{10,9... | collective-permute-start | bytes 221192 | tf_op jit(solution)/shard_map/ppermute | solution.py:456
  27.7 3.0 %far.1 = f32[32,128]{1,0:T(8,128)} custom-call(s32[1]{0:T(128)} %bitcast.4.ident_ref, s32[5]{0:T(128)S(1)} %get-tuple-element.25.place_ref, bf16[1536,1536]{1,0:T(8,128)(2,1)S(1)} %order.1.weight_ref, f32[40,128]{1,0:T(8,128)S(1)} %get-tuple-element.31.near_sum_ref, f32[240,1536]{1,0:T(8,128)S(1)} %get-tuple-element.32.late_ref, ...), custom_call_target="tpu_custom_call" | custom-call | flops 1132462080 | bytes 4718592 | tf_op jit(solution)/shard_map/far/pallas_call | solution.py:511
  30.7 2.9 %all-to-all-start = ((f32[32,1,128]{2,1,0:T(1,128)}), f32[32,1,128]{2,1,0:T(1,128)S(1)}, u32[]{:S(2)}, u32[]{:S(2)}) async-start(f32[32,1,128]{2,1,0:T(1,128)} %bitcast.6), calls=%async_computation | async-start | bytes 32768 | tf_op jit(solution)/shard_map/all_to_all | solution.py:540
  33.7 1.9 %assemble.1 = bf16[3,36864]{1,0:T(4,128)(2,1)} custom-call(s32[1]{0:T(128)} %bitcast.ident_ref, s32[5,4]{1,0:T(8,128)S(1)} %pad_add_fusion.table_ref, bf16[5,36864]{1,0:T(8,128)(2,1)S(1)} %copy-done.1, bf16[24,1536]{1,0:T(8,128)(2,1)S(1)} %collective-permute-done.3.refs_0_, bf16[24,1536]{1,0:T(8,128)(2,1)S(1)} %collective-permute-done.4.refs_1_, ...), custom_call_target="tpu_custom_call" | custom-call | tf_op jit(solution)/shard_map/assemble/pallas_call | solution.py:525
  35.6 5.2 %all-to-all-done = f32[32,1,128]{2,1,0:T(1,128)S(1)} async-done(((f32[32,1,128]{2,1,0:T(1,128)}), f32[32,1,128]{2,1,0:T(1,128)S(1)}, u32[]{:S(2)}, u32[]{:S(2)}) %all-to-all-start) | async-done | bytes 16416 | tf_op jit(solution)/shard_map/all_to_all | solution.py:540
  40.9 0.6 %dynamic-slice_multiply_fusion = f32[3]{0:T(128)} fusion(f32[128]{0:T(128)S(1)} %reduce_sum.9, s32[]{:T(128)S(6)} %select_n.3), kind=kLoop, calls=%fused_computation.1 | loop fusion | flops 3 | bytes 28 | tf_op jit(solution)/shard_map/mul | solution.py:545
  (15 shorter events, 0.2 us)
Async XLA Ops:
  0.6 1.1 %copy-start = (bf16[5,36864]{1,0:T(8,128)(2,1)S(1)}, bf16[5,36864]{1,0:T(8,128)(2,1)}, u32[]{:S(2)}) copy-start(bf16[5,36864]{1,0:T(8,128)(2,1)} %green_ref.3) | copy-start | bytes 1105924
  2.0 16.4 %collective-permute-start = (bf16[120,1536]{1,0:T(8,128)(2,1)S(1)}, bf16[120,1536]{1,0:T(8,128)(2,1)S(1)}, u32[]{:S(2)}, u32[]{:S(2)}) collective-permute-start(bf16[120,1536]{1,0:T(8,128)(2,1)S(1)} %pack.1.own_ref.refs_0_), channel_id=1, source_target_pairs={{0,8},{4,12},{8,0},{12,4},{16,24},{20,28},{24,16},{28,20},{1,9},{5... | collective-permute-start | bytes 1105928 | tf_op jit(solution)/shard_map/ppermute | solution.py:398
  5.0 13.4 %collective-permute-start.1 = (bf16[120,1536]{1,0:T(8,128)(2,1)S(1)}, bf16[120,1536]{1,0:T(8,128)(2,1)S(1)}, u32[]{:S(2)}, u32[]{:S(2)}) collective-permute-start(bf16[120,1536]{1,0:T(8,128)(2,1)S(1)} %pack.1.own_ref.refs_0_), channel_id=1, source_target_pairs={{0,16},{4,20},{8,24},{12,28},{16,0},{20,4},{24,8},{28,12},{1,17},{... | collective-permute-start | bytes 1105928 | tf_op jit(solution)/shard_map/ppermute | solution.py:398
  6.5 11.9 %collective-permute-start.2 = (bf16[120,1536]{1,0:T(8,128)(2,1)S(1)}, bf16[120,1536]{1,0:T(8,128)(2,1)S(1)}, u32[]{:S(2)}, u32[]{:S(2)}) collective-permute-start(bf16[120,1536]{1,0:T(8,128)(2,1)S(1)} %pack.1.own_ref.refs_0_), channel_id=1, source_target_pairs={{0,4},{4,0},{8,12},{12,8},{16,20},{20,16},{24,28},{28,24},{1,5},{5... | collective-permute-start | bytes 1105928 | tf_op jit(solution)/shard_map/ppermute | solution.py:398
  8.6 7.0 %collective-permute-start.3 = (bf16[24,1536]{1,0:T(8,128)(2,1)S(1)}, bf16[24,1536]{1,0:T(8,128)(2,1)S(1)}, u32[]{:S(2)}, u32[]{:S(2)}) collective-permute-start(bf16[24,1536]{1,0:T(8,128)(2,1)S(1)} %get-tuple-element.20), channel_id=1, source_target_pairs={{0,1},{1,2},{2,3},{3,0},{4,5},{5,6},{6,7},{7,4},{8,9},{9,10},{10,1... | collective-permute-start | bytes 221192 | tf_op jit(solution)/shard_map/ppermute | solution.py:456
  10.3 8.1 %collective-permute-start.4 = (bf16[24,1536]{1,0:T(8,128)(2,1)S(1)}, bf16[24,1536]{1,0:T(8,128)(2,1)S(1)}, u32[]{:S(2)}, u32[]{:S(2)}) collective-permute-start(bf16[24,1536]{1,0:T(8,128)(2,1)S(1)} %get-tuple-element.21), channel_id=1, source_target_pairs={{0,2},{1,3},{2,0},{3,1},{4,6},{5,7},{6,4},{7,5},{8,10},{9,11},{10,... | collective-permute-start | bytes 221192 | tf_op jit(solution)/shard_map/ppermute | solution.py:456
  18.5 2.3 %collective-permute-start.8 = (bf16[2,120,1536]{2,1,0:T(8,128)(2,1)S(1)}, bf16[2,120,1536]{2,1,0:T(8,128)(2,1)S(1)}, u32[]{:S(2)}, u32[]{:S(2)}) collective-permute-start(bf16[2,120,1536]{2,1,0:T(8,128)(2,1)S(1)} %pair.2), channel_id=1, source_target_pairs={{0,4},{4,0},{8,12},{12,8},{16,20},{20,16},{24,28},{28,24},{1,5},{5... | collective-permute-start | bytes 2211848 | tf_op jit(solution)/shard_map/ppermute | solution.py:398
  18.6 7.1 %collective-permute-start.6 = (bf16[120,768]{1,0:T(8,128)(2,1)S(1)}, bf16[120,768]{1,0:T(8,128)(2,1)S(1)}, u32[]{:S(2)}, u32[]{:S(2)}) collective-permute-start(bf16[120,768]{1,0:T(8,128)(2,1)S(1)} %slice.6), channel_id=1, source_target_pairs={{0,8},{4,12},{8,0},{12,4},{16,24},{20,28},{24,16},{28,20},{1,9},{5... | collective-permute-start | bytes 552968 | tf_op jit(solution)/shard_map/ppermute | solution.py:398
  19.2 6.7 %collective-permute-start.7 = (bf16[120,768]{1,0:T(8,128)(2,1)S(1)}, bf16[120,768]{1,0:T(8,128)(2,1)S(1)}, u32[]{:S(2)}, u32[]{:S(2)}) collective-permute-start(bf16[120,768]{1,0:T(8,128)(2,1)S(1)} %slice.7), channel_id=1, source_target_pairs={{0,16},{4,20},{8,24},{12,28},{16,0},{20,4},{24,8},{28,12},{1,17},{... | collective-permute-start | bytes 552968 | tf_op jit(solution)/shard_map/ppermute | solution.py:398
  25.5 8.2 %copy-start.1 = (bf16[5,36864]{1,0:T(8,128)(2,1)S(1)}, bf16[5,36864]{1,0:T(8,128)(2,1)}, u32[]{:S(2)}) copy-start(bf16[5,36864]{1,0:T(8,128)(2,1)} %green_ref.3) | copy-start | bytes 1105924
  26.0 1.8 %collective-permute-start.9 = (bf16[2,120,768]{2,1,0:T(8,128)(2,1)S(1)}, bf16[2,120,768]{2,1,0:T(8,128)(2,1)S(1)}, u32[]{:S(2)}, u32[]{:S(2)}) collective-permute-start(bf16[2,120,768]{2,1,0:T(8,128)(2,1)S(1)} %pair.3.refs_0_), channel_id=1, source_target_pairs={{0,4},{4,0},{8,12},{12,8},{16,20},{20,16},{24,28},{28,24},{1,5},{5... | collective-permute-start | bytes 1105928 | tf_op jit(solution)/shard_map/ppermute | solution.py:398
  26.0 7.6 %collective-permute-start.5 = (bf16[24,1536]{1,0:T(8,128)(2,1)S(1)}, bf16[24,1536]{1,0:T(8,128)(2,1)S(1)}, u32[]{:S(2)}, u32[]{:S(2)}) collective-permute-start(bf16[24,1536]{1,0:T(8,128)(2,1)S(1)} %get-tuple-element.24), channel_id=1, source_target_pairs={{0,3},{1,0},{2,1},{3,2},{4,7},{5,4},{6,5},{7,6},{8,11},{9,8},{10,9... | collective-permute-start | bytes 221192 | tf_op jit(solution)/shard_map/ppermute | solution.py:456
  30.7 10.1 %all-to-all-start = ((f32[32,1,128]{2,1,0:T(1,128)}), f32[32,1,128]{2,1,0:T(1,128)S(1)}, u32[]{:S(2)}, u32[]{:S(2)}) async-start(f32[32,1,128]{2,1,0:T(1,128)} %bitcast.6), calls=%async_computation | async-start | bytes 32768 | tf_op jit(solution)/shard_map/all_to_all | solution.py:540

commit v9 on v6

--- a/solution.py
+++ b/solution.py
@@ -228,11 +228,9 @@
         rank = rank + jnp.where(stays, 1, 0)
 
 
-def order_kernel(
-    dims, ident_ref, walker_ref, table_ref, chol_ref, core_ref, out_ref, place_ref, sems
-):
-    del core_ref
-    group, groups, chip_rows, place_dims = dims
+def order_kernel(dims, ident_ref, chol_ref, own_ref, out_ref, sems):
+    del own_ref
+    group, groups, chip_rows = dims
     chip = ident_ref[0] // 2
     edge = LANES - 2 * chip_rows
     rest = 2 * chip_rows - edge
@@ -260,7 +258,6 @@
             add(vec, 3, 0, chip_rows, place + chip_rows - edge)
     for copy in copies:
         copy.start()
-    find_places(place_dims, walker_ref[0], Moves(table_ref, place_dims[2]), place_ref)
     for copy in copies:
         copy.wait()
 
@@ -285,11 +282,12 @@
     )
 
 
-def near_kernel(dims, ident_ref, weight_ref, *refs):
+def near_kernel(dims, place_dims, ident_ref, walker_ref, table_ref, weight_ref, *refs):
     slots, share_rows, group, groups, chip_rows = dims
     piece_refs = refs[:6]
-    sum_ref, late_ref = refs[6:8]
-    trans_refs = refs[8:]
+    sum_ref, late_ref, place_ref = refs[6:9]
+    trans_refs = refs[9:]
+    find_places(place_dims, walker_ref[0], Moves(table_ref, place_dims[2]), place_ref)
     own = ident_ref[0]
     core = lax.rem(own, 2)
     pad_rows = padded(piece_refs[0].shape[0])
@@ -455,23 +453,18 @@
     from_x = swap(own_rows, near_x, blocks)
     from_y = swap(own_rows, near_y, blocks)
     from_core = swap(own_rows, core, blocks)
-    weights, place = pl.pallas_call(
-        functools.partial(
-            order_kernel, (group, groups, chip_rows, (slots, walkers, moves, keep))
-        ),
-        out_shape=[
-            jax.ShapeDtypeStruct((vectors * occ_count, orb_count), jnp.bfloat16),
-            jax.ShapeDtypeStruct((slots,), jnp.int32),
-        ],
-        in_specs=[smem] * 3 + [pl.BlockSpec(memory_space=pl.ANY)] * 2,
-        out_specs=[vmem, smem],
+    weights = pl.pallas_call(
+        functools.partial(order_kernel, (group, groups, chip_rows)),
+        out_shape=jax.ShapeDtypeStruct((vectors * occ_count, orb_count), jnp.bfloat16),
+        in_specs=[smem] + [pl.BlockSpec(memory_space=pl.ANY)] * 2,
+        out_specs=vmem,
         scratch_shapes=[pltpu.SemaphoreType.DMA((5 * vectors,))],
         compiler_params=pltpu.CompilerParams(vmem_limit_bytes=48 * 1024 * 1024),
         cost_estimate=pl.CostEstimate(
             flops=0, bytes_accessed=4 * chol.size, transcendentals=0
         ),
         name="order",
-    )(block_index, walker_index, table, chol, own_rows)
+    )(block_index, chol, own_rows)
     width = orb_count // 2
     from_x, from_y, weights, coming[:2] = lax.optimization_barrier(
         (from_x, from_y, weights, coming[:2])
@@ -483,14 +476,15 @@
 
     dims = (slots, share_rows, group, groups, chip_rows)
     work = 2 * vectors * occ_count * orb_count * pack_rows
-    near_sums, late = pl.pallas_call(
-        functools.partial(near_kernel, dims),
+    near_sums, late, place = pl.pallas_call(
+        functools.partial(near_kernel, dims, (slots, walkers, moves, keep)),
         out_shape=[
             jax.ShapeDtypeStruct((slots * ROWS, LANES), jnp.float32),
             jax.ShapeDtypeStruct((slots * chip_rows, vectors * occ_count), jnp.float32),
+            jax.ShapeDtypeStruct((slots,), jnp.int32),
         ],
-        in_specs=[smem] + [vmem] * 7,
-        out_specs=[vmem] * 2,
+        in_specs=[smem] * 3 + [vmem] * 7,
+        out_specs=[vmem] * 2 + [smem],
         scratch_shapes=[pltpu.VMEM((slots * 3 * chip_rows, group * occ_count), jnp.float32)]
         * groups,
         compiler_params=limit,
@@ -498,7 +492,7 @@
             flops=6 * work, bytes_accessed=2 * chol.size, transcendentals=0
         ),
         name="near",
-    )(block_index, weights, *near_pieces)
+    )(block_index, walker_index, table, weights, *near_pieces)
     far, near_sums = lax.optimization_barrier((far, near_sums))
     far_pieces = far + [swap(piece, core, blocks) for piece in far]
     all_sums = pl.pallas_call(

time: 41 us -> 41.6 us (1.015)
  waiting for transfers between devices: 6.86 us -> 7.31 us
    ppermute x3, waiting for transfers between devices: 0.33 us -> 1.53 us  [body(): lax.ppermute(leaving[shift - 1], 'walker', [(z, (z + shift) % walkers) fo...]
    all_to_all x1, starting transfers between devices: 3.33 us -> 2.55 us  [body(): lax.all_to_all(all_sums, ('block', 'walker'), split_axis=0, concat_axis=0...]
    ppermute x9, waiting for transfers between devices: 1.31 us -> 0.57 us  [swap(): lax.ppermute(value, 'block', [(index, index ^ mask) for index in range(bl...]
    ppermute x3, starting transfers between devices: 6.24 us -> 6.9 us  [body(): lax.ppermute(leaving[shift - 1], 'walker', [(z, (z + shift) % walkers) fo...]
  transfers between devices with their start and end apart: 13 -> 13, of which waited for: 5 -> 3; matrix products, arithmetic and copies ran while one was open for 2% -> 2% of each run, Pallas kernels for 35% -> 35%
where the time goes in v9:
time: 41.6 us; the launch traced here: 41.3 us
  starting transfers between devices  16.2 us (39%)
  Pallas kernels  14.7 us (35%)
  waiting for transfers between devices  7.31 us (18%)
  other arithmetic  1.34 us (3%)
  local copies, waits for them, and re-layouts  1.09 us (3%)
  between operations  0.75 us (2%)
    ppermute x3, starting transfers between devices, body(): lax.ppermute(leaving[shift - 1], 'walker', [(z, (z + shift) % walkers) fo...  6.9 us
    ppermute x9, starting transfers between devices, swap(): lax.ppermute(value, 'block', [(index, index ^ mask) for index in range(bl...  6.71 us
    pallas_call x1, Pallas kernels, body(): pl.pallas_call(functools.partial(near_kernel, dims, (slots, walkers, move...  6.01 us
    all_to_all x1, waiting for transfers between devices, body(): lax.all_to_all(all_sums, ('block', 'walker'), split_axis=0, concat_axis=0...  5.21 us
    pallas_call x1, Pallas kernels, body(): pl.pallas_call(functools.partial(far_kernel, dims), out_shape=jax.ShapeDt...  3.02 us
    pallas_call x1, Pallas kernels, body(): pl.pallas_call(functools.partial(order_kernel, (group, groups, chip_rows)...  2.76 us
    all_to_all x1, starting transfers between devices, body(): lax.all_to_all(all_sums, ('block', 'walker'), split_axis=0, concat_axis=0...  2.55 us
    pallas_call x1, Pallas kernels, body(): pl.pallas_call(functools.partial(assemble_kernel, move_dims), out_shape=j...  1.93 us
  transfers between devices with their start and end apart: 13, of which 3 were waited for; matrix products, arithmetic and copies ran while one was open for 2% of the time, Pallas kernels for 35%

profile of v9, /device:TPU:0, one launch (start us, length us, event | category | flops | bytes accessed | tf_op | source)
XLA Modules:
  0.0 41.3 jit_solution(8376600174865371705)
XLA Ops:
  0.6 1.1 %copy-done = bf16[5,36864]{1,0:T(8,128)(2,1)S(1)} copy-done((bf16[5,36864]{1,0:T(8,128)(2,1)S(1)}, bf16[5,36864]{1,0:T(8,128)(2,1)}, u32[]{:S(2)}) %copy-start) | copy-done | bytes 368664
  1.7 0.3 pack.1.own_ref.refs_0_
  2.0 3.0 %collective-permute-start = (bf16[120,1536]{1,0:T(8,128)(2,1)S(1)}, bf16[120,1536]{1,0:T(8,128)(2,1)S(1)}, u32[]{:S(2)}, u32[]{:S(2)}) collective-permute-start(bf16[120,1536]{1,0:T(8,128)(2,1)S(1)} %pack.1.own_ref.refs_0_), channel_id=1, source_target_pairs={{0,8},{4,12},{8,0},{12,4},{16,24},{20,28},{24,16},{28,20},{1,9},{5... | collective-permute-start | bytes 1105928 | tf_op jit(solution)/shard_map/ppermute | solution.py:403
  5.0 1.5 %collective-permute-start.1 = (bf16[120,1536]{1,0:T(8,128)(2,1)S(1)}, bf16[120,1536]{1,0:T(8,128)(2,1)S(1)}, u32[]{:S(2)}, u32[]{:S(2)}) collective-permute-start(bf16[120,1536]{1,0:T(8,128)(2,1)S(1)} %pack.1.own_ref.refs_0_), channel_id=1, source_target_pairs={{0,16},{4,20},{8,24},{12,28},{16,0},{20,4},{24,8},{28,12},{1,17},{... | collective-permute-start | bytes 1105928 | tf_op jit(solution)/shard_map/ppermute | solution.py:403
  6.5 0.7 %pad_add_fusion.table_ref = s32[5,4]{1,0:T(8,128)S(1)} fusion(s32[2,4]{1,0:T(2,128)} %bitcast.8, s32[2,4]{1,0:T(2,128)} %bitcast.9, s32[1,4]{1,0:T(1,128)} %bitcast.10), kind=kLoop, calls=%fused_computation | loop fusion | flops 40 | bytes 160 | tf_op jit(solution)/shard_map/concatenate | solution.py:415
  7.2 0.7 %leave.1 = (bf16[24,1536]{1,0:T(8,128)(2,1)S(1)}, bf16[24,1536]{1,0:T(8,128)(2,1)S(1)}, bf16[24,1536]{1,0:T(8,128)(2,1)S(1)}) custom-call(s32[1]{0:T(128)} %bitcast.ident_ref.walker_ref, s32[5,4]{1,0:T(8,128)S(1)} %pad_add_fusion.table_ref, bf16[120,1536]{1,0:T(8,128)(2,1)S(1)} %pack.1.own_ref.refs_0_), custom_call_target="tpu_custom_call" | custom-call | tf_op jit(solution)/shard_map/leave/pallas_call | solution.py:433
  7.9 1.6 %collective-permute-start.2 = (bf16[24,1536]{1,0:T(8,128)(2,1)S(1)}, bf16[24,1536]{1,0:T(8,128)(2,1)S(1)}, u32[]{:S(2)}, u32[]{:S(2)}) collective-permute-start(bf16[24,1536]{1,0:T(8,128)(2,1)S(1)} %get-tuple-element.19), channel_id=1, source_target_pairs={{0,1},{1,2},{2,3},{3,0},{4,5},{5,6},{6,7},{7,4},{8,9},{9,10},{10,1... | collective-permute-start | bytes 221192 | tf_op jit(solution)/shard_map/ppermute | solution.py:443
  9.5 2.6 %collective-permute-start.3 = (bf16[24,1536]{1,0:T(8,128)(2,1)S(1)}, bf16[24,1536]{1,0:T(8,128)(2,1)S(1)}, u32[]{:S(2)}, u32[]{:S(2)}) collective-permute-start(bf16[24,1536]{1,0:T(8,128)(2,1)S(1)} %get-tuple-element.20), channel_id=1, source_target_pairs={{0,2},{1,3},{2,0},{3,1},{4,6},{5,7},{6,4},{7,5},{8,10},{9,11},{10,... | collective-permute-start | bytes 221192 | tf_op jit(solution)/shard_map/ppermute | solution.py:443
  12.1 2.8 %order.1.weight_ref = bf16[1536,1536]{1,0:T(8,128)(2,1)S(1)} custom-call(s32[1]{0:T(128)} %bitcast.4.ident_ref, bf16[8,192,1536]{2,1,0:T(8,128)(2,1)} %chol_ref.1, bf16[120,1536]{1,0:T(8,128)(2,1)S(1)} %pack.1.own_ref.refs_0_), custom_call_target="tpu_custom_call" | custom-call | bytes 9437184 | tf_op jit(solution)/shard_map/order/pallas_call | solution.py:456
  14.9 1.5 %collective-permute-done.3.refs_1_ = bf16[24,1536]{1,0:T(8,128)(2,1)S(1)} collective-permute-done((bf16[24,1536]{1,0:T(8,128)(2,1)S(1)}, bf16[24,1536]{1,0:T(8,128)(2,1)S(1)}, u32[]{:S(2)}, u32[]{:S(2)}) %collective-permute-start.3) | collective-permute-done | bytes 73760 | tf_op jit(solution)/shard_map/ppermute | solution.py:443
  16.4 0.5 %collective-permute-start.7 = (bf16[120,1536]{1,0:T(8,128)(2,1)S(1)}, bf16[120,1536]{1,0:T(8,128)(2,1)S(1)}, u32[]{:S(2)}, u32[]{:S(2)}) collective-permute-start(bf16[120,1536]{1,0:T(8,128)(2,1)S(1)} %collective-permute-done.1.refs_4_), channel_id=1, source_target_pairs={{0,4},{4,0},{8,12},{12,8},{16,20},{20,16},{24,28},{28,24},{1,5},{5... | collective-permute-start | bytes 1105928 | tf_op jit(solution)/shard_map/ppermute | solution.py:403
  17.0 0.6 %collective-permute-start.8 = (bf16[120,768]{1,0:T(8,128)(2,1)S(1)}, bf16[120,768]{1,0:T(8,128)(2,1)S(1)}, u32[]{:S(2)}, u32[]{:S(2)}) collective-permute-start(bf16[120,768]{1,0:T(8,128)(2,1)S(1)} %slice.6), channel_id=1, source_target_pairs={{0,8},{4,12},{8,0},{12,4},{16,24},{20,28},{24,16},{28,20},{1,9},{5... | collective-permute-start | bytes 552968 | tf_op jit(solution)/shard_map/ppermute | solution.py:403
  17.6 0.5 %collective-permute-start.9 = (bf16[120,768]{1,0:T(8,128)(2,1)S(1)}, bf16[120,768]{1,0:T(8,128)(2,1)S(1)}, u32[]{:S(2)}, u32[]{:S(2)}) collective-permute-start(bf16[120,768]{1,0:T(8,128)(2,1)S(1)} %slice.7), channel_id=1, source_target_pairs={{0,16},{4,20},{8,24},{12,28},{16,0},{20,4},{24,8},{28,12},{1,17},{... | collective-permute-start | bytes 552968 | tf_op jit(solution)/shard_map/ppermute | solution.py:403
  18.1 0.5 %collective-permute-done.7.refs_5_ = bf16[120,1536]{1,0:T(8,128)(2,1)S(1)} collective-permute-done((bf16[120,1536]{1,0:T(8,128)(2,1)S(1)}, bf16[120,1536]{1,0:T(8,128)(2,1)S(1)}, u32[]{:S(2)}, u32[]{:S(2)}) %collective-permute-start.7) | collective-permute-done | bytes 368672 | tf_op jit(solution)/shard_map/ppermute | solution.py:403
  18.6 6.0 %near.1 = (f32[40,128]{1,0:T(8,128)S(1)}, f32[240,1536]{1,0:T(8,128)S(1)}, s32[5]{0:T(128)S(1)}) custom-call(s32[1]{0:T(128)} %bitcast.4.ident_ref, s32[1]{0:T(128)} %bitcast.ident_ref.walker_ref, s32[5,4]{1,0:T(8,128)S(1)} %pad_add_fusion.table_ref, bf16[1536,1536]{1,0:T(8,128)(2,1)S(1)} %order.1.weight_ref, bf16[120,1536]{1,0:T(8,128)(2,1)S(1)} %pack.1.own_ref.refs_0_, ...), custom_call_target="tpu_custom_call" | custom-call | flops 3397386240 | bytes 4718592 | tf_op jit(solution)/shard_map/near/pallas_call | solution.py:479
  24.7 0.2 collective-permute-start.10
  24.9 0.4 collective-permute-start.11
  25.3 2.7 %collective-permute-start.4 = (bf16[24,1536]{1,0:T(8,128)(2,1)S(1)}, bf16[24,1536]{1,0:T(8,128)(2,1)S(1)}, u32[]{:S(2)}, u32[]{:S(2)}) collective-permute-start(bf16[24,1536]{1,0:T(8,128)(2,1)S(1)} %get-tuple-element.23), channel_id=1, source_target_pairs={{0,3},{1,0},{2,1},{3,2},{4,7},{5,4},{6,5},{7,6},{8,11},{9,8},{10,9... | collective-permute-start | bytes 221192 | tf_op jit(solution)/shard_map/ppermute | solution.py:443
  28.0 3.0 %far.1 = f32[32,128]{1,0:T(8,128)} custom-call(s32[1]{0:T(128)} %bitcast.4.ident_ref, s32[5]{0:T(128)S(1)} %get-tuple-element.27.place_ref, bf16[1536,1536]{1,0:T(8,128)(2,1)S(1)} %order.1.weight_ref, f32[40,128]{1,0:T(8,128)S(1)} %get-tuple-element.29.near_sum_ref, f32[240,1536]{1,0:T(8,128)S(1)} %get-tuple-element.30.late_ref, ...), custom_call_target="tpu_custom_call" | custom-call | flops 1132462080 | bytes 4718592 | tf_op jit(solution)/shard_map/far/pallas_call | solution.py:498
  31.0 2.5 %all-to-all-start = ((f32[32,1,128]{2,1,0:T(1,128)}), f32[32,1,128]{2,1,0:T(1,128)S(1)}, u32[]{:S(2)}, u32[]{:S(2)}) async-start(f32[32,1,128]{2,1,0:T(1,128)} %bitcast.6), calls=%async_computation | async-start | bytes 32768 | tf_op jit(solution)/shard_map/all_to_all | solution.py:527
  33.6 1.9 %assemble.1 = bf16[3,36864]{1,0:T(4,128)(2,1)} custom-call(s32[1]{0:T(128)} %bitcast.ident_ref.walker_ref, s32[5,4]{1,0:T(8,128)S(1)} %pad_add_fusion.table_ref, bf16[5,36864]{1,0:T(8,128)(2,1)S(1)} %copy-done.1, bf16[24,1536]{1,0:T(8,128)(2,1)S(1)} %collective-permute-done.2.refs_0_, bf16[24,1536]{1,0:T(8,128)(2,1)S(1)} %collective-permute-done.3.refs_1_, ...), custom_call_target="tpu_custom_call" | custom-call | tf_op jit(solution)/shard_map/assemble/pallas_call | solution.py:512
  35.5 5.2 %all-to-all-done = f32[32,1,128]{2,1,0:T(1,128)S(1)} async-done(((f32[32,1,128]{2,1,0:T(1,128)}), f32[32,1,128]{2,1,0:T(1,128)S(1)}, u32[]{:S(2)}, u32[]{:S(2)}) %all-to-all-start) | async-done | bytes 16416 | tf_op jit(solution)/shard_map/all_to_all | solution.py:527
  40.7 0.1 reduce_sum.9
  40.8 0.6 %dynamic-slice_multiply_fusion = f32[3]{0:T(128)} fusion(f32[128]{0:T(128)S(1)} %reduce_sum.9, s32[]{:T(128)S(6)} %select_n.3), kind=kLoop, calls=%fused_computation.1 | loop fusion | flops 3 | bytes 28 | tf_op jit(solution)/shard_map/mul | solution.py:532
  (17 shorter events, 0.1 us)
Async XLA Ops:
  0.6 1.1 %copy-start = (bf16[5,36864]{1,0:T(8,128)(2,1)S(1)}, bf16[5,36864]{1,0:T(8,128)(2,1)}, u32[]{:S(2)}) copy-start(bf16[5,36864]{1,0:T(8,128)(2,1)} %green_ref.3) | copy-start | bytes 1105924
  2.0 14.4 %collective-permute-start = (bf16[120,1536]{1,0:T(8,128)(2,1)S(1)}, bf16[120,1536]{1,0:T(8,128)(2,1)S(1)}, u32[]{:S(2)}, u32[]{:S(2)}) collective-permute-start(bf16[120,1536]{1,0:T(8,128)(2,1)S(1)} %pack.1.own_ref.refs_0_), channel_id=1, source_target_pairs={{0,8},{4,12},{8,0},{12,4},{16,24},{20,28},{24,16},{28,20},{1,9},{5... | collective-permute-start | bytes 1105928 | tf_op jit(solution)/shard_map/ppermute | solution.py:403
  5.0 11.4 %collective-permute-start.1 = (bf16[120,1536]{1,0:T(8,128)(2,1)S(1)}, bf16[120,1536]{1,0:T(8,128)(2,1)S(1)}, u32[]{:S(2)}, u32[]{:S(2)}) collective-permute-start(bf16[120,1536]{1,0:T(8,128)(2,1)S(1)} %pack.1.own_ref.refs_0_), channel_id=1, source_target_pairs={{0,16},{4,20},{8,24},{12,28},{16,0},{20,4},{24,8},{28,12},{1,17},{... | collective-permute-start | bytes 1105928 | tf_op jit(solution)/shard_map/ppermute | solution.py:403
  7.9 7.0 %collective-permute-start.2 = (bf16[24,1536]{1,0:T(8,128)(2,1)S(1)}, bf16[24,1536]{1,0:T(8,128)(2,1)S(1)}, u32[]{:S(2)}, u32[]{:S(2)}) collective-permute-start(bf16[24,1536]{1,0:T(8,128)(2,1)S(1)} %get-tuple-element.19), channel_id=1, source_target_pairs={{0,1},{1,2},{2,3},{3,0},{4,5},{5,6},{6,7},{7,4},{8,9},{9,10},{10,1... | collective-permute-start | bytes 221192 | tf_op jit(solution)/shard_map/ppermute | solution.py:443
  9.5 6.9 %collective-permute-start.3 = (bf16[24,1536]{1,0:T(8,128)(2,1)S(1)}, bf16[24,1536]{1,0:T(8,128)(2,1)S(1)}, u32[]{:S(2)}, u32[]{:S(2)}) collective-permute-start(bf16[24,1536]{1,0:T(8,128)(2,1)S(1)} %get-tuple-element.20), channel_id=1, source_target_pairs={{0,2},{1,3},{2,0},{3,1},{4,6},{5,7},{6,4},{7,5},{8,10},{9,11},{10,... | collective-permute-start | bytes 221192 | tf_op jit(solution)/shard_map/ppermute | solution.py:443
  12.1 6.0 %collective-permute-start.5 = (bf16[120,1536]{1,0:T(8,128)(2,1)S(1)}, bf16[120,1536]{1,0:T(8,128)(2,1)S(1)}, u32[]{:S(2)}, u32[]{:S(2)}) collective-permute-start(bf16[120,1536]{1,0:T(8,128)(2,1)S(1)} %pack.1.own_ref.refs_0_), channel_id=1, source_target_pairs={{0,4},{4,0},{8,12},{12,8},{16,20},{20,16},{24,28},{28,24},{1,5},{5... | collective-permute-start | bytes 1105928 | tf_op jit(solution)/shard_map/ppermute | solution.py:403
  16.4 1.7 %collective-permute-start.6 = (bf16[120,1536]{1,0:T(8,128)(2,1)S(1)}, bf16[120,1536]{1,0:T(8,128)(2,1)S(1)}, u32[]{:S(2)}, u32[]{:S(2)}) collective-permute-start(bf16[120,1536]{1,0:T(8,128)(2,1)S(1)} %collective-permute-done.refs_2_), channel_id=1, source_target_pairs={{0,4},{4,0},{8,12},{12,8},{16,20},{20,16},{24,28},{28,24},{1,5},{5... | collective-permute-start | bytes 1105928 | tf_op jit(solution)/shard_map/ppermute | solution.py:403
  16.4 2.2 %collective-permute-start.7 = (bf16[120,1536]{1,0:T(8,128)(2,1)S(1)}, bf16[120,1536]{1,0:T(8,128)(2,1)S(1)}, u32[]{:S(2)}, u32[]{:S(2)}) collective-permute-start(bf16[120,1536]{1,0:T(8,128)(2,1)S(1)} %collective-permute-done.1.refs_4_), channel_id=1, source_target_pairs={{0,4},{4,0},{8,12},{12,8},{16,20},{20,16},{24,28},{28,24},{1,5},{5... | collective-permute-start | bytes 1105928 | tf_op jit(solution)/shard_map/ppermute | solution.py:403
  17.0 7.7 %collective-permute-start.8 = (bf16[120,768]{1,0:T(8,128)(2,1)S(1)}, bf16[120,768]{1,0:T(8,128)(2,1)S(1)}, u32[]{:S(2)}, u32[]{:S(2)}) collective-permute-start(bf16[120,768]{1,0:T(8,128)(2,1)S(1)} %slice.6), channel_id=1, source_target_pairs={{0,8},{4,12},{8,0},{12,4},{16,24},{20,28},{24,16},{28,20},{1,9},{5... | collective-permute-start | bytes 552968 | tf_op jit(solution)/shard_map/ppermute | solution.py:403
  17.6 7.1 %collective-permute-start.9 = (bf16[120,768]{1,0:T(8,128)(2,1)S(1)}, bf16[120,768]{1,0:T(8,128)(2,1)S(1)}, u32[]{:S(2)}, u32[]{:S(2)}) collective-permute-start(bf16[120,768]{1,0:T(8,128)(2,1)S(1)} %slice.7), channel_id=1, source_target_pairs={{0,16},{4,20},{8,24},{12,28},{16,0},{20,4},{24,8},{28,12},{1,17},{... | collective-permute-start | bytes 552968 | tf_op jit(solution)/shard_map/ppermute | solution.py:403
  24.7 8.9 %copy-start.1 = (bf16[5,36864]{1,0:T(8,128)(2,1)S(1)}, bf16[5,36864]{1,0:T(8,128)(2,1)}, u32[]{:S(2)}) copy-start(bf16[5,36864]{1,0:T(8,128)(2,1)} %green_ref.3) | copy-start | bytes 1105924
  24.7 3.3 %collective-permute-start.10 = (bf16[120,768]{1,0:T(8,128)(2,1)S(1)}, bf16[120,768]{1,0:T(8,128)(2,1)S(1)}, u32[]{:S(2)}, u32[]{:S(2)}) collective-permute-start(bf16[120,768]{1,0:T(8,128)(2,1)S(1)} %collective-permute-done.8.refs_0_), channel_id=1, source_target_pairs={{0,4},{4,0},{8,12},{12,8},{16,20},{20,16},{24,28},{28,24},{1,5},{5... | collective-permute-start | bytes 552968 | tf_op jit(solution)/shard_map/ppermute | solution.py:403
  24.9 3.1 %collective-permute-start.11 = (bf16[120,768]{1,0:T(8,128)(2,1)S(1)}, bf16[120,768]{1,0:T(8,128)(2,1)S(1)}, u32[]{:S(2)}, u32[]{:S(2)}) collective-permute-start(bf16[120,768]{1,0:T(8,128)(2,1)S(1)} %collective-permute-done.9.refs_1_), channel_id=1, source_target_pairs={{0,4},{4,0},{8,12},{12,8},{16,20},{20,16},{24,28},{28,24},{1,5},{5... | collective-permute-start | bytes 552968 | tf_op jit(solution)/shard_map/ppermute | solution.py:403
  25.3 8.3 %collective-permute-start.4 = (bf16[24,1536]{1,0:T(8,128)(2,1)S(1)}, bf16[24,1536]{1,0:T(8,128)(2,1)S(1)}, u32[]{:S(2)}, u32[]{:S(2)}) collective-permute-start(bf16[24,1536]{1,0:T(8,128)(2,1)S(1)} %get-tuple-element.23), channel_id=1, source_target_pairs={{0,3},{1,0},{2,1},{3,2},{4,7},{5,4},{6,5},{7,6},{8,11},{9,8},{10,9... | collective-permute-start | bytes 221192 | tf_op jit(solution)/shard_map/ppermute | solution.py:443
  31.0 9.7 %all-to-all-start = ((f32[32,1,128]{2,1,0:T(1,128)}), f32[32,1,128]{2,1,0:T(1,128)S(1)}, u32[]{:S(2)}, u32[]{:S(2)}) async-start(f32[32,1,128]{2,1,0:T(1,128)} %bitcast.6), calls=%async_computation | async-start | bytes 32768 | tf_op jit(solution)/shard_map/all_to_all | solution.py:527
